TPU v7x, 128 devices: a whole 4x4x4 slice. The times are simulated.
128 devices in a mesh: ctx: 8 (over y_hi, z), exp: 16 (over y_lo, x, core).
Axes of the slice: x: 4, y: 4 (y_hi: 2, y_lo: 2; y = y_hi * 2 + y_lo), z: 4, core: 2. Of those that a mesh axis runs over, the one named last changes fastest.
Arguments:
- queries: bfloat16 [1024, 64, 576], P('ctx', 'exp'), may hold values from -16 to 16
- prior_codes: bfloat16 [3072, 576], P('ctx'), may hold values from -4 to 4
- fresh_codes: bfloat16 [1024, 576], P('ctx'), may hold values from -4 to 4
- prior_powers: int32 [24], P('ctx'), may hold values from -1 to 1
- fresh_powers: int32 [8], P('ctx'), may hold values from -1 to 1
- block_mask: int32 [8, 32], replicated, may hold values from 0 to 1, as said below
- value_up: bfloat16 [64, 512, 128], P('exp'), may hold values from -0.25 to 0.25
- output_weight: bfloat16 [8192, 7168], P('exp'), may hold values from -0.0625 to 0.0625
- residual: bfloat16 [1024, 7168], P(('ctx', 'exp')), may hold values from -2 to 2
- norm_gain: bfloat16 [7168], replicated, may hold values from 0.5 to 1.5
- router: bfloat16 [7168, 16], replicated, may hold values from -0.0625 to 0.0625
- route_ids: int32 [1024, 2], P(('ctx', 'exp')), may hold values from 0 to 15, all different within a row; in each aligned block of 8 rows (0 to 7, 8 to 15, ...) at most 2 rows name the same one
- gate_weight: bfloat16 [16, 7168, 2048], P('exp', None, 'ctx'), may hold values from -0.0625 to 0.0625
- up_weight: bfloat16 [16, 7168, 2048], P('exp', None, 'ctx'), may hold values from -0.0625 to 0.0625
- down_weight: bfloat16 [16, 2048, 7168], P('exp', 'ctx'), may hold values from -0.125 to 0.125
Outputs:
- layer_out: bfloat16 [1024, 7168], P(('ctx', 'exp'))
Inputs may be any that keep to these rules, and one draw needn't show every extreme that they name: block_mask[q, k] is 1 exactly when key block k (the prior blocks first, then the new ones) lies in the same document as new block q and not after it; every new block sees itself. `route_ids`: the 8 tokens of one device name one expert at most 2 times in all.
All inputs are finite; a program needn't handle non-finite values.
Results may differ from a plain program's by a relative error of at most 0.034.
Values may be sent and summed in bfloat16 or wider, within the bound.
No kernel may reach another device: no remote copies, remote signals or barrier semaphores. Data moves between devices by JAX's collectives and lax.ppermute only.
A program may use at most 128 MiB of HBM per device.

v0:
```python
import jax
import jax.numpy as jnp
from jax import lax
from jax.sharding import PartitionSpec as P

ROPE = 64
NOPE = 128


def shifted(value, axis, by):
    devices = lax.axis_size(axis)
    return lax.ppermute(value, axis, [(i, (i + by) % devices) for i in range(devices)])


def power_two(powers):
    return jnp.where(powers < 0, 0.5, jnp.where(powers > 0, 2.0, 1.0)).astype(jnp.float32)


def expert_rows(token_rows, gate_part, up_part, down_part):
    gate_proj = jnp.dot(token_rows, gate_part, preferred_element_type=jnp.float32)
    up_proj = jnp.dot(token_rows, up_part, preferred_element_type=jnp.float32)
    inner_act = (jax.nn.silu(gate_proj) * up_proj).astype(jnp.bfloat16)
    return jnp.dot(inner_act, down_part, preferred_element_type=jnp.float32).astype(jnp.bfloat16)


def on_device(
    queries,
    prior_codes,
    fresh_codes,
    prior_powers,
    fresh_powers,
    block_mask,
    value_up,
    output_weight,
    residual,
    norm_gain,
    router,
    route_ids,
    gate_weight,
    up_weight,
    down_weight,
):
    ctx_count = lax.axis_size("ctx")
    ctx_index = lax.axis_index("ctx")
    rows_block, head_count, key_width = queries.shape
    prior_blocks = prior_powers.shape[0]
    latent_width = value_up.shape[1]
    factor = 1.0 / (NOPE + ROPE) ** 0.5
    code_rows = jnp.concatenate([prior_codes, fresh_codes], axis=0)
    scales = power_two(jnp.concatenate([prior_powers, fresh_powers], axis=0)).astype(jnp.bfloat16)
    mask_row = lax.dynamic_index_in_dim(block_mask, ctx_index, 0, keepdims=False)
    query_pos = jnp.arange(rows_block)
    causal = query_pos[:, None] >= query_pos[None, :]

    def add_block(softmax_state, key_rows, weight_scale, allowed):
        row_top, row_total, mixture = softmax_state
        scores = jnp.einsum(
            "qhd,kd->qhk", queries, key_rows, preferred_element_type=jnp.float32
        ) * (factor * weight_scale)
        scores = jnp.where(allowed[:, None, :], scores, -1e30)
        new_top = jnp.maximum(row_top, jnp.max(scores, axis=2))
        shrink = jnp.exp(row_top - new_top)
        weights = jnp.where(allowed[:, None, :], jnp.exp(scores - new_top[:, :, None]), 0.0)
        row_total = row_total * shrink + jnp.sum(weights, axis=2)
        values = jnp.einsum(
            "qhk,kl->qhl",
            weights.astype(jnp.bfloat16),
            key_rows[:, :latent_width],
            preferred_element_type=jnp.float32,
        )
        mixture = mixture * shrink[:, :, None] + values * weight_scale
        return (new_top, row_total, mixture)

    def absorb(softmax_state, owner_index, codes_now, scales_now):
        for block_number in range(prior_blocks + 1):
            if block_number < prior_blocks:
                global_block = owner_index * prior_blocks + block_number
            else:
                global_block = prior_blocks * ctx_count + owner_index
            block_live = lax.dynamic_index_in_dim(mask_row, global_block, 0, keepdims=False) > 0
            key_rows = codes_now[block_number * rows_block : (block_number + 1) * rows_block]
            weight_scale = scales_now[block_number].astype(jnp.float32)
            if block_number == prior_blocks:
                allowed = jnp.logical_and(
                    block_live, jnp.logical_or(owner_index != ctx_index, causal)
                )
            else:
                allowed = jnp.broadcast_to(block_live, (rows_block, rows_block))
            softmax_state = add_block(softmax_state, key_rows, weight_scale, allowed)
        return softmax_state

    softmax_state = (
        jnp.full((rows_block, head_count), -1e30, jnp.float32),
        jnp.zeros((rows_block, head_count), jnp.float32),
        jnp.zeros((rows_block, head_count, latent_width), jnp.float32),
    )
    softmax_state = absorb(softmax_state, ctx_index, code_rows, scales)

    def cycle_turn(turn_index, cycle_carry):
        current, codes_now, scales_now = cycle_carry
        codes_now, scales_now = shifted((codes_now, scales_now), "ctx", 1)
        owner_index = (ctx_index - turn_index) % ctx_count
        current = absorb(current, owner_index, codes_now, scales_now)
        return (current, codes_now, scales_now)

    softmax_state, code_rows, scales = lax.fori_loop(
        1, ctx_count, cycle_turn, (softmax_state, code_rows, scales)
    )
    row_top, row_total, mixture = softmax_state
    attended = (mixture / row_total[:, :, None]).astype(jnp.bfloat16)
    per_head = jnp.einsum(
        "qhl,hlv->qhv", attended, value_up, preferred_element_type=jnp.float32
    ).astype(jnp.bfloat16)
    flat_heads = per_head.reshape(rows_block, head_count * value_up.shape[2])
    head_term = jnp.dot(flat_heads, output_weight, preferred_element_type=jnp.float32)
    attention = lax.psum_scatter(
        head_term.astype(jnp.bfloat16), "exp", scatter_dimension=0, tiled=True
    ).astype(jnp.float32)
    hidden = (residual.astype(jnp.float32) + attention).astype(jnp.bfloat16)
    hidden_wide = hidden.astype(jnp.float32)
    normed = (
        hidden_wide
        * lax.rsqrt(jnp.mean(hidden_wide * hidden_wide, axis=1, keepdims=True) + 1e-06)
        * norm_gain.astype(jnp.float32)
    ).astype(jnp.bfloat16)
    expert_count = router.shape[1]
    token_count, route_count = route_ids.shape
    model_width = normed.shape[1]
    capacity = token_count * route_count * 2 // expert_count
    affinity = jax.nn.sigmoid(jnp.dot(normed, router, preferred_element_type=jnp.float32))
    route_hits = route_ids[:, :, None] == jnp.arange(expert_count)[None, None, :]
    chosen = jnp.sum(jnp.where(route_hits, affinity[:, None, :], 0.0), axis=2)
    gate_values = 2.5 * chosen / jnp.sum(chosen, axis=1, keepdims=True)
    flat_hits = route_hits.reshape(token_count * route_count, expert_count).astype(jnp.int32)
    before = jnp.cumsum(flat_hits, axis=0) - flat_hits
    slot_index = jnp.sum(before * flat_hits, axis=1)
    target = route_ids.reshape(-1) * capacity + slot_index
    placing = (target[None, :] == jnp.arange(expert_count * capacity)[:, None]).astype(jnp.bfloat16)
    repeated = jnp.repeat(normed, route_count, axis=0)
    buffer = jnp.dot(placing, repeated, preferred_element_type=jnp.float32).astype(jnp.bfloat16)
    gate_part = gate_weight[0]
    up_part = up_weight[0]
    down_part = down_weight[0]
    sectioned = lax.all_to_all(
        buffer.reshape(expert_count, capacity, model_width),
        "exp",
        split_axis=0,
        concat_axis=0,
        tiled=True,
    )
    partials = expert_rows(
        lax.all_gather(
            sectioned.reshape(expert_count * capacity, model_width), "ctx", axis=0, tiled=True
        ),
        gate_part,
        up_part,
        down_part,
    )
    partials = partials.reshape(ctx_count * expert_count, capacity, model_width)
    returned = lax.all_to_all(partials, ("ctx", "exp"), split_axis=0, concat_axis=0, tiled=True)
    summed = jnp.sum(
        returned.reshape(ctx_count, expert_count * capacity, model_width).astype(jnp.float32),
        axis=0,
    ).astype(jnp.bfloat16)
    gathered_back = jnp.dot(
        jnp.transpose(placing), summed, preferred_element_type=jnp.float32
    ).reshape(token_count, route_count, model_width)
    expert_mix = jnp.sum(gate_values[:, :, None] * gathered_back, axis=1)
    return (hidden_wide + expert_mix).astype(jnp.bfloat16)


def solution(mesh):
    in_specs = (
        P("ctx", "exp", None),
        P("ctx", None),
        P("ctx", None),
        P("ctx"),
        P("ctx"),
        P(),
        P("exp", None, None),
        P("exp", None),
        P(("ctx", "exp"), None),
        P(),
        P(),
        P(("ctx", "exp"), None),
        P("exp", None, "ctx"),
        P("exp", None, "ctx"),
        P("exp", "ctx", None),
    )
    out_specs = P(("ctx", "exp"), None)
    return jax.shard_map(
        on_device, mesh=mesh, in_specs=in_specs, out_specs=out_specs, check_vma=False
    )
```

profile of v0, /device:TPU:1, one launch (start us, length us, event | category | flops | bytes accessed | tf_op | source)
XLA Modules:
  0.0 448.4 jit_solution(6899249186943810920)
XLA Ops:
  14.5 1.5 fusion.141
  21.0 1.4 fusion.146
  22.5 1.4 fusion.144
  26.0 173.0 %while.24 = (s32[]{:T(128)}, f32[128,4]{0,1:T(4,128)S(1)}, f32[128,4]{0,1:T(4,128)S(1)}, f32[128,4,512]{2,0,1:T(8,128)S(1)}, bf16[512,576]{0,1:T(8,128)(2,1)S(1)...) while((s32[]{:T(128)}, f32[128,4]{0,1:T(4,128)S(1)}, ...), condition=%wide.region_17.18_spmd.clone, body=%wide.region_8.17_spmd.clone.sunk | while | flops 575983616 | bytes 18707276 | solution.py:106
  26.0 2.5 collective-permute-start.1
  28.6 1.6 collective-permute-start
  33.4 13.0 %collective-permute-done = bf16[4]{0:T(256)(128)(2,1)S(1)} collective-permute-done((bf16[4]{0:T(256)(128)(2,1)S(1)}, bf16[4]{0:T(256)(128)(2,1)S(1)}, u32[]{:S(2)}, u32[]{:S(2)}) %collective-permute-start) | collective-permute-done | bytes 40 | tf_op jit(solution)/shard_map/while/body/eval_jaxpr/ppermute | solution.py:12
  58.9 13.8 %collective-permute-done = bf16[4]{0:T(256)(128)(2,1)S(1)} collective-permute-done((bf16[4]{0:T(256)(128)(2,1)S(1)}, bf16[4]{0:T(256)(128)(2,1)S(1)}, u32[]{:S(2)}, u32[]{:S(2)}) %collective-permute-start) | collective-permute-done | bytes 40 | tf_op jit(solution)/shard_map/while/body/eval_jaxpr/ppermute | solution.py:12
  85.3 12.8 %collective-permute-done = bf16[4]{0:T(256)(128)(2,1)S(1)} collective-permute-done((bf16[4]{0:T(256)(128)(2,1)S(1)}, bf16[4]{0:T(256)(128)(2,1)S(1)}, u32[]{:S(2)}, u32[]{:S(2)}) %collective-permute-start) | collective-permute-done | bytes 40 | tf_op jit(solution)/shard_map/while/body/eval_jaxpr/ppermute | solution.py:12
  110.7 11.8 %collective-permute-done = bf16[4]{0:T(256)(128)(2,1)S(1)} collective-permute-done((bf16[4]{0:T(256)(128)(2,1)S(1)}, bf16[4]{0:T(256)(128)(2,1)S(1)}, u32[]{:S(2)}, u32[]{:S(2)}) %collective-permute-start) | collective-permute-done | bytes 40 | tf_op jit(solution)/shard_map/while/body/eval_jaxpr/ppermute | solution.py:12
  135.1 10.8 %collective-permute-done = bf16[4]{0:T(256)(128)(2,1)S(1)} collective-permute-done((bf16[4]{0:T(256)(128)(2,1)S(1)}, bf16[4]{0:T(256)(128)(2,1)S(1)}, u32[]{:S(2)}, u32[]{:S(2)}) %collective-permute-start) | collective-permute-done | bytes 40 | tf_op jit(solution)/shard_map/while/body/eval_jaxpr/ppermute | solution.py:12
  158.5 9.9 %collective-permute-done = bf16[4]{0:T(256)(128)(2,1)S(1)} collective-permute-done((bf16[4]{0:T(256)(128)(2,1)S(1)}, bf16[4]{0:T(256)(128)(2,1)S(1)}, u32[]{:S(2)}, u32[]{:S(2)}) %collective-permute-start) | collective-permute-done | bytes 40 | tf_op jit(solution)/shard_map/while/body/eval_jaxpr/ppermute | solution.py:12
  180.9 9.1 %collective-permute-done = bf16[4]{0:T(256)(128)(2,1)S(1)} collective-permute-done((bf16[4]{0:T(256)(128)(2,1)S(1)}, bf16[4]{0:T(256)(128)(2,1)S(1)}, u32[]{:S(2)}, u32[]{:S(2)}) %collective-permute-start) | collective-permute-done | bytes 40 | tf_op jit(solution)/shard_map/while/body/eval_jaxpr/ppermute | solution.py:12
  199.6 5.5 %convolution_convert_fusion.1 = bf16[128,7168]{1,0:T(8,128)(2,1)} fusion(bf16[128,512]{0,1:T(8,128)(2,1)S(1)} %bitcast.171, bf16[512,7168]{1,0:T(8,128)(2,1)} %param.24), kind=kOutput, calls=%fused_computation.65 | convolution fusion | flops 940441600 | bytes 9306112 | tf_op jit(solution)/shard_map/dot_general | solution.py:115
  205.7 61.7 %reduce-scatter.2.cloned.1.call-done = bf16[8,7168]{1,0:T(8,128)(2,1)} async-done(((bf16[128,7168]{1,0:T(8,128)(2,1)}), bf16[8,7168]{1,0:T(8,128)(2,1)}) %reduce-scatter.2.cloned.1.call-update) | async-done | bytes 114704 | tf_op jit(solution)/shard_map/reduce_scatter | solution.py:116
  270.1 15.8 %all_to_all.10 = bf16[16,2,7168]{2,1,0:T(2,128)(2,1)S(1)} all-to-all(bf16[16,2,7168]{2,1,0:T(2,128)(2,1)S(1)} %reshape.192), channel_id=1, replica_groups=mesh['ctx'=8,'exp'=16] {'exp'}, dimensions={0} | all-to-all | bytes 917504 | tf_op jit(solution)/shard_map/all_to_all | solution.py:144
  286.9 66.4 %all-gather.2.cloned.1.call-done = bf16[256,7168]{1,0:T(8,128)(2,1)} async-done(((bf16[32,7168]{1,0:T(8,128)(2,1)}), bf16[256,7168]{1,0:T(8,128)(2,1)}) %all-gather.2.cloned.1.call-update) | async-done | bytes 3670032 | tf_op jit(solution)/shard_map/all_gather | solution.py:152
  353.3 4.3 fusion.46
  357.6 10.0 %convolution_convert_fusion = bf16[256,7168]{1,0:T(8,128)(2,1)} fusion(bf16[1,256,7168]{2,1,0:T(8,128)(2,1)} %param.31, bf16[256,7168]{1,0:T(8,128)(2,1)} %all-gather.2.cloned.1.call-done, bf16[1,7168,256]{2,1,0:T(8,128)(2,1)} %param.30, f32[256,256]{1,0:T(8,128)S(1)} %fusion.46), kind=kOutput, calls=%fused_computation.64 | convolution fusion | flops 1881276416 | bytes 14942208 | tf_op jit(solution)/shard_map/dot_general | solution.py:23
  367.6 8.1 %reshape.194 = bf16[128,2,7168]{2,1,0:T(2,128)(2,1)} reshape(bf16[256,7168]{1,0:T(8,128)(2,1)} %convolution_convert_fusion) | data formatting | bytes 7340032 | tf_op jit(solution)/shard_map/reshape | solution.py:159
  375.7 6.8 %all-to-all-start.1 = ((bf16[128,2,7168]{2,1,0:T(2,128)(2,1)}), bf16[128,2,7168]{2,1,0:T(2,128)(2,1)}, u32[]{:S(2)}, u32[]{:S(2)}) async-start(bf16[128,2,7168]{2,1,0:T(2,128)(2,1)} %reshape.194), calls=%async_computation.2 | async-start | bytes 7340032 | tf_op jit(solution)/shard_map/all_to_all | solution.py:160
  383.1 46.4 %all-to-all-done.1 = bf16[128,2,7168]{2,1,0:T(2,128)(2,1)} async-done(((bf16[128,2,7168]{2,1,0:T(2,128)(2,1)}), bf16[128,2,7168]{2,1,0:T(2,128)(2,1)}, u32[]{:S(2)}, u32[]{:S(2)}) %all-to-all-start.1) | async-done | bytes 3670048 | tf_op jit(solution)/shard_map/all_to_all | solution.py:160
  429.5 8.4 %reshape.195 = bf16[8,32,7168]{2,1,0:T(8,128)(2,1)} reshape(bf16[128,2,7168]{2,1,0:T(2,128)(2,1)} %all-to-all-done.1) | data formatting | bytes 7340032 | tf_op jit(solution)/shard_map/reshape | solution.py:162
  437.9 2.7 reduce_sum.168
  (206 shorter events, 47.2 us)
Async XLA Ops:
  6.5 192.6 %copy-start = (bf16[4,512,128]{2,1,0:T(8,128)(2,1)S(1)}, bf16[4,512,128]{2,1,0:T(8,128)(2,1)}, u32[]{:S(2)}) copy-start(bf16[4,512,128]{2,1,0:T(8,128)(2,1)} %param.23) | copy-start | bytes 1572868
  6.5 17.3 %copy-start.1 = (bf16[384,576]{0,1:T(8,128)(2,1)S(1)}, bf16[384,576]{0,1:T(8,128)(2,1)}, u32[]{:S(2)}) copy-start(bf16[384,576]{0,1:T(8,128)(2,1)} %param.18) | copy-start | bytes 1327108
  6.5 17.3 %copy-start.8 = (bf16[128,4,576]{0,2,1:T(8,128)(2,1)S(1)}, bf16[128,4,576]{0,2,1:T(8,128)(2,1)}, u32[]{:S(2)}) copy-start(bf16[128,4,576]{0,2,1:T(8,128)(2,1)} %param.17) | copy-start | bytes 1769476
  6.5 260.8 %reduce-scatter.2.cloned.1.call-start = ((), (), s32[]{:S(2)}) async-start(), calls=%async_computation.3 | async-start | bytes 1949696 | tf_op jit(solution)/shard_map/reduce_scatter | solution.py:116
  26.0 26.0 %collective-permute-start.1 = (bf16[512,576]{0,1:T(8,128)(2,1)S(1)}, bf16[512,576]{0,1:T(8,128)(2,1)S(1)}, u32[]{:S(2)}, u32[]{:S(2)}) collective-permute-start(bf16[512,576]{0,1:T(8,128)(2,1)S(1)} %get-tuple-element.491), channel_id=1, source_target_pairs={{0,16},{16,32},{32,48},{48,64},{64,80},{80,96},{96,112},{112,0},{1... | collective-permute-start | bytes 1769480 | tf_op jit(solution)/shard_map/while/body/eval_jaxpr/ppermute | solution.py:12
  28.6 17.8 %collective-permute-start = (bf16[4]{0:T(256)(128)(2,1)S(1)}, bf16[4]{0:T(256)(128)(2,1)S(1)}, u32[]{:S(2)}, u32[]{:S(2)}) collective-permute-start(bf16[4]{0:T(256)(128)(2,1)S(1)} %get-tuple-element.492), channel_id=1, source_target_pairs={{0,16},{16,32},{32,48},{48,64},{64,80},{80,96},{96,112},{112,0},{1... | collective-permute-start | bytes 32 | tf_op jit(solution)/shard_map/while/body/eval_jaxpr/ppermute | solution.py:12
  55.5 22.9 %collective-permute-start.1 = (bf16[512,576]{0,1:T(8,128)(2,1)S(1)}, bf16[512,576]{0,1:T(8,128)(2,1)S(1)}, u32[]{:S(2)}, u32[]{:S(2)}) collective-permute-start(bf16[512,576]{0,1:T(8,128)(2,1)S(1)} %get-tuple-element.491), channel_id=1, source_target_pairs={{0,16},{16,32},{32,48},{48,64},{64,80},{80,96},{96,112},{112,0},{1... | collective-permute-start | bytes 1769480 | tf_op jit(solution)/shard_map/while/body/eval_jaxpr/ppermute | solution.py:12
  55.6 17.1 %collective-permute-start = (bf16[4]{0:T(256)(128)(2,1)S(1)}, bf16[4]{0:T(256)(128)(2,1)S(1)}, u32[]{:S(2)}, u32[]{:S(2)}) collective-permute-start(bf16[4]{0:T(256)(128)(2,1)S(1)} %get-tuple-element.492), channel_id=1, source_target_pairs={{0,16},{16,32},{32,48},{48,64},{64,80},{80,96},{96,112},{112,0},{1... | collective-permute-start | bytes 32 | tf_op jit(solution)/shard_map/while/body/eval_jaxpr/ppermute | solution.py:12
  81.9 21.9 %collective-permute-start.1 = (bf16[512,576]{0,1:T(8,128)(2,1)S(1)}, bf16[512,576]{0,1:T(8,128)(2,1)S(1)}, u32[]{:S(2)}, u32[]{:S(2)}) collective-permute-start(bf16[512,576]{0,1:T(8,128)(2,1)S(1)} %get-tuple-element.491), channel_id=1, source_target_pairs={{0,16},{16,32},{32,48},{48,64},{64,80},{80,96},{96,112},{112,0},{1... | collective-permute-start | bytes 1769480 | tf_op jit(solution)/shard_map/while/body/eval_jaxpr/ppermute | solution.py:12
  82.0 16.1 %collective-permute-start = (bf16[4]{0:T(256)(128)(2,1)S(1)}, bf16[4]{0:T(256)(128)(2,1)S(1)}, u32[]{:S(2)}, u32[]{:S(2)}) collective-permute-start(bf16[4]{0:T(256)(128)(2,1)S(1)} %get-tuple-element.492), channel_id=1, source_target_pairs={{0,16},{16,32},{32,48},{48,64},{64,80},{80,96},{96,112},{112,0},{1... | collective-permute-start | bytes 32 | tf_op jit(solution)/shard_map/while/body/eval_jaxpr/ppermute | solution.py:12
  107.3 20.9 %collective-permute-start.1 = (bf16[512,576]{0,1:T(8,128)(2,1)S(1)}, bf16[512,576]{0,1:T(8,128)(2,1)S(1)}, u32[]{:S(2)}, u32[]{:S(2)}) collective-permute-start(bf16[512,576]{0,1:T(8,128)(2,1)S(1)} %get-tuple-element.491), channel_id=1, source_target_pairs={{0,16},{16,32},{32,48},{48,64},{64,80},{80,96},{96,112},{112,0},{1... | collective-permute-start | bytes 1769480 | tf_op jit(solution)/shard_map/while/body/eval_jaxpr/ppermute | solution.py:12
  107.4 15.1 %collective-permute-start = (bf16[4]{0:T(256)(128)(2,1)S(1)}, bf16[4]{0:T(256)(128)(2,1)S(1)}, u32[]{:S(2)}, u32[]{:S(2)}) collective-permute-start(bf16[4]{0:T(256)(128)(2,1)S(1)} %get-tuple-element.492), channel_id=1, source_target_pairs={{0,16},{16,32},{32,48},{48,64},{64,80},{80,96},{96,112},{112,0},{1... | collective-permute-start | bytes 32 | tf_op jit(solution)/shard_map/while/body/eval_jaxpr/ppermute | solution.py:12
  131.7 19.9 %collective-permute-start.1 = (bf16[512,576]{0,1:T(8,128)(2,1)S(1)}, bf16[512,576]{0,1:T(8,128)(2,1)S(1)}, u32[]{:S(2)}, u32[]{:S(2)}) collective-permute-start(bf16[512,576]{0,1:T(8,128)(2,1)S(1)} %get-tuple-element.491), channel_id=1, source_target_pairs={{0,16},{16,32},{32,48},{48,64},{64,80},{80,96},{96,112},{112,0},{1... | collective-permute-start | bytes 1769480 | tf_op jit(solution)/shard_map/while/body/eval_jaxpr/ppermute | solution.py:12
  131.7 14.2 %collective-permute-start = (bf16[4]{0:T(256)(128)(2,1)S(1)}, bf16[4]{0:T(256)(128)(2,1)S(1)}, u32[]{:S(2)}, u32[]{:S(2)}) collective-permute-start(bf16[4]{0:T(256)(128)(2,1)S(1)} %get-tuple-element.492), channel_id=1, source_target_pairs={{0,16},{16,32},{32,48},{48,64},{64,80},{80,96},{96,112},{112,0},{1... | collective-permute-start | bytes 32 | tf_op jit(solution)/shard_map/while/body/eval_jaxpr/ppermute | solution.py:12
  155.1 18.9 %collective-permute-start.1 = (bf16[512,576]{0,1:T(8,128)(2,1)S(1)}, bf16[512,576]{0,1:T(8,128)(2,1)S(1)}, u32[]{:S(2)}, u32[]{:S(2)}) collective-permute-start(bf16[512,576]{0,1:T(8,128)(2,1)S(1)} %get-tuple-element.491), channel_id=1, source_target_pairs={{0,16},{16,32},{32,48},{48,64},{64,80},{80,96},{96,112},{112,0},{1... | collective-permute-start | bytes 1769480 | tf_op jit(solution)/shard_map/while/body/eval_jaxpr/ppermute | solution.py:12
  155.1 13.2 %collective-permute-start = (bf16[4]{0:T(256)(128)(2,1)S(1)}, bf16[4]{0:T(256)(128)(2,1)S(1)}, u32[]{:S(2)}, u32[]{:S(2)}) collective-permute-start(bf16[4]{0:T(256)(128)(2,1)S(1)} %get-tuple-element.492), channel_id=1, source_target_pairs={{0,16},{16,32},{32,48},{48,64},{64,80},{80,96},{96,112},{112,0},{1... | collective-permute-start | bytes 32 | tf_op jit(solution)/shard_map/while/body/eval_jaxpr/ppermute | solution.py:12
  177.5 18.1 %collective-permute-start.1 = (bf16[512,576]{0,1:T(8,128)(2,1)S(1)}, bf16[512,576]{0,1:T(8,128)(2,1)S(1)}, u32[]{:S(2)}, u32[]{:S(2)}) collective-permute-start(bf16[512,576]{0,1:T(8,128)(2,1)S(1)} %get-tuple-element.491), channel_id=1, source_target_pairs={{0,16},{16,32},{32,48},{48,64},{64,80},{80,96},{96,112},{112,0},{1... | collective-permute-start | bytes 1769480 | tf_op jit(solution)/shard_map/while/body/eval_jaxpr/ppermute | solution.py:12
  177.6 12.4 %collective-permute-start = (bf16[4]{0:T(256)(128)(2,1)S(1)}, bf16[4]{0:T(256)(128)(2,1)S(1)}, u32[]{:S(2)}, u32[]{:S(2)}) collective-permute-start(bf16[4]{0:T(256)(128)(2,1)S(1)} %get-tuple-element.492), channel_id=1, source_target_pairs={{0,16},{16,32},{32,48},{48,64},{64,80},{80,96},{96,112},{112,0},{1... | collective-permute-start | bytes 32 | tf_op jit(solution)/shard_map/while/body/eval_jaxpr/ppermute | solution.py:12
  199.5 5.7 %copy-start.7 = (s32[8,2]{0,1:T(2,128)S(1)}, s32[8,2]{0,1:T(2,128)}, u32[]{:S(2)}) copy-start(s32[8,2]{0,1:T(2,128)} %param.28) | copy-start | bytes 196
  199.5 5.9 %copy-start.6 = (bf16[7168]{0:T(1024)(128)(2,1)S(1)}, bf16[7168]{0:T(1024)(128)(2,1)}, u32[]{:S(2)}) copy-start(bf16[7168]{0:T(1024)(128)(2,1)} %param.26) | copy-start | bytes 43012
  199.6 67.8 %copy-start.2 = (bf16[8,7168]{1,0:T(8,128)(2,1)S(1)}, bf16[8,7168]{1,0:T(8,128)(2,1)}, u32[]{:S(2)}) copy-start(bf16[8,7168]{1,0:T(8,128)(2,1)} %param.25) | copy-start | bytes 344068
  205.1 148.2 %all-gather.2.cloned.1.call-start = ((), (), s32[]{:S(2)}) async-start(), calls=%async_computation.4 | async-start | bytes 4128768 | tf_op jit(solution)/shard_map/all_gather | solution.py:152
  375.7 7.0 %copy-start.5 = (bf16[7168,16]{0,1:T(8,128)(2,1)S(1)}, bf16[7168,16]{0,1:T(8,128)(2,1)}, u32[]{:S(2)}) copy-start(bf16[7168,16]{0,1:T(8,128)(2,1)} %param.27) | copy-start | bytes 688132
  375.7 53.8 %all-to-all-start.1 = ((bf16[128,2,7168]{2,1,0:T(2,128)(2,1)}), bf16[128,2,7168]{2,1,0:T(2,128)(2,1)}, u32[]{:S(2)}, u32[]{:S(2)}) async-start(bf16[128,2,7168]{2,1,0:T(2,128)(2,1)} %reshape.194), calls=%async_computation.2 | async-start | bytes 7340032 | tf_op jit(solution)/shard_map/all_to_all | solution.py:160
  (2 other events, 4.4 us)
Sparse Core Ops, SparseCore 0:
  205.3 62.0 reduce-scatter.1
  287.0 66.2 all-gather.1
where the time goes:
time: 450 us; the launch traced here: 448 us
  waiting for transfers between devices  256 us (57%)
  loops' own time  53.4 us (12%)
  matrix products  48.8 us (11%)
  local copies, waits for them, and re-layouts  30.7 us (7%)
  between operations  22 us (5%)
  blocking collectives  15.8 us (4%)
  starting transfers between devices  11.9 us (3%)
  other arithmetic  10.1 us (2%)
    ppermute x14, waiting for transfers between devices, shifted(): lax.ppermute(value, axis, [(i, (i + by) % devices) for i in range(devices)])  81.3 us
    all_gather x1, waiting for transfers between devices, on_device(): lax.all_gather(sectioned.reshape(expert_count * capacity, model_width), '...  66.4 us
    reduce_scatter x1, waiting for transfers between devices, on_device(): lax.psum_scatter(head_term.astype(jnp.bfloat16), 'exp', scatter_dimension...  61.7 us
    another operation x1, loops' own time, on_device(): lax.fori_loop(1, ctx_count, cycle_turn, (softmax_state, code_rows, scales))  53.4 us
    all_to_all x1, waiting for transfers between devices, on_device(): lax.all_to_all(partials, ('ctx', 'exp'), split_axis=0, concat_axis=0, til...  46.4 us
    all_to_all x1, blocking collectives, on_device(): lax.all_to_all(buffer.reshape(expert_count, capacity, model_width), 'exp'...  15.8 us
    dot_general x32, matrix products, add_block(): jnp.einsum('qhd,kd->qhk', queries, key_rows, preferred_element_type=jnp.f...  14 us
    dot_general x32, matrix products, add_block(): jnp.einsum('qhk,kl->qhl', weights.astype(jnp.bfloat16), key_rows[:, :late...  13.7 us
  transfers between devices with their start and end apart: 17, of which 10 were waited for; matrix products, arithmetic and copies ran while one was open for 2% of the time, Pallas kernels for 0%

commit v1 on v0

v1 whole, which is shorter than its diff:
```python
import jax
import jax.numpy as jnp
from jax import lax
from jax.experimental import pallas as pl
from jax.experimental.pallas import tpu as pltpu
from jax.sharding import PartitionSpec as P

ROPE = 64
NOPE = 128
Y_HI, Z, Y_LO, X, CORES = 2, 4, 2, 4, 2
F32 = jnp.float32
BF16 = jnp.bfloat16


def ctx_pairs(move):
    return [
        (y * Z + z, move(y, z)[0] * Z + move(y, z)[1]) for y in range(Y_HI) for z in range(Z)
    ]


Z_UP = ctx_pairs(lambda y, z: (y, (z + 1) % Z))
Z_DOWN = ctx_pairs(lambda y, z: (y, (z - 1) % Z))
Y_SWAP = ctx_pairs(lambda y, z: (1 - y, z))
CORE_SWAP = [(i, i ^ 1) for i in range(Y_LO * X * CORES)]
SAME_CORE = [[2 * i + core for i in range(Y_LO * X)] for core in range(CORES)]


def over_ctx(value, pairs):
    return lax.ppermute(value, "ctx", pairs)


def core_swap(value):
    return lax.ppermute(value, "exp", CORE_SWAP)


def power_two(powers):
    return jnp.where(powers < 0, 0.5, jnp.where(powers > 0, 2.0, 1.0)).astype(jnp.float32)


def attention_kernel(
    live, queries, own, mine1, other1, mine2, other2, mine3, other3, value_up, weight_hbm,
    out_keep, out_send, scores, top, total, mixture, weight, weight_sem,
):
    copy = pltpu.make_async_copy(weight_hbm, weight, weight_sem)
    copy.start()
    rows = queries.shape[0]
    heads, latent_width, head_width = value_up.shape
    tokens = rows // heads
    unit = scores.shape[2]
    block = unit // 2
    parts = (own, mine1, other1, mine2, other2, mine3, other3)
    factor = 1.4426950408889634 / (NOPE + ROPE) ** 0.5
    top[...] = jnp.full_like(top, -1e30)
    total[...] = jnp.zeros_like(total)
    mixture[...] = jnp.zeros_like(mixture)

    def each_unit(body):
        first = 0
        for part in parts:
            count = part.shape[0] // unit
            if part is own:
                for u in range(count):
                    body(part, u, u, u == count - 1)
            else:
                def step(u, part=part, first=first):
                    body(part, u, first + u, False)
                pl.loop(0, count)(step)
            first += count

    def score(part, u, number, diagonal):
        live0, live1 = live[2 * number], live[2 * number + 1]

        @pl.when(live0 + live1 > 0)
        def _():
            keys = part[pl.ds(u * unit, unit), :]
            found = lax.dot_general(
                queries[...], keys, (((1,), (1,)), ((), ())), preferred_element_type=F32
            )
            column = lax.broadcasted_iota(jnp.int32, (1, unit), 1)
            column_live = jnp.where(column < block, live0, live1) > 0
            if diagonal:
                row = lax.broadcasted_iota(jnp.int32, (rows, 1), 0) % tokens
                relative = row // (tokens // 2)
                within = row % (tokens // 2)
                side = jnp.where(relative == 0, live[32], 1 - live[32])
                token = within // 8 * 16 + side * 8 + within % 8
                seen = jnp.logical_or(column < block, column - block <= token)
                allowed = jnp.logical_and(column_live, seen)
            else:
                allowed = column_live
            found = jnp.where(allowed, found, -1e30)
            scores[number] = found
            top[...] = jnp.maximum(top[...], found)

    def mix(part, u, number, diagonal):
        live0, live1 = live[2 * number], live[2 * number + 1]

        @pl.when(live0 + live1 > 0)
        def _():
            weights = jnp.exp2((scores[number] - row_top) * factor)
            total[...] += weights
            mixture[...] += jnp.dot(
                weights.astype(BF16),
                part[pl.ds(u * unit, unit), :latent_width],
                preferred_element_type=F32,
            )

    each_unit(score)
    row_top = jnp.max(top[...], axis=1, keepdims=True)
    each_unit(mix)
    row_total = jnp.sum(total[...], axis=1, keepdims=True)
    per_head = []
    for head in range(heads):
        span = slice(head * tokens, (head + 1) * tokens)
        attended = (mixture[span] / row_total[span]).astype(BF16)
        per_head.append(
            jnp.dot(attended, value_up[head], preferred_element_type=F32).astype(BF16)
        )
    flat_heads = jnp.concatenate(per_head, axis=1)
    copy.wait()
    width = 1024
    half = tokens // 2

    @pl.loop(0, weight.shape[1] // width)
    def _(step):
        columns = pl.ds(pl.multiple_of(step * width, width), width)
        term = jnp.dot(flat_heads, weight[:, columns], preferred_element_type=F32)
        out_keep[:, columns] = term[:half].astype(BF16)
        out_send[:, columns] = term[half:].astype(BF16)


def attention_call(live, queries, parts, value_up, output_weight):
    rows = queries.shape[0]
    tokens = rows // value_up.shape[0]
    width = output_weight.shape[1]
    key_total = sum(part.shape[0] for part in parts)
    unit = 256
    vmem = pl.BlockSpec(memory_space=pltpu.VMEM)
    out = jax.ShapeDtypeStruct((tokens // 2, width), BF16)
    return pl.pallas_call(
        attention_kernel,
        out_shape=(out, out),
        in_specs=[pl.BlockSpec(memory_space=pltpu.SMEM)]
        + [vmem] * (2 + len(parts))
        + [pl.BlockSpec(memory_space=pl.ANY)],
        out_specs=(vmem, vmem),
        scratch_shapes=[
            pltpu.VMEM((key_total // unit, rows, unit), F32),
            pltpu.VMEM((rows, unit), F32),
            pltpu.VMEM((rows, unit), F32),
            pltpu.VMEM((rows, value_up.shape[1]), F32),
            pltpu.VMEM(output_weight.shape, BF16),
            pltpu.SemaphoreType.DMA,
        ],
        compiler_params=pltpu.CompilerParams(vmem_limit_bytes=44 * 2**20),
        cost_estimate=pl.CostEstimate(
            flops=6 * 10**9, bytes_accessed=16 * 10**6, transcendentals=2 * 10**6
        ),
        name="attention",
    )(live, queries, *parts, value_up, output_weight)


def gather_codes(codes, core):
    rows = codes.shape[0]
    half = lax.dynamic_slice_in_dim(codes, core * (rows // 2), rows // 2, 0)
    quarter = rows // 4
    down = over_ctx(half, Z_UP)
    up = over_ctx(half, Z_DOWN)
    side = over_ctx(half, Y_SWAP)
    mine1 = jnp.concatenate([down, up, side], axis=0)
    other1 = core_swap(mine1)
    side_down = over_ctx(side, Z_UP)
    side_up = over_ctx(side, Z_DOWN)
    far_low = over_ctx(down[:quarter], Z_UP)
    far_high = over_ctx(up[quarter:], Z_DOWN)
    mine2 = jnp.concatenate([side_down, side_up, far_low, far_high], axis=0)
    other2 = core_swap(mine2)
    side_far_low = over_ctx(side_down[:quarter], Z_UP)
    side_far_high = over_ctx(side_up[quarter:], Z_DOWN)
    mine3 = jnp.concatenate([side_far_low, side_far_high], axis=0)
    other3 = core_swap(mine3)
    return (codes, mine1, other1, mine2, other2, mine3, other3)


def block_numbers(ctx_index, core, prior_blocks):
    y, z = ctx_index // Z, ctx_index % Z

    def owner(dy, dz):
        return (y + dy) % Y_HI * Z + (z + dz) % Z

    def numbers(dy, dz, side):
        index = owner(dy, dz)
        found = []
        for sub in range(2):
            place = side * 2 + sub
            found.append(
                jnp.where(
                    place < prior_blocks,
                    index * prior_blocks + place,
                    prior_blocks * Y_HI * Z + index,
                )
            )
        return found

    groups = (
        ((0, -1), (0, 1), (1, 0)),
        ((1, -1), (1, 1), (0, 2)),
        ((1, 2),),
    )
    found = numbers(0, 0, 0) + numbers(0, 0, 1)
    for group in groups:
        for side in (core, 1 - core):
            for dy, dz in group:
                found = found + numbers(dy, dz, side)
    return jnp.stack([jnp.asarray(f, jnp.int32) for f in found])


def experts_kernel(
    own, down, up, side, side_down, side_up, far_low, far_high, side_far_low, side_far_high,
    gate_hbm, up_hbm, down_hbm,
    o_own, o_down, o_up, o_side, o_side_down, o_side_up, o_far_low, o_far_high, o_sf_low, o_sf_high,
    rows, gate_weight, up_weight, down_weight, acc, sems,
):
    sources = (own, down, up, side, side_down, side_up, far_low, far_high, side_far_low, side_far_high)
    results = (o_own, o_down, o_up, o_side, o_side_down, o_side_up, o_far_low, o_far_high, o_sf_low, o_sf_high)
    weight_copies = [
        pltpu.make_async_copy(source.at[0], target, sems.at[i])
        for i, (source, target) in enumerate(
            ((gate_hbm, gate_weight), (up_hbm, up_weight), (down_hbm, down_weight))
        )
    ]
    for copy in weight_copies:
        copy.start()
    starts = []
    at = 0
    for source in sources:
        starts.append(at)
        rows[at : at + source.shape[0], :] = source[...]
        at += source.shape[0]
    weight_copies[0].wait()
    gate_proj = jnp.dot(rows[...], gate_weight[...], preferred_element_type=F32)
    weight_copies[1].wait()
    up_proj = jnp.dot(rows[...], up_weight[...], preferred_element_type=F32)
    inner_act = (gate_proj / (1.0 + jnp.exp(-gate_proj)) * up_proj).astype(BF16)
    weight_copies[2].wait()
    width = 1024

    @pl.loop(0, down_weight.shape[1] // width)
    def _(step):
        columns = pl.ds(pl.multiple_of(step * width, width), width)
        term = jnp.dot(inner_act, down_weight[:, columns], preferred_element_type=F32)
        for start, result in zip(starts, results):
            result[:, columns] = term[start : start + result.shape[0]].astype(BF16)


def experts_call(blocks, gate_weight, up_weight, down_weight):
    vmem = pl.BlockSpec(memory_space=pltpu.VMEM)
    anywhere = pl.BlockSpec(memory_space=pl.ANY)
    row_count = sum(block.shape[0] for block in blocks)
    return pl.pallas_call(
        experts_kernel,
        out_shape=tuple(jax.ShapeDtypeStruct(block.shape, BF16) for block in blocks),
        in_specs=[vmem] * len(blocks) + [anywhere] * 3,
        out_specs=tuple([vmem] * len(blocks)),
        scratch_shapes=[
            pltpu.VMEM((row_count, blocks[0].shape[1]), BF16),
            pltpu.VMEM(gate_weight.shape[1:], BF16),
            pltpu.VMEM(up_weight.shape[1:], BF16),
            pltpu.VMEM(down_weight.shape[1:], BF16),
            pltpu.VMEM((8, 128), F32),
            pltpu.SemaphoreType.DMA((3,)),
        ],
        compiler_params=pltpu.CompilerParams(vmem_limit_bytes=44 * 2**20),
        cost_estimate=pl.CostEstimate(
            flops=3 * 10**9, bytes_accessed=19 * 10**6, transcendentals=65536
        ),
        name="experts",
    )(*blocks, gate_weight, up_weight, down_weight)


def gather_rows(own):
    half = own.shape[0] // 2
    down = over_ctx(own, Z_UP)
    up = over_ctx(own, Z_DOWN)
    side = over_ctx(own, Y_SWAP)
    side_down = over_ctx(side, Z_UP)
    side_up = over_ctx(side, Z_DOWN)
    far_low = over_ctx(down[:half], Z_UP)
    far_high = over_ctx(up[half:], Z_DOWN)
    side_far_low = over_ctx(side_down[:half], Z_UP)
    side_far_high = over_ctx(side_up[half:], Z_DOWN)
    return (own, down, up, side, side_down, side_up, far_low, far_high, side_far_low, side_far_high)


def added(*terms):
    total = terms[0].astype(F32)
    for term in terms[1:]:
        total = total + term.astype(F32)
    return total.astype(BF16)


def reduce_rows(blocks):
    own, down, up, side, side_down, side_up, far_low, far_high, sf_low, sf_high = blocks
    half = own.shape[0] // 2

    def add_half(block, low=None, high=None):
        first, second = block[:half], block[half:]
        if low is not None:
            first = added(first, low)
        if high is not None:
            second = added(second, high)
        return jnp.concatenate([first, second], axis=0)

    sf_low_in = over_ctx(sf_low, Z_UP)
    sf_high_in = over_ctx(sf_high, Z_DOWN)
    side_up = add_half(side_up, low=sf_low_in)
    side_down = add_half(side_down, high=sf_high_in)
    far_low_in = over_ctx(far_low, Z_UP)
    far_high_in = over_ctx(far_high, Z_DOWN)
    side_up_in = over_ctx(side_up, Z_UP)
    side_down_in = over_ctx(side_down, Z_DOWN)
    up = add_half(up, low=far_low_in)
    down = add_half(down, high=far_high_in)
    side = added(side, side_up_in, side_down_in)
    side_in = over_ctx(side, Y_SWAP)
    up_in = over_ctx(up, Z_UP)
    down_in = over_ctx(down, Z_DOWN)
    return added(own, up_in, down_in, side_in)


def on_device(
    queries,
    prior_codes,
    fresh_codes,
    prior_powers,
    fresh_powers,
    block_mask,
    value_up,
    output_weight,
    residual,
    norm_gain,
    router,
    route_ids,
    gate_weight,
    up_weight,
    down_weight,
):
    ctx_index = lax.axis_index("ctx")
    core = lax.axis_index("exp") % CORES
    rows_block, head_count, key_width = queries.shape
    prior_blocks = prior_powers.shape[0]
    scales = power_two(jnp.concatenate([prior_powers, fresh_powers], axis=0))
    codes = jnp.concatenate([prior_codes, fresh_codes], axis=0).astype(F32)
    codes = (codes * jnp.repeat(scales, rows_block)[:, None]).astype(BF16)
    parts = gather_codes(codes, core)

    mask_row = lax.dynamic_index_in_dim(block_mask, ctx_index, 0, keepdims=False)
    numbers = block_numbers(ctx_index, core, prior_blocks)
    chosen_blocks = numbers[:, None] == jnp.arange(mask_row.shape[0])[None, :]
    live = jnp.sum(jnp.where(chosen_blocks, mask_row[None, :], 0), axis=1)
    live = jnp.concatenate([live, core[None]]).astype(jnp.int32)
    groups = rows_block // 16
    split = queries.reshape(groups, 2, 8, head_count, key_width)
    first = jnp.where(core == 0, split[:, 0], split[:, 1])
    second = jnp.where(core == 0, split[:, 1], split[:, 0])
    ordered = jnp.stack([first, second], axis=0)
    ordered = jnp.transpose(ordered, (3, 0, 1, 2, 4)).reshape(head_count * rows_block, key_width)

    keep, send = attention_call(live, ordered, parts, value_up, output_weight)
    paired = added(keep, core_swap(send))
    model_width = residual.shape[1]
    pieces = lax.all_to_all(
        paired.reshape(groups, 8, model_width),
        "exp",
        split_axis=0,
        concat_axis=0,
        tiled=True,
        axis_index_groups=SAME_CORE,
    )
    attention = jnp.sum(pieces.astype(F32), axis=0)
    hidden = (residual.astype(F32) + attention).astype(BF16)
    hidden_wide = hidden.astype(F32)
    normed = (
        hidden_wide
        * lax.rsqrt(jnp.mean(hidden_wide * hidden_wide, axis=1, keepdims=True) + 1e-06)
        * norm_gain.astype(F32)
    ).astype(BF16)
    expert_count = router.shape[1]
    token_count, route_count = route_ids.shape
    capacity = token_count * route_count * 2 // expert_count
    affinity = jax.nn.sigmoid(jnp.dot(normed, router, preferred_element_type=F32))
    route_hits = route_ids[:, :, None] == jnp.arange(expert_count)[None, None, :]
    chosen = jnp.sum(jnp.where(route_hits, affinity[:, None, :], 0.0), axis=2)
    gate_values = 2.5 * chosen / jnp.sum(chosen, axis=1, keepdims=True)
    flat_hits = route_hits.reshape(token_count * route_count, expert_count).astype(jnp.int32)
    before = jnp.cumsum(flat_hits, axis=0) - flat_hits
    slot_index = jnp.sum(before * flat_hits, axis=1)
    target = route_ids.reshape(-1) * capacity + slot_index
    placing = (target[None, :] == jnp.arange(expert_count * capacity)[:, None]).astype(BF16)
    repeated = jnp.repeat(normed, route_count, axis=0)
    buffer = jnp.dot(placing, repeated, preferred_element_type=F32).astype(BF16)
    sectioned = lax.all_to_all(
        buffer.reshape(expert_count, capacity, model_width),
        "exp",
        split_axis=0,
        concat_axis=0,
        tiled=True,
    )
    blocks = gather_rows(sectioned.reshape(expert_count * capacity, model_width))
    partials = experts_call(blocks, gate_weight, up_weight, down_weight)
    summed = reduce_rows(partials)
    returned = lax.all_to_all(
        summed.reshape(expert_count, capacity, model_width),
        "exp",
        split_axis=0,
        concat_axis=0,
        tiled=True,
    ).reshape(expert_count * capacity, model_width)
    gathered_back = jnp.dot(
        jnp.transpose(placing), returned, preferred_element_type=F32
    ).reshape(token_count, route_count, model_width)
    expert_mix = jnp.sum(gate_values[:, :, None] * gathered_back, axis=1)
    return (hidden_wide + expert_mix).astype(BF16)


def solution(mesh):
    in_specs = (
        P("ctx", "exp", None),
        P("ctx", None),
        P("ctx", None),
        P("ctx"),
        P("ctx"),
        P(),
        P("exp", None, None),
        P("exp", None),
        P(("ctx", "exp"), None),
        P(),
        P(),
        P(("ctx", "exp"), None),
        P("exp", None, "ctx"),
        P("exp", None, "ctx"),
        P("exp", "ctx", None),
    )
    out_specs = P(("ctx", "exp"), None)
    return jax.shard_map(
        on_device, mesh=mesh, in_specs=in_specs, out_specs=out_specs, check_vma=False
    )
```

time: 450 us -> 217 us (0.48)
  waiting for transfers between devices: 256 us -> 80.6 us
  loops' own time: 53.4 us -> 0 us
  starting transfers between devices: 11.9 us -> 61 us
  matrix products: 48.8 us -> 0.7 us
  Pallas kernels: 0 us -> 21.9 us
  between operations: 22 us -> 1.06 us
    all_gather x1 -> x0, waiting for transfers between devices: 66.4 us -> none  [on_device(): lax.all_gather(sectioned.reshape(expert_count * capacity, model_width), '...]
    reduce_scatter x1 -> x0, waiting for transfers between devices: 61.7 us -> none  [on_device(): lax.psum_scatter(head_term.astype(jnp.bfloat16), 'exp', scatter_dimension...]
    another operation x1 -> x0, loops' own time: 53.4 us -> none  [on_device(): lax.fori_loop(1, ctx_count, cycle_turn, (softmax_state, code_rows, scales))]
    dot_general x71 -> x3, matrix products: 48.8 us -> 0.7 us  [the longest x1 0.26 us: on_device(): jnp.dot(jnp.transpose(placing), returned, preferred_element_type=F32)]
    ppermute x14 -> x31, starting transfers between devices: 5.07 us -> 44.4 us  [the longest x27 38.7 us: over_ctx(): return lax.ppermute(value, 'ctx', pairs)]
    all_to_all x1 -> x2, waiting for transfers between devices: 46.4 us -> 22.5 us  [the longest x1 14 us: on_device(): lax.all_to_all(paired.reshape(groups, 8, model_width), 'exp', split_axis=...]
    ppermute x14 -> x31, waiting for transfers between devices: 81.3 us -> 58.1 us  [the longest x27 55.6 us: over_ctx(): return lax.ppermute(value, 'ctx', pairs)]
    pallas_call x0 -> x2, Pallas kernels: none -> 21.9 us  [the longest x1 13.6 us: attention_call(): pl.pallas_call(attention_kernel, out_shape=(out, out), in_specs=[pl.Block...]
  transfers between devices with their start and end apart: 17 -> 33, of which waited for: 10 -> 14; matrix products, arithmetic and copies ran while one was open for 2% -> 13% of each run, Pallas kernels for 0% -> 0%
where the time goes in v1:
time: 217 us
  waiting for transfers between devices  80.6 us (37%)
  starting transfers between devices  61 us (28%)
  local copies, waits for them, and re-layouts  31.2 us (14%)
  Pallas kernels  21.9 us (10%)
  blocking collectives  12.2 us (6%)
  other arithmetic  8.35 us (4%)
    ppermute x27, waiting for transfers between devices, over_ctx(): return lax.ppermute(value, 'ctx', pairs)  55.6 us
    ppermute x27, starting transfers between devices, over_ctx(): return lax.ppermute(value, 'ctx', pairs)  38.7 us
    all_to_all x1, waiting for transfers between devices, on_device(): lax.all_to_all(paired.reshape(groups, 8, model_width), 'exp', split_axis=...  14 us
    pallas_call x1, Pallas kernels, attention_call(): pl.pallas_call(attention_kernel, out_shape=(out, out), in_specs=[pl.Block...  13.6 us
    all_to_all x1, blocking collectives, on_device(): lax.all_to_all(buffer.reshape(expert_count, capacity, model_width), 'exp'...  12.2 us
    unnamed x26, local copies, waits for them, and re-layouts  11.9 us
    all_to_all x1, starting transfers between devices, on_device(): lax.all_to_all(summed.reshape(expert_count, capacity, model_width), 'exp'...  11.5 us
    all_to_all x1, waiting for transfers between devices, on_device(): lax.all_to_all(summed.reshape(expert_count, capacity, model_width), 'exp'...  8.51 us
  transfers between devices with their start and end apart: 33, of which 14 were waited for; matrix products, arithmetic and copies ran while one was open for 13% of the time, Pallas kernels for 0%

profile of v1, /device:TPU:1, one launch (start us, length us, event | category | flops | bytes accessed | tf_op | source)
XLA Modules:
  0.0 217.0 jit_solution(1137358251191294256)
XLA Ops:
  4.1 2.5 %collective-permute-start = (bf16[256,576]{1,0:T(8,128)(2,1)S(1)}, bf16[256,576]{1,0:T(8,128)(2,1)S(1)}, u32[]{:S(2)}, u32[]{:S(2)}) collective-permute-start(bf16[256,576]{1,0:T(8,128)(2,1)S(1)} %constant_dynamic-slice_fusion), channel_id=1, source_target_pairs={{0,16},{16,32},{32,48},{48,0},{64,80},{80,96},{96,112},{112,64},{1... | collective-permute-start | bytes 884744 | tf_op jit(solution)/shard_map/ppermute | solution.py:29
  8.8 2.9 %collective-permute-start.2 = (bf16[256,576]{1,0:T(8,128)(2,1)S(1)}, bf16[256,576]{1,0:T(8,128)(2,1)}, u32[]{:S(2)}, u32[]{:S(2)}) collective-permute-start(bf16[256,576]{1,0:T(8,128)(2,1)S(1)} %constant_dynamic-slice_fusion), channel_id=1, source_target_pairs={{0,64},{16,80},{32,96},{48,112},{64,0},{80,16},{96,32},{112,48},{1... | collective-permute-start | bytes 884744 | tf_op jit(solution)/shard_map/ppermute | solution.py:29
  17.6 2.7 %collective-permute-start.7 = (bf16[128,576]{1,0:T(8,128)(2,1)}, bf16[128,576]{1,0:T(8,128)(2,1)}, u32[]{:S(2)}, u32[]{:S(2)}) collective-permute-start(bf16[128,576]{1,0:T(8,128)(2,1)} %slice.77), channel_id=1, source_target_pairs={{0,48},{16,0},{32,16},{48,32},{64,112},{80,64},{96,80},{112,96},{1... | collective-permute-start | bytes 442376 | tf_op jit(solution)/shard_map/ppermute | solution.py:29
  20.3 2.7 %collective-permute-start.5 = (bf16[256,576]{1,0:T(8,128)(2,1)}, bf16[256,576]{1,0:T(8,128)(2,1)}, u32[]{:S(2)}, u32[]{:S(2)}) collective-permute-start(bf16[256,576]{1,0:T(8,128)(2,1)} %collective-permute-done.2), channel_id=1, source_target_pairs={{0,48},{16,0},{32,16},{48,32},{64,112},{80,64},{96,80},{112,96},{1... | collective-permute-start | bytes 884744 | tf_op jit(solution)/shard_map/ppermute | solution.py:29
  34.9 2.5 %collective-permute-start.8 = (bf16[768,576]{0,1:T(8,128)(2,1)}, bf16[768,576]{0,1:T(8,128)(2,1)}, u32[]{:S(2)}, u32[]{:S(2)}) collective-permute-start(bf16[768,576]{0,1:T(8,128)(2,1)} %copy.62), channel_id=1, source_target_pairs={{0,1},{1,0},{2,3},{3,2},{4,5},{5,4},{6,7},{7,6},{8,9},{9,8},{10,11... | collective-permute-start | bytes 2654216 | tf_op jit(solution)/shard_map/ppermute | solution.py:33
  40.6 2.7 %collective-permute-start.10 = (bf16[128,576]{1,0:T(8,128)(2,1)}, bf16[128,576]{1,0:T(8,128)(2,1)}, u32[]{:S(2)}, u32[]{:S(2)}) collective-permute-start(bf16[128,576]{1,0:T(8,128)(2,1)} %slice.79), channel_id=1, source_target_pairs={{0,48},{16,0},{32,16},{48,32},{64,112},{80,64},{96,80},{112,96},{1... | collective-permute-start | bytes 442376 | tf_op jit(solution)/shard_map/ppermute | solution.py:29
  59.1 13.6 %attention.1 = (bf16[64,7168]{1,0:T(8,128)(2,1)S(1)}, bf16[64,7168]{1,0:T(8,128)(2,1)S(1)}) custom-call(s32[33]{0:T(128)S(1)} %pad_add_fusion.live, bf16[512,576]{1,0:T(8,128)(2,1)S(1)} %bitcast.66, bf16[512,576]{1,0:T(8,128)(2,1)S(1)} %multiply_convert_fusion.own, bf16[768,576]{1,0:T(8,128)(2,1)S(1)} %constant_dynamic-update-slice_fusion.mine1, ...), custom_call_target="tpu_custom_call" | custom-call | flops 6000000000 | bytes 16000000 | tf_op jit(solution)/shard_map/attention/pallas_call | solution.py:140
  72.9 2.5 %collective-permute-done.12 = bf16[64,7168]{1,0:T(8,128)(2,1)S(1)} collective-permute-done((bf16[64,7168]{1,0:T(8,128)(2,1)S(1)}, bf16[64,7168]{1,0:T(8,128)(2,1)S(1)}, u32[]{:S(2)}, u32[]{:S(2)}) %collective-permute-start.12) | collective-permute-done | bytes 917536 | tf_op jit(solution)/shard_map/ppermute | solution.py:33
  76.5 5.1 %all-to-all-start = ((bf16[8,8,7168]{2,1,0:T(8,128)(2,1)}), bf16[8,8,7168]{2,1,0:T(8,128)(2,1)S(1)}, u32[]{:S(2)}, u32[]{:S(2)}) async-start(bf16[8,8,7168]{2,1,0:T(8,128)(2,1)} %fusion.4), calls=%async_computation | async-start | bytes 1835008 | tf_op jit(solution)/shard_map/all_to_all | solution.py:372
  82.1 14.0 %all-to-all-done = bf16[8,8,7168]{2,1,0:T(8,128)(2,1)S(1)} async-done(((bf16[8,8,7168]{2,1,0:T(8,128)(2,1)}), bf16[8,8,7168]{2,1,0:T(8,128)(2,1)S(1)}, u32[]{:S(2)}, u32[]{:S(2)}) %all-to-all-start) | async-done | bytes 917536 | tf_op jit(solution)/shard_map/all_to_all | solution.py:372
  97.1 12.2 %all_to_all.15 = bf16[16,2,7168]{2,1,0:T(2,128)(2,1)S(1)} all-to-all(bf16[16,2,7168]{2,1,0:T(2,128)(2,1)S(1)} %reshape.131), channel_id=1, replica_groups=mesh['ctx'=8,'exp'=16] {'exp'}, dimensions={0} | all-to-all | bytes 917504 | tf_op jit(solution)/shard_map/all_to_all | solution.py:402
  113.2 8.6 %collective-permute-done.15.side = bf16[32,7168]{1,0:T(8,128)(2,1)S(1)} collective-permute-done((bf16[32,7168]{1,0:T(8,128)(2,1)S(1)}, bf16[32,7168]{1,0:T(8,128)(2,1)S(1)}, u32[]{:S(2)}, u32[]{:S(2)}) %collective-permute-start.15) | collective-permute-done | bytes 458784 | tf_op jit(solution)/shard_map/ppermute | solution.py:29
  125.4 2.7 %collective-permute-start.19 = (bf16[16,7168]{1,0:T(8,128)(2,1)S(1)}, bf16[16,7168]{1,0:T(8,128)(2,1)S(1)}, u32[]{:S(2)}, u32[]{:S(2)}) collective-permute-start(bf16[16,7168]{1,0:T(8,128)(2,1)S(1)} %slice.81), channel_id=1, source_target_pairs={{0,48},{16,0},{32,16},{48,32},{64,112},{80,64},{96,80},{112,96},{1... | collective-permute-start | bytes 688136 | tf_op jit(solution)/shard_map/ppermute | solution.py:29
  128.1 5.7 %collective-permute-done.16.side_down = bf16[32,7168]{1,0:T(8,128)(2,1)S(1)} collective-permute-done((bf16[32,7168]{1,0:T(8,128)(2,1)S(1)}, bf16[32,7168]{1,0:T(8,128)(2,1)S(1)}, u32[]{:S(2)}, u32[]{:S(2)}) %collective-permute-start.16) | collective-permute-done | bytes 458784 | tf_op jit(solution)/shard_map/ppermute | solution.py:29
  134.0 2.7 %collective-permute-start.21 = (bf16[16,7168]{1,0:T(8,128)(2,1)S(1)}, bf16[16,7168]{1,0:T(8,128)(2,1)S(1)}, u32[]{:S(2)}, u32[]{:S(2)}) collective-permute-start(bf16[16,7168]{1,0:T(8,128)(2,1)S(1)} %slice.83), channel_id=1, source_target_pairs={{0,48},{16,0},{32,16},{48,32},{64,112},{80,64},{96,80},{112,96},{1... | collective-permute-start | bytes 688136 | tf_op jit(solution)/shard_map/ppermute | solution.py:29
  138.8 4.9 %collective-permute-done.20.side_far_low = bf16[16,7168]{1,0:T(8,128)(2,1)S(1)} collective-permute-done((bf16[16,7168]{1,0:T(8,128)(2,1)S(1)}, bf16[16,7168]{1,0:T(8,128)(2,1)S(1)}, u32[]{:S(2)}, u32[]{:S(2)}) %collective-permute-start.20) | collective-permute-done | bytes 229408 | tf_op jit(solution)/shard_map/ppermute | solution.py:29
  143.7 8.3 %experts.1 = (bf16[32,7168]{1,0:T(8,128)(2,1)S(1)}, bf16[32,7168]{1,0:T(8,128)(2,1)S(1)}, bf16[32,7168]{1,0:T(8,128)(2,1)S(1)}, bf16[32,7168]{1,0:T(8,128)(2,1)S...) custom-call(bf16[32,7168]{1,0:T(8,128)(2,1)S(1)} %reshape.132.own, ...), custom_call_target="tpu_custom_call" | custom-call | flops 3000000000 | bytes 19000000 | tf_op jit(solution)/shard_map/experts/pallas_call | solution.py:260
  154.9 2.7 %collective-permute-start.28 = (bf16[16,7168]{1,0:T(8,128)(2,1)S(1)}, bf16[16,7168]{1,0:T(8,128)(2,1)S(1)}, u32[]{:S(2)}, u32[]{:S(2)}) collective-permute-start(bf16[16,7168]{1,0:T(8,128)(2,1)S(1)} %get-tuple-element.28), channel_id=1, source_target_pairs={{0,48},{16,0},{32,16},{48,32},{64,112},{80,64},{96,80},{112,96},{1... | collective-permute-start | bytes 688136 | tf_op jit(solution)/shard_map/ppermute | solution.py:29
  158.3 4.9 %collective-permute-done.26 = bf16[16,7168]{1,0:T(8,128)(2,1)S(1)} collective-permute-done((bf16[16,7168]{1,0:T(8,128)(2,1)S(1)}, bf16[16,7168]{1,0:T(8,128)(2,1)S(1)}, u32[]{:S(2)}, u32[]{:S(2)}) %collective-permute-start.26) | collective-permute-done | bytes 229408 | tf_op jit(solution)/shard_map/ppermute | solution.py:29
  163.5 2.7 %collective-permute-start.29 = (bf16[32,7168]{1,0:T(8,128)(2,1)S(1)}, bf16[32,7168]{1,0:T(8,128)(2,1)S(1)}, u32[]{:S(2)}, u32[]{:S(2)}) collective-permute-start(bf16[32,7168]{1,0:T(8,128)(2,1)S(1)} %pad_maximum_fusion.3), channel_id=1, source_target_pairs={{0,48},{16,0},{32,16},{48,32},{64,112},{80,64},{96,80},{112,96},{1... | collective-permute-start | bytes 1376264 | tf_op jit(solution)/shard_map/ppermute | solution.py:29
  167.1 15.6 %collective-permute-done.27 = bf16[32,7168]{1,0:T(8,128)(2,1)S(1)} collective-permute-done((bf16[32,7168]{1,0:T(8,128)(2,1)S(1)}, bf16[32,7168]{1,0:T(8,128)(2,1)S(1)}, u32[]{:S(2)}, u32[]{:S(2)}) %collective-permute-start.27) | collective-permute-done | bytes 458784 | tf_op jit(solution)/shard_map/ppermute | solution.py:29
  184.9 8.2 %collective-permute-done.30 = bf16[32,7168]{1,0:T(8,128)(2,1)S(1)} collective-permute-done((bf16[32,7168]{1,0:T(8,128)(2,1)S(1)}, bf16[32,7168]{1,0:T(8,128)(2,1)S(1)}, u32[]{:S(2)}, u32[]{:S(2)}) %collective-permute-start.30) | collective-permute-done | bytes 458784 | tf_op jit(solution)/shard_map/ppermute | solution.py:29
  195.4 11.5 %all-to-all-start.2 = ((bf16[16,2,7168]{2,1,0:T(2,128)(2,1)}), bf16[16,2,7168]{2,1,0:T(2,128)(2,1)S(1)}, u32[]{:S(2)}, u32[]{:S(2)}) async-start(bf16[16,2,7168]{2,1,0:T(2,128)(2,1)} %reshape.133), calls=%async_computation.2 | async-start | bytes 917504 | tf_op jit(solution)/shard_map/all_to_all | solution.py:412
  207.4 8.5 %all-to-all-done.2 = bf16[16,2,7168]{2,1,0:T(2,128)(2,1)S(1)} async-done(((bf16[16,2,7168]{2,1,0:T(2,128)(2,1)}), bf16[16,2,7168]{2,1,0:T(2,128)(2,1)S(1)}, u32[]{:S(2)}, u32[]{:S(2)}) %all-to-all-start.2) | async-done | bytes 458784 | tf_op jit(solution)/shard_map/all_to_all | solution.py:412
  (138 shorter events, 65.6 us)
Async XLA Ops:
  4.1 12.2 %collective-permute-start = (bf16[256,576]{1,0:T(8,128)(2,1)S(1)}, bf16[256,576]{1,0:T(8,128)(2,1)S(1)}, u32[]{:S(2)}, u32[]{:S(2)}) collective-permute-start(bf16[256,576]{1,0:T(8,128)(2,1)S(1)} %constant_dynamic-slice_fusion), channel_id=1, source_target_pairs={{0,16},{16,32},{32,48},{48,0},{64,80},{80,96},{96,112},{112,64},{1... | collective-permute-start | bytes 884744 | tf_op jit(solution)/shard_map/ppermute | solution.py:29
  6.6 10.3 %collective-permute-start.1 = (bf16[256,576]{1,0:T(8,128)(2,1)S(1)}, bf16[256,576]{1,0:T(8,128)(2,1)S(1)}, u32[]{:S(2)}, u32[]{:S(2)}) collective-permute-start(bf16[256,576]{1,0:T(8,128)(2,1)S(1)} %constant_dynamic-slice_fusion), channel_id=1, source_target_pairs={{0,48},{16,0},{32,16},{48,32},{64,112},{80,64},{96,80},{112,96},{1... | collective-permute-start | bytes 884744 | tf_op jit(solution)/shard_map/ppermute | solution.py:29
  8.8 11.5 %collective-permute-start.2 = (bf16[256,576]{1,0:T(8,128)(2,1)S(1)}, bf16[256,576]{1,0:T(8,128)(2,1)}, u32[]{:S(2)}, u32[]{:S(2)}) collective-permute-start(bf16[256,576]{1,0:T(8,128)(2,1)S(1)} %constant_dynamic-slice_fusion), channel_id=1, source_target_pairs={{0,64},{16,80},{32,96},{48,112},{64,0},{80,16},{96,32},{112,48},{1... | collective-permute-start | bytes 884744 | tf_op jit(solution)/shard_map/ppermute | solution.py:29
  16.9 14.7 %collective-permute-start.6 = (bf16[128,576]{1,0:T(8,128)(2,1)}, bf16[128,576]{1,0:T(8,128)(2,1)}, u32[]{:S(2)}, u32[]{:S(2)}) collective-permute-start(bf16[128,576]{1,0:T(8,128)(2,1)} %slice.76), channel_id=1, source_target_pairs={{0,16},{16,32},{32,48},{48,0},{64,80},{80,96},{96,112},{112,64},{1... | collective-permute-start | bytes 442376 | tf_op jit(solution)/shard_map/ppermute | solution.py:29
  17.6 15.0 %collective-permute-start.7 = (bf16[128,576]{1,0:T(8,128)(2,1)}, bf16[128,576]{1,0:T(8,128)(2,1)}, u32[]{:S(2)}, u32[]{:S(2)}) collective-permute-start(bf16[128,576]{1,0:T(8,128)(2,1)} %slice.77), channel_id=1, source_target_pairs={{0,48},{16,0},{32,16},{48,32},{64,112},{80,64},{96,80},{112,96},{1... | collective-permute-start | bytes 442376 | tf_op jit(solution)/shard_map/ppermute | solution.py:29
  20.3 10.3 %collective-permute-start.5 = (bf16[256,576]{1,0:T(8,128)(2,1)}, bf16[256,576]{1,0:T(8,128)(2,1)}, u32[]{:S(2)}, u32[]{:S(2)}) collective-permute-start(bf16[256,576]{1,0:T(8,128)(2,1)} %collective-permute-done.2), channel_id=1, source_target_pairs={{0,48},{16,0},{32,16},{48,32},{64,112},{80,64},{96,80},{112,96},{1... | collective-permute-start | bytes 884744 | tf_op jit(solution)/shard_map/ppermute | solution.py:29
  25.4 25.8 %collective-permute-start.3 = (bf16[768,576]{0,1:T(8,128)(2,1)}, bf16[768,576]{0,1:T(8,128)(2,1)}, u32[]{:S(2)}, u32[]{:S(2)}) collective-permute-start(bf16[768,576]{0,1:T(8,128)(2,1)} %copy.61), channel_id=1, source_target_pairs={{0,1},{1,0},{2,3},{3,2},{4,5},{5,4},{6,7},{7,6},{8,9},{9,8},{10,11... | collective-permute-start | bytes 2654216 | tf_op jit(solution)/shard_map/ppermute | solution.py:33
  34.9 18.6 %collective-permute-start.8 = (bf16[768,576]{0,1:T(8,128)(2,1)}, bf16[768,576]{0,1:T(8,128)(2,1)}, u32[]{:S(2)}, u32[]{:S(2)}) collective-permute-start(bf16[768,576]{0,1:T(8,128)(2,1)} %copy.62), channel_id=1, source_target_pairs={{0,1},{1,0},{2,3},{3,2},{4,5},{5,4},{6,7},{7,6},{8,9},{9,8},{10,11... | collective-permute-start | bytes 2654216 | tf_op jit(solution)/shard_map/ppermute | solution.py:33
  76.5 19.5 %all-to-all-start = ((bf16[8,8,7168]{2,1,0:T(8,128)(2,1)}), bf16[8,8,7168]{2,1,0:T(8,128)(2,1)S(1)}, u32[]{:S(2)}, u32[]{:S(2)}) async-start(bf16[8,8,7168]{2,1,0:T(8,128)(2,1)} %fusion.4), calls=%async_computation | async-start | bytes 1835008 | tf_op jit(solution)/shard_map/all_to_all | solution.py:372
  109.5 12.3 %collective-permute-start.15 = (bf16[32,7168]{1,0:T(8,128)(2,1)S(1)}, bf16[32,7168]{1,0:T(8,128)(2,1)S(1)}, u32[]{:S(2)}, u32[]{:S(2)}) collective-permute-start(bf16[32,7168]{1,0:T(8,128)(2,1)S(1)} %reshape.132.own), channel_id=1, source_target_pairs={{0,64},{16,80},{32,96},{48,112},{64,0},{80,16},{96,32},{112,48},{1... | collective-permute-start | bytes 1376264 | tf_op jit(solution)/shard_map/ppermute | solution.py:29
  109.6 15.6 %collective-permute-start.13 = (bf16[32,7168]{1,0:T(8,128)(2,1)S(1)}, bf16[32,7168]{1,0:T(8,128)(2,1)S(1)}, u32[]{:S(2)}, u32[]{:S(2)}) collective-permute-start(bf16[32,7168]{1,0:T(8,128)(2,1)S(1)} %reshape.132.own), channel_id=1, source_target_pairs={{0,16},{16,32},{32,48},{48,0},{64,80},{80,96},{96,112},{112,64},{1... | collective-permute-start | bytes 1376264 | tf_op jit(solution)/shard_map/ppermute | solution.py:29
  111.2 14.1 %collective-permute-start.14 = (bf16[32,7168]{1,0:T(8,128)(2,1)S(1)}, bf16[32,7168]{1,0:T(8,128)(2,1)S(1)}, u32[]{:S(2)}, u32[]{:S(2)}) collective-permute-start(bf16[32,7168]{1,0:T(8,128)(2,1)S(1)} %reshape.132.own), channel_id=1, source_target_pairs={{0,48},{16,0},{32,16},{48,32},{64,112},{80,64},{96,80},{112,96},{1... | collective-permute-start | bytes 1376264 | tf_op jit(solution)/shard_map/ppermute | solution.py:29
  121.8 12.0 %collective-permute-start.16 = (bf16[32,7168]{1,0:T(8,128)(2,1)S(1)}, bf16[32,7168]{1,0:T(8,128)(2,1)S(1)}, u32[]{:S(2)}, u32[]{:S(2)}) collective-permute-start(bf16[32,7168]{1,0:T(8,128)(2,1)S(1)} %collective-permute-done.15.side), channel_id=1, source_target_pairs={{0,16},{16,32},{32,48},{48,0},{64,80},{80,96},{96,112},{112,64},{1... | collective-permute-start | bytes 1376264 | tf_op jit(solution)/shard_map/ppermute | solution.py:29
  123.3 10.6 %collective-permute-start.17 = (bf16[32,7168]{1,0:T(8,128)(2,1)S(1)}, bf16[32,7168]{1,0:T(8,128)(2,1)S(1)}, u32[]{:S(2)}, u32[]{:S(2)}) collective-permute-start(bf16[32,7168]{1,0:T(8,128)(2,1)S(1)} %collective-permute-done.15.side), channel_id=1, source_target_pairs={{0,48},{16,0},{32,16},{48,32},{64,112},{80,64},{96,80},{112,96},{1... | collective-permute-start | bytes 1376264 | tf_op jit(solution)/shard_map/ppermute | solution.py:29
  125.3 13.5 %collective-permute-start.18 = (bf16[16,7168]{1,0:T(8,128)(2,1)S(1)}, bf16[16,7168]{1,0:T(8,128)(2,1)S(1)}, u32[]{:S(2)}, u32[]{:S(2)}) collective-permute-start(bf16[16,7168]{1,0:T(8,128)(2,1)S(1)} %slice.80), channel_id=1, source_target_pairs={{0,16},{16,32},{32,48},{48,0},{64,80},{80,96},{96,112},{112,64},{1... | collective-permute-start | bytes 688136 | tf_op jit(solution)/shard_map/ppermute | solution.py:29
  125.4 13.4 %collective-permute-start.19 = (bf16[16,7168]{1,0:T(8,128)(2,1)S(1)}, bf16[16,7168]{1,0:T(8,128)(2,1)S(1)}, u32[]{:S(2)}, u32[]{:S(2)}) collective-permute-start(bf16[16,7168]{1,0:T(8,128)(2,1)S(1)} %slice.81), channel_id=1, source_target_pairs={{0,48},{16,0},{32,16},{48,32},{64,112},{80,64},{96,80},{112,96},{1... | collective-permute-start | bytes 688136 | tf_op jit(solution)/shard_map/ppermute | solution.py:29
  133.9 9.8 %collective-permute-start.20 = (bf16[16,7168]{1,0:T(8,128)(2,1)S(1)}, bf16[16,7168]{1,0:T(8,128)(2,1)S(1)}, u32[]{:S(2)}, u32[]{:S(2)}) collective-permute-start(bf16[16,7168]{1,0:T(8,128)(2,1)S(1)} %slice.82), channel_id=1, source_target_pairs={{0,16},{16,32},{32,48},{48,0},{64,80},{80,96},{96,112},{112,64},{1... | collective-permute-start | bytes 688136 | tf_op jit(solution)/shard_map/ppermute | solution.py:29
  152.5 13.7 %collective-permute-start.24 = (bf16[16,7168]{1,0:T(8,128)(2,1)S(1)}, bf16[16,7168]{1,0:T(8,128)(2,1)S(1)}, u32[]{:S(2)}, u32[]{:S(2)}) collective-permute-start(bf16[16,7168]{1,0:T(8,128)(2,1)S(1)} %get-tuple-element.23), channel_id=1, source_target_pairs={{0,48},{16,0},{32,16},{48,32},{64,112},{80,64},{96,80},{112,96},{1... | collective-permute-start | bytes 688136 | tf_op jit(solution)/shard_map/ppermute | solution.py:29
  158.2 26.7 %collective-permute-start.23 = (bf16[32,7168]{1,0:T(8,128)(2,1)S(1)}, bf16[32,7168]{1,0:T(8,128)(2,1)}, u32[]{:S(2)}, u32[]{:S(2)}) collective-permute-start(bf16[32,7168]{1,0:T(8,128)(2,1)S(1)} %pad_maximum_fusion), channel_id=1, source_target_pairs={{0,16},{16,32},{32,48},{48,0},{64,80},{80,96},{96,112},{112,64},{1... | collective-permute-start | bytes 1376264 | tf_op jit(solution)/shard_map/ppermute | solution.py:29
  163.3 19.5 %collective-permute-start.27 = (bf16[32,7168]{1,0:T(8,128)(2,1)S(1)}, bf16[32,7168]{1,0:T(8,128)(2,1)S(1)}, u32[]{:S(2)}, u32[]{:S(2)}) collective-permute-start(bf16[32,7168]{1,0:T(8,128)(2,1)S(1)} %pad_maximum_fusion.2), channel_id=1, source_target_pairs={{0,16},{16,32},{32,48},{48,0},{64,80},{80,96},{96,112},{112,64},{1... | collective-permute-start | bytes 1376264 | tf_op jit(solution)/shard_map/ppermute | solution.py:29
  163.5 19.3 %collective-permute-start.29 = (bf16[32,7168]{1,0:T(8,128)(2,1)S(1)}, bf16[32,7168]{1,0:T(8,128)(2,1)S(1)}, u32[]{:S(2)}, u32[]{:S(2)}) collective-permute-start(bf16[32,7168]{1,0:T(8,128)(2,1)S(1)} %pad_maximum_fusion.3), channel_id=1, source_target_pairs={{0,48},{16,0},{32,16},{48,32},{64,112},{80,64},{96,80},{112,96},{1... | collective-permute-start | bytes 1376264 | tf_op jit(solution)/shard_map/ppermute | solution.py:29
  167.1 17.8 %collective-permute-start.25 = (bf16[32,7168]{1,0:T(8,128)(2,1)}, bf16[32,7168]{1,0:T(8,128)(2,1)}, u32[]{:S(2)}, u32[]{:S(2)}) collective-permute-start(bf16[32,7168]{1,0:T(8,128)(2,1)} %pad_maximum_fusion.1), channel_id=1, source_target_pairs={{0,48},{16,0},{32,16},{48,32},{64,112},{80,64},{96,80},{112,96},{1... | collective-permute-start | bytes 1376264 | tf_op jit(solution)/shard_map/ppermute | solution.py:29
  183.0 10.1 %collective-permute-start.30 = (bf16[32,7168]{1,0:T(8,128)(2,1)S(1)}, bf16[32,7168]{1,0:T(8,128)(2,1)S(1)}, u32[]{:S(2)}, u32[]{:S(2)}) collective-permute-start(bf16[32,7168]{1,0:T(8,128)(2,1)S(1)} %add_convert_fusion.2), channel_id=1, source_target_pairs={{0,64},{16,80},{32,96},{48,112},{64,0},{80,16},{96,32},{112,48},{1... | collective-permute-start | bytes 1376264 | tf_op jit(solution)/shard_map/ppermute | solution.py:29
  195.4 20.5 %all-to-all-start.2 = ((bf16[16,2,7168]{2,1,0:T(2,128)(2,1)}), bf16[16,2,7168]{2,1,0:T(2,128)(2,1)S(1)}, u32[]{:S(2)}, u32[]{:S(2)}) async-start(bf16[16,2,7168]{2,1,0:T(2,128)(2,1)} %reshape.133), calls=%async_computation.2 | async-start | bytes 917504 | tf_op jit(solution)/shard_map/all_to_all | solution.py:412
  (17 other events, 316.3 us)

commit v2 on v0

v2 whole, which is shorter than its diff:
```python
import functools

import jax
import jax.numpy as jnp
from jax import lax
from jax.experimental import pallas as pl
from jax.experimental.pallas import tpu as pltpu
from jax.sharding import PartitionSpec as P

ROPE = 64
NOPE = 128
Y_HI, Z, Y_LO, X, CORES = 2, 4, 2, 4, 2
STEP_BLOCKS = 4
VMEM_LIMIT = 40 * 2**20
HEADS_HERE = 4
F32 = jnp.float32
BF16 = jnp.bfloat16


def ctx_pairs(move):
    pairs = []
    for y in range(Y_HI):
        for z in range(Z):
            for i in range(Y_LO * X * CORES):
                to_y, to_z = move(y, z, 1 - 2 * (i % CORES))
                pairs.append(
                    (
                        (y * Z + z) * Y_LO * X * CORES + i,
                        (to_y * Z + to_z) * Y_LO * X * CORES + i,
                    )
                )
    return pairs


AHEAD = ctx_pairs(lambda y, z, way: (y, (z + way) % Z))
BACK = ctx_pairs(lambda y, z, way: (y, (z - way) % Z))
ACROSS = ctx_pairs(lambda y, z, way: (1 - y, z))
CORE_SWAP = [(i, i ^ 1) for i in range(Y_LO * X * CORES)]
SAME_CORE = [[2 * i + core for i in range(Y_LO * X)] for core in range(CORES)]


def over_ctx(value, pairs):
    return lax.ppermute(value, ("ctx", "exp"), pairs)


def core_swap(value):
    return lax.ppermute(value, "exp", CORE_SWAP)


def power_two(powers):
    return jnp.where(powers < 0, 0.5, jnp.where(powers > 0, 2.0, 1.0)).astype(jnp.float32)


def attend(live, first_flag, queries, steps, diagonal, scores, top, total, mixture):
    rows = queries.shape[0]
    latent_width = mixture.shape[1]
    block = top.shape[1]
    factor = 1.4426950408889634 / (NOPE + ROPE) ** 0.5
    top[...] = jnp.full_like(top, -1e30)
    total[...] = jnp.zeros_like(total)
    mixture[...] = jnp.zeros_like(mixture)

    def keys_of(step, height):
        return jnp.concatenate([part[i, :height] for part, i in step], axis=1)

    def lane_fold(value, fold):
        folded = value[:, :block]
        for i in range(1, STEP_BLOCKS):
            folded = fold(folded, value[:, i * block : (i + 1) * block])
        return folded

    def flags_of(number):
        return [live[first_flag + STEP_BLOCKS * number + i] for i in range(STEP_BLOCKS)]

    def score(step, number):
        flags = flags_of(number)

        @pl.when(sum(flags) > 0)
        def _():
            found = jnp.dot(
                queries[...], keys_of(step, queries.shape[1]), preferred_element_type=F32
            )
            column = lax.broadcasted_iota(jnp.int32, (1, STEP_BLOCKS * block), 1) // block
            shown = jnp.zeros(column.shape, jnp.int32)
            for i, flag in enumerate(flags):
                shown = jnp.where(column == i, flag, shown)
            found = jnp.where(shown > 0, found, -1e30)
            if diagonal and number == 0:
                last = (STEP_BLOCKS - 1) * block
                seen = jnp.where(causal(), found[:, last:], -1e30)
                found = jnp.concatenate([found[:, :last], seen], axis=1)
            scores[number] = found
            top[...] = jnp.maximum(top[...], lane_fold(found, jnp.maximum))

    def causal():
        tokens = rows // HEADS_HERE
        row = lax.broadcasted_iota(jnp.int32, (rows, 1), 0) % tokens
        relative = row // (tokens // 2)
        within = row % (tokens // 2)
        side = jnp.where(relative == 0, live[live.shape[0] - 1], 1 - live[live.shape[0] - 1])
        token = within // 8 * 16 + side * 8 + within % 8
        return lax.broadcasted_iota(jnp.int32, (1, block), 1) <= token

    for number, step in enumerate(steps):
        score(step, number)
    row_top = jnp.max(top[...], axis=1, keepdims=True)

    def mix(step, number):
        @pl.when(sum(flags_of(number)) > 0)
        def _():
            weights = jnp.exp2((scores[number] - row_top) * factor)
            total[...] += lane_fold(weights, jnp.add)
            mixture[...] += lax.dot_general(
                weights.astype(BF16),
                keys_of(step, latent_width),
                (((1,), (1,)), ((), ())),
                preferred_element_type=F32,
            )

    for number, step in enumerate(steps):
        mix(step, number)
    return row_top


def near_kernel(
    live, queries, own, beside, beside_other, side, side_other, top, total, mixture, done, scores
):
    steps = [[(part, i) for i in range(STEP_BLOCKS)] for part in (own, beside, beside_other)]
    steps.append([(part, i) for part in (side, side_other) for i in range(STEP_BLOCKS // 2)])
    row_top = attend(live, 0, queries, steps, True, scores, top, total, mixture)
    top[...] = jnp.broadcast_to(row_top, top.shape)
    done[...] = jnp.ones_like(done)


def far_kernel(
    live, queries, beside, beside_other, far, far_other, side_far, side_far_other,
    near_top, near_total, near_mixture, value_up, weight_hbm,
    out_keep, out_send, scores, top, total, mixture, weight, weight_sem,
):
    copy = pltpu.make_async_copy(weight_hbm, weight, weight_sem)
    copy.start()
    heads = value_up.shape[0]
    tokens = queries.shape[0] // heads
    factor = 1.4426950408889634 / (NOPE + ROPE) ** 0.5
    steps = [[(part, i) for i in range(STEP_BLOCKS)] for part in (beside, beside_other)]
    for halves in ((far, far_other), (side_far, side_far_other)):
        steps.append([(part, i) for part in halves for i in range(STEP_BLOCKS // 2)])
    far_top = attend(
        live, 4 * STEP_BLOCKS, queries, steps, False, scores, top, total, mixture
    )
    near_row_top = near_top[:, :1]
    both_top = jnp.maximum(near_row_top, far_top)
    near_scale = jnp.exp2((near_row_top - both_top) * factor)
    far_scale = jnp.exp2((far_top - both_top) * factor)
    row_total = jnp.sum(near_total[...] * near_scale + total[...] * far_scale, axis=1, keepdims=True)
    near_scale = near_scale / row_total
    far_scale = far_scale / row_total
    per_head = []
    for head in range(heads):
        span = slice(head * tokens, (head + 1) * tokens)
        attended = near_mixture[span] * near_scale[span] + mixture[span] * far_scale[span]
        per_head.append(
            jnp.dot(
                attended.astype(BF16), value_up[head], preferred_element_type=F32
            ).astype(BF16)
        )
    flat_heads = jnp.concatenate(per_head, axis=1)
    copy.wait()
    out_width = 1024
    half = tokens // 2

    @pl.loop(0, weight.shape[1] // out_width)
    def _(step):
        columns = pl.ds(pl.multiple_of(step * out_width, out_width), out_width)
        term = jnp.dot(flat_heads, weight[:, columns], preferred_element_type=F32)
        out_keep[:, columns] = term[:half].astype(BF16)
        out_send[:, columns] = term[half:].astype(BF16)


def score_scratch(blocks, rows, block):
    return pltpu.VMEM((blocks // STEP_BLOCKS, rows, STEP_BLOCKS * block), F32)


def near_call(live, queries, near, value_up):
    rows, block = queries.shape[0], near[0].shape[2]
    vmem = pl.BlockSpec(memory_space=pltpu.VMEM)
    lanes = jax.ShapeDtypeStruct((rows, block), F32)
    return pl.pallas_call(
        near_kernel,
        out_shape=(
            lanes,
            lanes,
            jax.ShapeDtypeStruct((rows, value_up.shape[1]), F32),
            jax.ShapeDtypeStruct((8, block), F32),
        ),
        in_specs=[pl.BlockSpec(memory_space=pltpu.SMEM)] + [vmem] * (1 + len(near)),
        out_specs=(vmem,) * 4,
        scratch_shapes=[score_scratch(sum(part.shape[0] for part in near), rows, block)],
        compiler_params=pltpu.CompilerParams(vmem_limit_bytes=VMEM_LIMIT),
        cost_estimate=pl.CostEstimate(
            flops=3 * 10**9, bytes_accessed=6 * 10**6, transcendentals=10**6
        ),
        name="attention_near",
    )(live, queries, *near)


def far_call(live, queries, far, state, value_up, output_weight):
    rows, block = queries.shape[0], far[0].shape[2]
    tokens = rows // value_up.shape[0]
    vmem = pl.BlockSpec(memory_space=pltpu.VMEM)
    out = jax.ShapeDtypeStruct((tokens // 2, output_weight.shape[1]), BF16)
    return pl.pallas_call(
        far_kernel,
        out_shape=(out, out),
        in_specs=[pl.BlockSpec(memory_space=pltpu.SMEM)]
        + [vmem] * 11
        + [pl.BlockSpec(memory_space=pltpu.HBM)],
        out_specs=(vmem, vmem),
        scratch_shapes=[
            score_scratch(sum(part.shape[0] for part in far), rows, block),
            pltpu.VMEM((rows, block), F32),
            pltpu.VMEM((rows, block), F32),
            pltpu.VMEM((rows, value_up.shape[1]), F32),
            pltpu.VMEM(output_weight.shape, BF16),
            pltpu.SemaphoreType.DMA,
        ],
        compiler_params=pltpu.CompilerParams(vmem_limit_bytes=49 * 2**20),
        cost_estimate=pl.CostEstimate(
            flops=4 * 10**9, bytes_accessed=14 * 10**6, transcendentals=10**6
        ),
        name="attention_far",
    )(live, queries, *far, *state, value_up, output_weight)


def own_half(blocks, core):
    half_blocks = blocks.shape[0] // 2
    return lax.dynamic_slice_in_dim(blocks, core * half_blocks, half_blocks, 0)


def gather_codes(blocks, core):
    side = over_ctx(own_half(blocks, core), ACROSS)
    beside = over_ctx(blocks, AHEAD)
    beside_half = own_half(beside, core)
    far = over_ctx(beside_half, AHEAD)
    side_other, _ = lax.optimization_barrier((core_swap(side), beside_half))
    side_beside = over_ctx(jnp.concatenate([side, side_other], axis=0), AHEAD)
    side_far = over_ctx(far, ACROSS)
    near = (blocks, beside, core_swap(beside), side, side_other)

    def far_blocks(done):
        held = side_far * done[0, 0].astype(BF16)
        swapped = [core_swap(part) for part in (side_beside, far, held)]
        return (side_beside, swapped[0], far, swapped[1], held, swapped[2])

    return near, far_blocks


def block_flags(block_mask, ctx_index, core, prior_blocks):
    owners = block_mask.shape[0]
    mask_row = lax.dynamic_index_in_dim(block_mask, ctx_index, 0, keepdims=False)
    prior = mask_row[: owners * prior_blocks].reshape(owners, prior_blocks)
    fresh = mask_row[owners * prior_blocks :].reshape(owners, 1)
    flags = jnp.concatenate([prior, fresh], axis=1)
    half = flags.shape[1] // 2
    y, z = ctx_index // Z, ctx_index % Z
    way = 1 - 2 * core

    def of(dy, dz):
        owner = (y + dy) % Y_HI * Z + (z + dz) % Z
        return jnp.sum(jnp.where(jnp.arange(owners)[:, None] == owner, flags, 0), axis=0)

    def mine_first(found):
        return jnp.where(core == 0, found, jnp.roll(found, half))

    ordered = (
        of(0, 0),
        of(0, -way),
        of(0, way),
        mine_first(of(1, 0)),
        mine_first(of(1, -way)),
        jnp.roll(mine_first(of(1, way)), half),
        mine_first(of(0, 2)),
        mine_first(of(1, 2)),
    )
    return jnp.concatenate(ordered + (core[None],)).astype(jnp.int32)


def store_rows(results, columns, term):
    at = 0
    for result in results:
        result[:, columns] = term[at : at + result.shape[0]].astype(BF16)
        at += result.shape[0]


def experts_kernel(count, holds, *refs):
    sources, weights_in = refs[:count], refs[count : count + 3]
    results = refs[count + 3 : 2 * count + 3]
    if holds:
        gate_weight, up_weight, down_weight, rows, sems = refs[2 * count + 3 :]
    else:
        gate_weight, up_weight, down_weight = weights_in
        (rows,) = refs[2 * count + 3 :]
    cuts = 4
    depth = rows.shape[1] // cuts
    width = depth // 2

    def weight_copy(kind, cut):
        span = slice(cut * depth, (cut + 1) * depth)
        source, target = weights_in[kind], (gate_weight, up_weight, down_weight)[kind]
        if kind == 2:
            return pltpu.make_async_copy(
                source.at[0, :, span], target.at[:, span], sems.at[kind, cut]
            )
        return pltpu.make_async_copy(source.at[0, span], target.at[span], sems.at[kind, cut])

    def arrived(kind, cut):
        if holds:
            weight_copy(kind, cut).wait()

    if holds:
        for cut in range(cuts):
            weight_copy(0, cut).start()
            weight_copy(1, cut).start()
        for cut in range(cuts):
            weight_copy(2, cut).start()
    at = 0
    for source in sources:
        rows[at : at + source.shape[0], :] = source[...]
        at += source.shape[0]
    gate_proj, up_proj = None, None
    for cut in range(cuts):
        span = slice(cut * depth, (cut + 1) * depth)
        arrived(0, cut)
        arrived(1, cut)
        gate_part = jnp.dot(rows[:, span], gate_weight[span], preferred_element_type=F32)
        up_part = jnp.dot(rows[:, span], up_weight[span], preferred_element_type=F32)
        gate_proj = gate_part if cut == 0 else gate_proj + gate_part
        up_proj = up_part if cut == 0 else up_proj + up_part
    inner_act = (gate_proj / (1.0 + jnp.exp(-gate_proj)) * up_proj).astype(BF16)
    for cut in range(cuts):
        arrived(2, cut)
        for part in range(2):
            columns = slice(cut * depth + part * width, cut * depth + (part + 1) * width)
            term = jnp.dot(inner_act, down_weight[:, columns], preferred_element_type=F32)
            store_rows(results, columns, term)


def experts_call(blocks, weights, holds, name):
    vmem = pl.BlockSpec(memory_space=pltpu.VMEM)
    anywhere = pl.BlockSpec(memory_space=pltpu.HBM)
    row_count = sum(block.shape[0] for block in blocks)
    out_shape = [jax.ShapeDtypeStruct(block.shape, BF16) for block in blocks]
    scratch = [pltpu.VMEM((row_count, blocks[0].shape[1]), BF16)]
    if holds:
        out_shape += [jax.ShapeDtypeStruct(weight.shape[1:], BF16) for weight in weights]
        scratch.append(pltpu.SemaphoreType.DMA((3, 4)))
    found = pl.pallas_call(
        functools.partial(experts_kernel, len(blocks), holds),
        out_shape=tuple(out_shape),
        in_specs=[vmem] * len(blocks) + [anywhere if holds else vmem] * 3,
        out_specs=tuple([vmem] * len(out_shape)),
        scratch_shapes=scratch,
        compiler_params=pltpu.CompilerParams(vmem_limit_bytes=VMEM_LIMIT),
        cost_estimate=pl.CostEstimate(
            flops=15 * 10**8, bytes_accessed=15 * 10**6, transcendentals=32768
        ),
        name=name,
    )(*blocks, *weights)
    return found[: len(blocks)], found[len(blocks) :]


def gather_rows(own):
    side = over_ctx(own, ACROSS)
    ahead = over_ctx(own, AHEAD)
    back = over_ctx(own, BACK)
    far = over_ctx(ahead, AHEAD)
    side_now, _ = lax.optimization_barrier((side, ahead))
    side_ahead = over_ctx(side_now, AHEAD)
    side_back = over_ctx(side_now, BACK)
    side_far = over_ctx(far, ACROSS)
    return (ahead, back, side), (far, side_ahead, side_back, side_far)


def added(*terms):
    total = terms[0].astype(F32)
    for term in terms[1:]:
        total = total + term.astype(F32)
    return total.astype(BF16)


def reduce_rows(own, near, far):
    ahead, back, side = near
    far, side_ahead, side_back, side_far = far
    side_far_in = over_ctx(side_far, ACROSS)
    side_ahead_in = over_ctx(side_ahead, BACK)
    side_back_in = over_ctx(side_back, AHEAD)
    far_in = over_ctx(added(far, side_far_in), BACK)
    side_in = over_ctx(added(side, side_ahead_in, side_back_in), ACROSS)
    back_in = over_ctx(back, AHEAD)
    ahead_in = over_ctx(added(ahead, far_in), BACK)
    return added(own, back_in, side_in, ahead_in)


def on_device(
    queries,
    prior_codes,
    fresh_codes,
    prior_powers,
    fresh_powers,
    block_mask,
    value_up,
    output_weight,
    residual,
    norm_gain,
    router,
    route_ids,
    gate_weight,
    up_weight,
    down_weight,
):
    ctx_index = lax.axis_index("ctx")
    core = lax.axis_index("exp") % CORES
    rows_block, head_count, key_width = queries.shape
    prior_blocks = prior_powers.shape[0]
    scales = power_two(jnp.concatenate([prior_powers, fresh_powers], axis=0))
    blocks_here = jnp.concatenate(
        [jnp.transpose(prior_codes), jnp.transpose(fresh_codes)], axis=1
    ).reshape(key_width, prior_blocks + 1, rows_block)
    blocks_here = jnp.transpose(blocks_here, (1, 0, 2)).astype(F32)
    blocks_here = (blocks_here * scales[:, None, None]).astype(BF16)
    near, far_blocks = gather_codes(blocks_here, core)
    live = block_flags(block_mask, ctx_index, core, prior_blocks)
    groups = rows_block // 16
    split = queries.reshape(groups, 2, 8, head_count, key_width)
    first = jnp.where(core == 0, split[:, 0], split[:, 1])
    second = jnp.where(core == 0, split[:, 1], split[:, 0])
    ordered = jnp.stack([first, second], axis=0)
    ordered = jnp.transpose(ordered, (3, 0, 1, 2, 4)).reshape(head_count * rows_block, key_width)

    state = near_call(live, ordered, near, value_up)
    *state, done = state
    far = far_blocks(done)
    keep, send = far_call(live, ordered, far, state, value_up, output_weight)
    expert_count = router.shape[1]
    token_count, route_count = route_ids.shape
    capacity = token_count * route_count * 2 // expert_count
    route_hits = route_ids[:, :, None] == jnp.arange(expert_count)[None, None, :]
    flat_hits = route_hits.reshape(token_count * route_count, expert_count).astype(jnp.int32)
    before = jnp.cumsum(flat_hits, axis=0) - flat_hits
    slot_index = jnp.sum(before * flat_hits, axis=1)
    target = route_ids.reshape(-1) * capacity + slot_index
    placing = (target[None, :] == jnp.arange(expert_count * capacity)[:, None]).astype(BF16)
    placing_back = jnp.transpose(placing)
    gain = norm_gain.astype(F32)
    keep, send, placing, placing_back, route_ids, gain = lax.optimization_barrier(
        (keep, send, placing, placing_back, route_ids, gain)
    )
    paired = added(keep, core_swap(send))
    model_width = residual.shape[1]
    pieces = lax.all_to_all(
        paired.reshape(groups, 8, model_width),
        "exp",
        split_axis=0,
        concat_axis=0,
        tiled=True,
        axis_index_groups=SAME_CORE,
    )
    attention = jnp.sum(pieces.astype(F32), axis=0)
    hidden = (residual.astype(F32) + attention).astype(BF16)
    hidden_wide = hidden.astype(F32)
    normed = (
        hidden_wide
        * lax.rsqrt(jnp.mean(hidden_wide * hidden_wide, axis=1, keepdims=True) + 1e-06)
        * gain
    ).astype(BF16)
    affinity = jax.nn.sigmoid(jnp.dot(normed, router, preferred_element_type=F32))
    route_hits = route_ids[:, :, None] == jnp.arange(expert_count)[None, None, :]
    chosen = jnp.sum(jnp.where(route_hits, affinity[:, None, :], 0.0), axis=2)
    gate_values = 2.5 * chosen / jnp.sum(chosen, axis=1, keepdims=True)
    repeated = jnp.repeat(normed, route_count, axis=0)
    buffer = jnp.dot(placing, repeated, preferred_element_type=F32).astype(BF16)
    sectioned = lax.all_to_all(
        buffer.reshape(expert_count, capacity, model_width),
        "exp",
        split_axis=0,
        concat_axis=0,
        tiled=True,
    )
    own_rows = sectioned.reshape(expert_count * capacity, model_width)
    near_rows, far_rows = gather_rows(own_rows)
    near_terms, weights = experts_call(
        (own_rows,) + near_rows, (gate_weight, up_weight, down_weight), True, "experts_near"
    )
    far_terms, _ = experts_call(far_rows, weights, False, "experts_far")
    summed = reduce_rows(near_terms[0], near_terms[1:], far_terms)
    summed, gate_values, hidden = lax.optimization_barrier((summed, gate_values, hidden))
    returned = lax.all_to_all(
        summed.reshape(expert_count, capacity, model_width),
        "exp",
        split_axis=0,
        concat_axis=0,
        tiled=True,
    ).reshape(expert_count * capacity, model_width)
    gathered_back = jnp.dot(
        placing_back, returned, preferred_element_type=F32
    ).reshape(token_count, route_count, model_width)
    expert_mix = jnp.sum(gate_values[:, :, None] * gathered_back, axis=1)
    return (hidden.astype(F32) + expert_mix).astype(BF16)


def solution(mesh):
    in_specs = (
        P("ctx", "exp", None),
        P("ctx", None),
        P("ctx", None),
        P("ctx"),
        P("ctx"),
        P(),
        P("exp", None, None),
        P("exp", None),
        P(("ctx", "exp"), None),
        P(),
        P(),
        P(("ctx", "exp"), None),
        P("exp", None, "ctx"),
        P("exp", None, "ctx"),
        P("exp", "ctx", None),
    )
    out_specs = P(("ctx", "exp"), None)
    return jax.shard_map(
        on_device, mesh=mesh, in_specs=in_specs, out_specs=out_specs, check_vma=False
    )
```

time: 450 us -> 171 us (0.38)
  waiting for transfers between devices: 256 us -> 50.2 us
  loops' own time: 53.4 us -> 0 us
  matrix products: 48.8 us -> 0.63 us
  blocking collectives: 15.8 us -> 47.7 us
  Pallas kernels: 0 us -> 25.6 us
  local copies, waits for them, and re-layouts: 30.7 us -> 5.7 us
  between operations: 22 us -> 1.11 us
  starting transfers between devices: 11.9 us -> 29.4 us
    all_gather x1 -> x0, waiting for transfers between devices: 66.4 us -> none  [on_device(): lax.all_gather(sectioned.reshape(expert_count * capacity, model_width), '...]
    reduce_scatter x1 -> x0, waiting for transfers between devices: 61.7 us -> none  [on_device(): lax.psum_scatter(head_term.astype(jnp.bfloat16), 'exp', scatter_dimension...]
    another operation x1 -> x0, loops' own time: 53.4 us -> none  [on_device(): lax.fori_loop(1, ctx_count, cycle_turn, (softmax_state, code_rows, scales))]
    dot_general x71 -> x3, matrix products: 48.8 us -> 0.63 us  [the longest x1 0.25 us: on_device(): buffer = jnp.dot(placing, repeated, preferred_element_type=F32).astype(BF16)]
    all_to_all x1 -> x0, waiting for transfers between devices: 46.4 us -> none  [on_device(): lax.all_to_all(partials, ('ctx', 'exp'), split_axis=0, concat_axis=0, til...]
    all_to_all x0 -> x2, blocking collectives: none -> 35.1 us  [the longest x1 19.1 us: on_device(): lax.all_to_all(paired.reshape(groups, 8, model_width), 'exp', split_axis=...]
    ppermute x14 -> x25, waiting for transfers between devices: 81.3 us -> 50.2 us  [the longest x19 46.7 us: over_ctx(): return lax.ppermute(value, ('ctx', 'exp'), pairs)]
    pallas_call x0 -> x4, Pallas kernels: none -> 25.6 us  [the longest x2 10.2 us: experts_call(): pl.pallas_call(functools.partial(experts_kernel, len(blocks), holds), out...]
  transfers between devices with their start and end apart: 17 -> 25, of which waited for: 10 -> 15; matrix products, arithmetic and copies ran while one was open for 2% -> 6% of each run, Pallas kernels for 0% -> 7%
where the time goes in v2:
time: 171 us
  waiting for transfers between devices  50.2 us (29%)
  blocking collectives  47.7 us (28%)
  starting transfers between devices  29.4 us (17%)
  Pallas kernels  25.6 us (15%)
  other arithmetic  10.3 us (6%)
  local copies, waits for them, and re-layouts  5.7 us (3%)
    ppermute x19, waiting for transfers between devices, over_ctx(): return lax.ppermute(value, ('ctx', 'exp'), pairs)  46.7 us
    ppermute x19, starting transfers between devices, over_ctx(): return lax.ppermute(value, ('ctx', 'exp'), pairs)  23.7 us
    all_to_all x1, blocking collectives, on_device(): lax.all_to_all(paired.reshape(groups, 8, model_width), 'exp', split_axis=...  19.1 us
    all_to_all x1, blocking collectives, on_device(): lax.all_to_all(summed.reshape(expert_count, capacity, model_width), 'exp'...  16 us
    all_to_all x1, blocking collectives, on_device(): lax.all_to_all(buffer.reshape(expert_count, capacity, model_width), 'exp'...  12.6 us
    pallas_call x2, Pallas kernels, experts_call(): pl.pallas_call(functools.partial(experts_kernel, len(blocks), holds), out...  10.2 us
    pallas_call x1, Pallas kernels, far_call(): pl.pallas_call(far_kernel, out_shape=(out, out), in_specs=[pl.BlockSpec(m...  9.71 us
    ppermute x6, starting transfers between devices, core_swap(): return lax.ppermute(value, 'exp', CORE_SWAP)  5.78 us
  transfers between devices with their start and end apart: 25, of which 15 were waited for; matrix products, arithmetic and copies ran while one was open for 6% of the time, Pallas kernels for 7%

profile of v2, /device:TPU:1, one launch (start us, length us, event | category | flops | bytes accessed | tf_op | source)
XLA Modules:
  0.0 170.6 jit_solution(6089773039072450347)
XLA Ops:
  2.8 3.8 %collective-permute-start = (bf16[2,576,128]{2,1,0:T(8,128)(2,1)S(1)}, bf16[2,576,128]{2,1,0:T(8,128)(2,1)S(1)}, u32[]{:S(2)}, u32[]{:S(2)}) collective-permute-start(bf16[2,576,128]{2,1,0:T(8,128)(2,1)S(1)} %dynamic-slice_bitcast_fusion), channel_id=1, source_target_pairs={{0,64},{1,65},{2,66},{3,67},{4,68},{5,69},{6,70},{7,71},{8,72},{9,... | collective-permute-start | bytes 884744 | tf_op jit(solution)/shard_map/ppermute | solution.py:43
  6.8 3.8 %collective-permute-start.2 = (bf16[4,576,128]{2,1,0:T(8,128)(2,1)S(1)}, bf16[4,576,128]{2,1,0:T(8,128)(2,1)S(1)}, u32[]{:S(2)}, u32[]{:S(2)}) collective-permute-start(bf16[4,576,128]{2,1,0:T(8,128)(2,1)S(1)} %fusion.26.own), channel_id=1, source_target_pairs={{0,16},{1,49},{2,18},{3,51},{4,20},{5,53},{6,22},{7,55},{8,24},{9,... | collective-permute-start | bytes 1769480 | tf_op jit(solution)/shard_map/ppermute | solution.py:43
  17.5 2.3 %collective-permute-start.8 = (bf16[4,576,128]{2,1,0:T(8,128)(2,1)S(1)}, bf16[4,576,128]{2,1,0:T(8,128)(2,1)}, u32[]{:S(2)}, u32[]{:S(2)}) collective-permute-start(bf16[4,576,128]{2,1,0:T(8,128)(2,1)S(1)} %collective-permute-done.2.beside), channel_id=1, source_target_pairs={{0,1},{1,0},{2,3},{3,2},{4,5},{5,4},{6,7},{7,6},{8,9},{9,8},{10,11... | collective-permute-start | bytes 1769480 | tf_op jit(solution)/shard_map/ppermute | solution.py:47
  22.6 3.1 %collective-permute-done.5.far = bf16[2,576,128]{2,1,0:T(8,128)(2,1)S(1)} collective-permute-done((bf16[2,576,128]{2,1,0:T(8,128)(2,1)S(1)}, bf16[2,576,128]{2,1,0:T(8,128)(2,1)S(1)}, u32[]{:S(2)}, u32[]{:S(2)}) %collective-permute-start.5) | collective-permute-done | bytes 294944 | tf_op jit(solution)/shard_map/ppermute | solution.py:43
  26.7 2.4 %collective-permute-start.6 = (bf16[2,576,128]{2,1,0:T(8,128)(2,1)S(1)}, bf16[2,576,128]{2,1,0:T(8,128)(2,1)S(1)}, u32[]{:S(2)}, u32[]{:S(2)}) collective-permute-start(bf16[2,576,128]{2,1,0:T(8,128)(2,1)S(1)} %collective-permute-done.5.far), channel_id=1, source_target_pairs={{0,1},{1,0},{2,3},{3,2},{4,5},{5,4},{6,7},{7,6},{8,9},{9,8},{10,11... | collective-permute-start | bytes 884744 | tf_op jit(solution)/shard_map/ppermute | solution.py:47
  29.1 5.7 %attention_near.1 = (f32[512,128]{1,0:T(8,128)S(1)}, f32[512,128]{1,0:T(8,128)S(1)}, f32[512,512]{1,0:T(8,128)S(1)}, f32[8,128]{1,0:T(8,128)S(1)}) custom-call(s32[33]{0:T(128)S(1)} %concatenate.46.live, bf16[512,576]{1,0:T(8,128)(2,1)S(1)} %bitcast.48, bf16[4,576,128]{2,1,0:T(8,128)(2,1)S(1)} %fusion.26.own, ...), custom_call_target="tpu_custom_call" | custom-call | flops 3000000000 | bytes 6000000 | tf_op jit(solution)/shard_map/attention_near/pallas_call | solution.py:188
  39.8 9.7 %attention_far.1 = (bf16[64,7168]{1,0:T(8,128)(2,1)S(1)}, bf16[64,7168]{1,0:T(8,128)(2,1)}) custom-call(s32[33]{0:T(128)S(1)} %concatenate.46.live, bf16[512,576]{1,0:T(8,128)(2,1)S(1)} %bitcast.49, bf16[4,576,128]{2,1,0:T(8,128)(2,1)S(1)} %collective-permute-done.3.beside, bf16[4,576,128]{2,1,0:T(8,128)(2,1)S(1)} %collective-permute-done.4.beside_other, ...), custom_call_target="tpu_custom_call" | custom-call | flops 4000000000 | bytes 14000000 | tf_op jit(solution)/shard_map/attention_far/pallas_call | solution.py:212
  49.9 2.3 %collective-permute-done.10 = bf16[64,7168]{1,0:T(8,128)(2,1)S(1)} collective-permute-done((bf16[64,7168]{1,0:T(8,128)(2,1)}, bf16[64,7168]{1,0:T(8,128)(2,1)S(1)}, u32[]{:S(2)}, u32[]{:S(2)}) %collective-permute-start.10) | collective-permute-done | bytes 917536 | tf_op jit(solution)/shard_map/ppermute | solution.py:47
  52.5 19.1 %all_to_all.15 = bf16[8,8,7168]{2,1,0:T(8,128)(2,1)S(1)} all-to-all(bf16[8,8,7168]{2,1,0:T(8,128)(2,1)S(1)} %fusion.5), channel_id=1, replica_groups={{0,2,4,6,8,10,12,14},{1,3,5,7,9,11,13,15},{16,18,20,22,24,26,28,30},{17..., dimensions={0} | all-to-all | bytes 1835008 | tf_op jit(solution)/shard_map/all_to_all | solution.py:460
  72.7 12.6 %all_to_all.16 = bf16[16,2,7168]{2,1,0:T(2,128)(2,1)S(1)} all-to-all(bf16[16,2,7168]{2,1,0:T(2,128)(2,1)S(1)} %reshape.183), channel_id=1, replica_groups=mesh['ctx'=8,'exp'=16] {'exp'}, dimensions={0} | all-to-all | bytes 917504 | tf_op jit(solution)/shard_map/all_to_all | solution.py:482
  86.5 6.6 %collective-permute-done.11.refs_1_ = bf16[32,7168]{1,0:T(8,128)(2,1)S(1)} collective-permute-done((bf16[32,7168]{1,0:T(8,128)(2,1)S(1)}, bf16[32,7168]{1,0:T(8,128)(2,1)S(1)}, u32[]{:S(2)}, u32[]{:S(2)}) %collective-permute-start.11) | collective-permute-done | bytes 458784 | tf_op jit(solution)/shard_map/ppermute | solution.py:43
  94.6 3.2 %collective-permute-done.13.refs_3_ = bf16[32,7168]{1,0:T(8,128)(2,1)S(1)} collective-permute-done((bf16[32,7168]{1,0:T(8,128)(2,1)S(1)}, bf16[32,7168]{1,0:T(8,128)(2,1)S(1)}, u32[]{:S(2)}, u32[]{:S(2)}) %collective-permute-start.13) | collective-permute-done | bytes 458784 | tf_op jit(solution)/shard_map/ppermute | solution.py:43
  97.8 2.1 %collective-permute-start.17 = (bf16[32,7168]{1,0:T(8,128)(2,1)S(1)}, bf16[32,7168]{1,0:T(8,128)(2,1)S(1)}, u32[]{:S(2)}, u32[]{:S(2)}) collective-permute-start(bf16[32,7168]{1,0:T(8,128)(2,1)S(1)} %collective-permute-done.13.refs_3_), channel_id=1, source_target_pairs={{0,48},{1,17},{2,50},{3,19},{4,52},{5,21},{6,54},{7,23},{8,56},{9,... | collective-permute-start | bytes 1376264 | tf_op jit(solution)/shard_map/ppermute | solution.py:43
  104.8 6.4 %experts_near.1 = (bf16[32,7168]{1,0:T(8,128)(2,1)S(1)}, bf16[32,7168]{1,0:T(8,128)(2,1)S(1)}, bf16[32,7168]{1,0:T(8,128)(2,1)S(1)}, bf16[32,7168]{1,0:T(8,128)(...) custom-call(bf16[32,7168]{1,0:T(8,128)(2,1)S(1)} %reshape.184.refs_0_, ...), custom_call_target="tpu_custom_call" | custom-call | flops 1500000000 | bytes 15000000 | tf_op jit(solution)/shard_map/experts_near/pallas_call | solution.py:357
  111.2 3.5 %collective-permute-done.17.refs_2_ = bf16[32,7168]{1,0:T(8,128)(2,1)S(1)} collective-permute-done((bf16[32,7168]{1,0:T(8,128)(2,1)S(1)}, bf16[32,7168]{1,0:T(8,128)(2,1)S(1)}, u32[]{:S(2)}, u32[]{:S(2)}) %collective-permute-start.17) | collective-permute-done | bytes 458784 | tf_op jit(solution)/shard_map/ppermute | solution.py:43
  114.7 3.8 %experts_far.1 = (bf16[32,7168]{1,0:T(8,128)(2,1)S(1)}, bf16[32,7168]{1,0:T(8,128)(2,1)S(1)}, bf16[32,7168]{1,0:T(8,128)(2,1)S(1)}, bf16[32,7168]{1,0:T(8,128)(2,1)S(1)}) custom-call(bf16[32,7168]{1,0:T(8,128)(2,1)S(1)} %collective-permute-done.15.refs_0_, bf16[32,7168]{1,0:T(8,128)(2,1)S(1)} %collective-permute-done.16.refs_1_, ...), custom_call_target="tpu_custom_call" | custom-call | flops 1500000000 | bytes 15000000 | tf_op jit(solution)/shard_map/experts_far/pallas_call | solution.py:357
  118.5 4.1 %collective-permute-start.22 = (bf16[32,7168]{1,0:T(8,128)(2,1)S(1)}, bf16[32,7168]{1,0:T(8,128)(2,1)S(1)}, u32[]{:S(2)}, u32[]{:S(2)}) collective-permute-start(bf16[32,7168]{1,0:T(8,128)(2,1)S(1)} %get-tuple-element.55), channel_id=1, source_target_pairs={{0,64},{1,65},{2,66},{3,67},{4,68},{5,69},{6,70},{7,71},{8,72},{9,... | collective-permute-start | bytes 1376264 | tf_op jit(solution)/shard_map/ppermute | solution.py:43
  125.3 4.9 %collective-permute-done.22 = bf16[32,7168]{1,0:T(8,128)(2,1)S(1)} collective-permute-done((bf16[32,7168]{1,0:T(8,128)(2,1)S(1)}, bf16[32,7168]{1,0:T(8,128)(2,1)S(1)}, u32[]{:S(2)}, u32[]{:S(2)}) %collective-permute-start.22) | collective-permute-done | bytes 458784 | tf_op jit(solution)/shard_map/ppermute | solution.py:43
  130.3 2.9 %collective-permute-done.19 = bf16[32,7168]{1,0:T(8,128)(2,1)S(1)} collective-permute-done((bf16[32,7168]{1,0:T(8,128)(2,1)S(1)}, bf16[32,7168]{1,0:T(8,128)(2,1)S(1)}, u32[]{:S(2)}, u32[]{:S(2)}) %collective-permute-start.19) | collective-permute-done | bytes 458784 | tf_op jit(solution)/shard_map/ppermute | solution.py:43
  133.2 8.4 %collective-permute-done.20 = bf16[32,7168]{1,0:T(8,128)(2,1)S(1)} collective-permute-done((bf16[32,7168]{1,0:T(8,128)(2,1)S(1)}, bf16[32,7168]{1,0:T(8,128)(2,1)S(1)}, u32[]{:S(2)}, u32[]{:S(2)}) %collective-permute-start.20) | collective-permute-done | bytes 458784 | tf_op jit(solution)/shard_map/ppermute | solution.py:43
  141.8 2.3 %collective-permute-done.23 = bf16[32,7168]{1,0:T(8,128)(2,1)S(1)} collective-permute-done((bf16[32,7168]{1,0:T(8,128)(2,1)S(1)}, bf16[32,7168]{1,0:T(8,128)(2,1)S(1)}, u32[]{:S(2)}, u32[]{:S(2)}) %collective-permute-start.23) | collective-permute-done | bytes 458784 | tf_op jit(solution)/shard_map/ppermute | solution.py:43
  145.7 5.0 %collective-permute-done.21 = bf16[32,7168]{1,0:T(8,128)(2,1)S(1)} collective-permute-done((bf16[32,7168]{1,0:T(8,128)(2,1)S(1)}, bf16[32,7168]{1,0:T(8,128)(2,1)S(1)}, u32[]{:S(2)}, u32[]{:S(2)}) %collective-permute-start.21) | collective-permute-done | bytes 458784 | tf_op jit(solution)/shard_map/ppermute | solution.py:43
  150.7 2.5 %collective-permute-done.24 = bf16[32,7168]{1,0:T(8,128)(2,1)S(1)} collective-permute-done((bf16[32,7168]{1,0:T(8,128)(2,1)S(1)}, bf16[32,7168]{1,0:T(8,128)(2,1)S(1)}, u32[]{:S(2)}, u32[]{:S(2)}) %collective-permute-start.24) | collective-permute-done | bytes 458784 | tf_op jit(solution)/shard_map/ppermute | solution.py:43
  153.6 16.0 %all_to_all.17 = bf16[16,2,7168]{2,1,0:T(2,128)(2,1)S(1)} all-to-all(bf16[16,2,7168]{2,1,0:T(2,128)(2,1)S(1)} %reshape.185), channel_id=1, replica_groups=mesh['ctx'=8,'exp'=16] {'exp'}, dimensions={0} | all-to-all | bytes 917504 | tf_op jit(solution)/shard_map/all_to_all | solution.py:497
  (123 shorter events, 33.1 us)
Async XLA Ops:
  2.8 13.0 %collective-permute-start = (bf16[2,576,128]{2,1,0:T(8,128)(2,1)S(1)}, bf16[2,576,128]{2,1,0:T(8,128)(2,1)S(1)}, u32[]{:S(2)}, u32[]{:S(2)}) collective-permute-start(bf16[2,576,128]{2,1,0:T(8,128)(2,1)S(1)} %dynamic-slice_bitcast_fusion), channel_id=1, source_target_pairs={{0,64},{1,65},{2,66},{3,67},{4,68},{5,69},{6,70},{7,71},{8,72},{9,... | collective-permute-start | bytes 884744 | tf_op jit(solution)/shard_map/ppermute | solution.py:43
  6.8 10.7 %collective-permute-start.2 = (bf16[4,576,128]{2,1,0:T(8,128)(2,1)S(1)}, bf16[4,576,128]{2,1,0:T(8,128)(2,1)S(1)}, u32[]{:S(2)}, u32[]{:S(2)}) collective-permute-start(bf16[4,576,128]{2,1,0:T(8,128)(2,1)S(1)} %fusion.26.own), channel_id=1, source_target_pairs={{0,16},{1,49},{2,18},{3,51},{4,20},{5,53},{6,22},{7,55},{8,24},{9,... | collective-permute-start | bytes 1769480 | tf_op jit(solution)/shard_map/ppermute | solution.py:43
  15.8 5.8 %collective-permute-start.1 = (bf16[2,576,128]{2,1,0:T(8,128)(2,1)S(1)}, bf16[2,576,128]{2,1,0:T(8,128)(2,1)S(1)}, u32[]{:S(2)}, u32[]{:S(2)}) collective-permute-start(bf16[2,576,128]{2,1,0:T(8,128)(2,1)S(1)} %collective-permute-done.side), channel_id=1, source_target_pairs={{0,1},{1,0},{2,3},{3,2},{4,5},{5,4},{6,7},{7,6},{8,9},{9,8},{10,11... | collective-permute-start | bytes 884744 | tf_op jit(solution)/shard_map/ppermute | solution.py:47
  17.5 11.6 %collective-permute-start.8 = (bf16[4,576,128]{2,1,0:T(8,128)(2,1)S(1)}, bf16[4,576,128]{2,1,0:T(8,128)(2,1)}, u32[]{:S(2)}, u32[]{:S(2)}) collective-permute-start(bf16[4,576,128]{2,1,0:T(8,128)(2,1)S(1)} %collective-permute-done.2.beside), channel_id=1, source_target_pairs={{0,1},{1,0},{2,3},{3,2},{4,5},{5,4},{6,7},{7,6},{8,9},{9,8},{10,11... | collective-permute-start | bytes 1769480 | tf_op jit(solution)/shard_map/ppermute | solution.py:47
  19.8 5.9 %collective-permute-start.5 = (bf16[2,576,128]{2,1,0:T(8,128)(2,1)S(1)}, bf16[2,576,128]{2,1,0:T(8,128)(2,1)S(1)}, u32[]{:S(2)}, u32[]{:S(2)}) collective-permute-start(bf16[2,576,128]{2,1,0:T(8,128)(2,1)S(1)} %constant_dynamic-slice_fusion), channel_id=1, source_target_pairs={{0,16},{1,49},{2,18},{3,51},{4,20},{5,53},{6,22},{7,55},{8,24},{9,... | collective-permute-start | bytes 884744 | tf_op jit(solution)/shard_map/ppermute | solution.py:43
  22.5 13.9 %collective-permute-start.3 = (bf16[4,576,128]{2,1,0:T(8,128)(2,1)}, bf16[4,576,128]{2,1,0:T(8,128)(2,1)S(1)}, u32[]{:S(2)}, u32[]{:S(2)}) collective-permute-start(bf16[4,576,128]{2,1,0:T(8,128)(2,1)} %pad_maximum_fusion), channel_id=1, source_target_pairs={{0,16},{1,49},{2,18},{3,51},{4,20},{5,53},{6,22},{7,55},{8,24},{9,... | collective-permute-start | bytes 1769480 | tf_op jit(solution)/shard_map/ppermute | solution.py:43
  25.7 10.7 %collective-permute-start.7 = (bf16[2,576,128]{2,1,0:T(8,128)(2,1)S(1)}, bf16[2,576,128]{2,1,0:T(8,128)(2,1)}, u32[]{:S(2)}, u32[]{:S(2)}) collective-permute-start(bf16[2,576,128]{2,1,0:T(8,128)(2,1)S(1)} %collective-permute-done.5.far), channel_id=1, source_target_pairs={{0,64},{1,65},{2,66},{3,67},{4,68},{5,69},{6,70},{7,71},{8,72},{9,... | collective-permute-start | bytes 884744 | tf_op jit(solution)/shard_map/ppermute | solution.py:43
  26.7 11.9 %collective-permute-start.6 = (bf16[2,576,128]{2,1,0:T(8,128)(2,1)S(1)}, bf16[2,576,128]{2,1,0:T(8,128)(2,1)S(1)}, u32[]{:S(2)}, u32[]{:S(2)}) collective-permute-start(bf16[2,576,128]{2,1,0:T(8,128)(2,1)S(1)} %collective-permute-done.5.far), channel_id=1, source_target_pairs={{0,1},{1,0},{2,3},{3,2},{4,5},{5,4},{6,7},{7,6},{8,9},{9,8},{10,11... | collective-permute-start | bytes 884744 | tf_op jit(solution)/shard_map/ppermute | solution.py:47
  36.3 3.4 %collective-permute-start.4 = (bf16[4,576,128]{2,1,0:T(8,128)(2,1)S(1)}, bf16[4,576,128]{2,1,0:T(8,128)(2,1)S(1)}, u32[]{:S(2)}, u32[]{:S(2)}) collective-permute-start(bf16[4,576,128]{2,1,0:T(8,128)(2,1)S(1)} %collective-permute-done.3.beside), channel_id=1, source_target_pairs={{0,1},{1,0},{2,3},{3,2},{4,5},{5,4},{6,7},{7,6},{8,9},{9,8},{10,11... | collective-permute-start | bytes 1769480 | tf_op jit(solution)/shard_map/ppermute | solution.py:47
  49.5 2.8 %collective-permute-start.10 = (bf16[64,7168]{1,0:T(8,128)(2,1)}, bf16[64,7168]{1,0:T(8,128)(2,1)S(1)}, u32[]{:S(2)}, u32[]{:S(2)}) collective-permute-start(bf16[64,7168]{1,0:T(8,128)(2,1)} %get-tuple-element.42), channel_id=1, source_target_pairs={{0,1},{1,0},{2,3},{3,2},{4,5},{5,4},{6,7},{7,6},{8,9},{9,8},{10,11... | collective-permute-start | bytes 2752520 | tf_op jit(solution)/shard_map/ppermute | solution.py:47
  85.5 7.7 %collective-permute-start.11 = (bf16[32,7168]{1,0:T(8,128)(2,1)S(1)}, bf16[32,7168]{1,0:T(8,128)(2,1)S(1)}, u32[]{:S(2)}, u32[]{:S(2)}) collective-permute-start(bf16[32,7168]{1,0:T(8,128)(2,1)S(1)} %reshape.184.refs_0_), channel_id=1, source_target_pairs={{0,16},{1,49},{2,18},{3,51},{4,20},{5,53},{6,22},{7,55},{8,24},{9,... | collective-permute-start | bytes 1376264 | tf_op jit(solution)/shard_map/ppermute | solution.py:43
  85.5 12.3 %collective-permute-start.13 = (bf16[32,7168]{1,0:T(8,128)(2,1)S(1)}, bf16[32,7168]{1,0:T(8,128)(2,1)S(1)}, u32[]{:S(2)}, u32[]{:S(2)}) collective-permute-start(bf16[32,7168]{1,0:T(8,128)(2,1)S(1)} %reshape.184.refs_0_), channel_id=1, source_target_pairs={{0,64},{1,65},{2,66},{3,67},{4,68},{5,69},{6,70},{7,71},{8,72},{9,... | collective-permute-start | bytes 1376264 | tf_op jit(solution)/shard_map/ppermute | solution.py:43
  93.2 8.6 %collective-permute-start.15 = (bf16[32,7168]{1,0:T(8,128)(2,1)S(1)}, bf16[32,7168]{1,0:T(8,128)(2,1)S(1)}, u32[]{:S(2)}, u32[]{:S(2)}) collective-permute-start(bf16[32,7168]{1,0:T(8,128)(2,1)S(1)} %collective-permute-done.11.refs_1_), channel_id=1, source_target_pairs={{0,16},{1,49},{2,18},{3,51},{4,20},{5,53},{6,22},{7,55},{8,24},{9,... | collective-permute-start | bytes 1376264 | tf_op jit(solution)/shard_map/ppermute | solution.py:43
  94.1 10.8 %collective-permute-start.12 = (bf16[32,7168]{1,0:T(8,128)(2,1)S(1)}, bf16[32,7168]{1,0:T(8,128)(2,1)S(1)}, u32[]{:S(2)}, u32[]{:S(2)}) collective-permute-start(bf16[32,7168]{1,0:T(8,128)(2,1)S(1)} %reshape.184.refs_0_), channel_id=1, source_target_pairs={{0,48},{1,17},{2,50},{3,19},{4,52},{5,21},{6,54},{7,23},{8,56},{9,... | collective-permute-start | bytes 1376264 | tf_op jit(solution)/shard_map/ppermute | solution.py:43
  97.8 16.8 %collective-permute-start.17 = (bf16[32,7168]{1,0:T(8,128)(2,1)S(1)}, bf16[32,7168]{1,0:T(8,128)(2,1)S(1)}, u32[]{:S(2)}, u32[]{:S(2)}) collective-permute-start(bf16[32,7168]{1,0:T(8,128)(2,1)S(1)} %collective-permute-done.13.refs_3_), channel_id=1, source_target_pairs={{0,48},{1,17},{2,50},{3,19},{4,52},{5,21},{6,54},{7,23},{8,56},{9,... | collective-permute-start | bytes 1376264 | tf_op jit(solution)/shard_map/ppermute | solution.py:43
  100.0 14.7 %collective-permute-start.16 = (bf16[32,7168]{1,0:T(8,128)(2,1)S(1)}, bf16[32,7168]{1,0:T(8,128)(2,1)S(1)}, u32[]{:S(2)}, u32[]{:S(2)}) collective-permute-start(bf16[32,7168]{1,0:T(8,128)(2,1)S(1)} %collective-permute-done.13.refs_3_), channel_id=1, source_target_pairs={{0,16},{1,49},{2,18},{3,51},{4,20},{5,53},{6,22},{7,55},{8,24},{9,... | collective-permute-start | bytes 1376264 | tf_op jit(solution)/shard_map/ppermute | solution.py:43
  101.8 12.9 %collective-permute-start.18 = (bf16[32,7168]{1,0:T(8,128)(2,1)S(1)}, bf16[32,7168]{1,0:T(8,128)(2,1)S(1)}, u32[]{:S(2)}, u32[]{:S(2)}) collective-permute-start(bf16[32,7168]{1,0:T(8,128)(2,1)S(1)} %collective-permute-done.15.refs_0_), channel_id=1, source_target_pairs={{0,64},{1,65},{2,66},{3,67},{4,68},{5,69},{6,70},{7,71},{8,72},{9,... | collective-permute-start | bytes 1376264 | tf_op jit(solution)/shard_map/ppermute | solution.py:43
  118.5 11.6 %collective-permute-start.22 = (bf16[32,7168]{1,0:T(8,128)(2,1)S(1)}, bf16[32,7168]{1,0:T(8,128)(2,1)S(1)}, u32[]{:S(2)}, u32[]{:S(2)}) collective-permute-start(bf16[32,7168]{1,0:T(8,128)(2,1)S(1)} %get-tuple-element.55), channel_id=1, source_target_pairs={{0,64},{1,65},{2,66},{3,67},{4,68},{5,69},{6,70},{7,71},{8,72},{9,... | collective-permute-start | bytes 1376264 | tf_op jit(solution)/shard_map/ppermute | solution.py:43
  122.6 23.1 %collective-permute-start.14 = (bf16[32,7168]{1,0:T(8,128)(2,1)S(1)}, bf16[32,7168]{1,0:T(8,128)(2,1)S(1)}, u32[]{:S(2)}, u32[]{:S(2)}) collective-permute-start(bf16[32,7168]{1,0:T(8,128)(2,1)S(1)} %get-tuple-element.45), channel_id=1, source_target_pairs={{0,16},{1,49},{2,18},{3,51},{4,20},{5,53},{6,22},{7,55},{8,24},{9,... | collective-permute-start | bytes 1376264 | tf_op jit(solution)/shard_map/ppermute | solution.py:43
  122.6 10.6 %collective-permute-start.19 = (bf16[32,7168]{1,0:T(8,128)(2,1)S(1)}, bf16[32,7168]{1,0:T(8,128)(2,1)S(1)}, u32[]{:S(2)}, u32[]{:S(2)}) collective-permute-start(bf16[32,7168]{1,0:T(8,128)(2,1)S(1)} %get-tuple-element.51), channel_id=1, source_target_pairs={{0,48},{1,17},{2,50},{3,19},{4,52},{5,21},{6,54},{7,23},{8,56},{9,... | collective-permute-start | bytes 1376264 | tf_op jit(solution)/shard_map/ppermute | solution.py:43
  124.1 17.5 %collective-permute-start.20 = (bf16[32,7168]{1,0:T(8,128)(2,1)S(1)}, bf16[32,7168]{1,0:T(8,128)(2,1)S(1)}, u32[]{:S(2)}, u32[]{:S(2)}) collective-permute-start(bf16[32,7168]{1,0:T(8,128)(2,1)S(1)} %get-tuple-element.52), channel_id=1, source_target_pairs={{0,16},{1,49},{2,18},{3,51},{4,20},{5,53},{6,22},{7,55},{8,24},{9,... | collective-permute-start | bytes 1376264 | tf_op jit(solution)/shard_map/ppermute | solution.py:43
  130.3 13.9 %collective-permute-start.23 = (bf16[32,7168]{1,0:T(8,128)(2,1)S(1)}, bf16[32,7168]{1,0:T(8,128)(2,1)S(1)}, u32[]{:S(2)}, u32[]{:S(2)}) collective-permute-start(bf16[32,7168]{1,0:T(8,128)(2,1)S(1)} %add_convert_fusion.3), channel_id=1, source_target_pairs={{0,48},{1,17},{2,50},{3,19},{4,52},{5,21},{6,54},{7,23},{8,56},{9,... | collective-permute-start | bytes 1376264 | tf_op jit(solution)/shard_map/ppermute | solution.py:43
  141.7 8.9 %collective-permute-start.21 = (bf16[32,7168]{1,0:T(8,128)(2,1)S(1)}, bf16[32,7168]{1,0:T(8,128)(2,1)S(1)}, u32[]{:S(2)}, u32[]{:S(2)}) collective-permute-start(bf16[32,7168]{1,0:T(8,128)(2,1)S(1)} %add_convert_fusion.4), channel_id=1, source_target_pairs={{0,64},{1,65},{2,66},{3,67},{4,68},{5,69},{6,70},{7,71},{8,72},{9,... | collective-permute-start | bytes 1376264 | tf_op jit(solution)/shard_map/ppermute | solution.py:43
  144.2 8.9 %collective-permute-start.24 = (bf16[32,7168]{1,0:T(8,128)(2,1)S(1)}, bf16[32,7168]{1,0:T(8,128)(2,1)S(1)}, u32[]{:S(2)}, u32[]{:S(2)}) collective-permute-start(bf16[32,7168]{1,0:T(8,128)(2,1)S(1)} %add_convert_fusion.2), channel_id=1, source_target_pairs={{0,48},{1,17},{2,50},{3,19},{4,52},{5,21},{6,54},{7,23},{8,56},{9,... | collective-permute-start | bytes 1376264 | tf_op jit(solution)/shard_map/ppermute | solution.py:43
  (12 other events, 234.2 us)

commit v3 on v2

--- a/solution.py
+++ b/solution.py
@@ -11,7 +11,7 @@
 NOPE = 128
 Y_HI, Z, Y_LO, X, CORES = 2, 4, 2, 4, 2
 STEP_BLOCKS = 4
-VMEM_LIMIT = 40 * 2**20
+VMEM_LIMIT = 36 * 2**20
 HEADS_HERE = 4
 F32 = jnp.float32
 BF16 = jnp.bfloat16
@@ -51,7 +51,11 @@
     return jnp.where(powers < 0, 0.5, jnp.where(powers > 0, 2.0, 1.0)).astype(jnp.float32)
 
 
-def attend(live, first_flag, queries, steps, diagonal, scores, top, total, mixture):
+def in_hbm(value):
+    return pltpu.with_memory_space_constraint(value, pltpu.HBM)
+
+
+def attend(mask, queries, steps, diagonal, scores, top, total, mixture):
     rows = queries.shape[0]
     latent_width = mixture.shape[1]
     block = top.shape[1]
@@ -61,7 +65,7 @@
     mixture[...] = jnp.zeros_like(mixture)
 
     def keys_of(step, height):
-        return jnp.concatenate([part[i, :height] for part, i in step], axis=1)
+        return jnp.concatenate([part[i, :height] for part, i, _ in step], axis=1)
 
     def lane_fold(value, fold):
         folded = value[:, :block]
@@ -69,8 +73,20 @@
             folded = fold(folded, value[:, i * block : (i + 1) * block])
         return folded
 
+    ctx_index = lax.axis_index("ctx")
+    core = lax.axis_index("exp") % CORES
+    owners = mask.shape[0]
+    prior_blocks = mask.shape[1] // owners - 1
+
+    def flag(place):
+        dy, dz, number = place
+        owner = (ctx_index // Z + dy) % Y_HI * Z + (ctx_index % Z + dz + Z) % Z
+        prior = owner * prior_blocks + jnp.minimum(number, prior_blocks - 1)
+        fresh = owners * prior_blocks + owner
+        return mask[ctx_index, jnp.where(number < prior_blocks, prior, fresh)]
+
     def flags_of(number):
-        return [live[first_flag + STEP_BLOCKS * number + i] for i in range(STEP_BLOCKS)]
+        return [flag(place) for _, _, place in steps[number]]
 
     def score(step, number):
         flags = flags_of(number)
@@ -97,7 +113,7 @@
         row = lax.broadcasted_iota(jnp.int32, (rows, 1), 0) % tokens
         relative = row // (tokens // 2)
         within = row % (tokens // 2)
-        side = jnp.where(relative == 0, live[live.shape[0] - 1], 1 - live[live.shape[0] - 1])
+        side = jnp.where(relative == 0, core, 1 - core)
         token = within // 8 * 16 + side * 8 + within % 8
         return lax.broadcasted_iota(jnp.int32, (1, block), 1) <= token
 
@@ -122,32 +138,64 @@
     return row_top
 
 
+def whole(part, dy, dz):
+    return [(part, i, (dy, dz, i)) for i in range(STEP_BLOCKS)]
+
+
+def halves(part, other, dy, dz, first):
+    half = STEP_BLOCKS // 2
+    return [
+        (array, i, (dy, dz, start + i))
+        for array, start in ((part, first), (other, half - first))
+        for i in range(half)
+    ]
+
+
 def near_kernel(
-    live, queries, own, beside, beside_other, side, side_other, top, total, mixture, done, scores
-):
-    steps = [[(part, i) for i in range(STEP_BLOCKS)] for part in (own, beside, beside_other)]
-    steps.append([(part, i) for part in (side, side_other) for i in range(STEP_BLOCKS // 2)])
-    row_top = attend(live, 0, queries, steps, True, scores, top, total, mixture)
-    top[...] = jnp.broadcast_to(row_top, top.shape)
-    done[...] = jnp.ones_like(done)
-
-
-def far_kernel(
-    live, queries, beside, beside_other, far, far_other, side_far, side_far_other,
-    near_top, near_total, near_mixture, value_up, weight_hbm,
-    out_keep, out_send, scores, top, total, mixture, weight, weight_sem,
+    mask, queries, own, beside, beside_other, side, side_other, weight_hbm,
+    top, total, mixture, weight, done, scores, weight_sem,
 ):
     copy = pltpu.make_async_copy(weight_hbm, weight, weight_sem)
     copy.start()
+    core = lax.axis_index("exp") % CORES
+    way = 1 - 2 * core
+    first = core * (STEP_BLOCKS // 2)
+    steps = [
+        whole(own, 0, 0),
+        whole(beside, 0, -way),
+        whole(beside_other, 0, way),
+        halves(side, side_other, 1, 0, first),
+    ]
+    row_top = attend(mask, queries, steps, True, scores, top, total, mixture)
+    top[...] = jnp.broadcast_to(row_top, top.shape)
+    done[...] = jnp.ones_like(done)
+    copy.wait()
+
+
+def far_kernel(
+    mask, queries, beside, beside_other, far, far_other, side_far, side_far_other,
+    near_top, near_total, near_mixture, weight, value_up,
+    out_keep, out_send, scores, top, total, mixture,
+):
     heads = value_up.shape[0]
     tokens = queries.shape[0] // heads
     factor = 1.4426950408889634 / (NOPE + ROPE) ** 0.5
-    steps = [[(part, i) for i in range(STEP_BLOCKS)] for part in (beside, beside_other)]
-    for halves in ((far, far_other), (side_far, side_far_other)):
-        steps.append([(part, i) for part in halves for i in range(STEP_BLOCKS // 2)])
-    far_top = attend(
-        live, 4 * STEP_BLOCKS, queries, steps, False, scores, top, total, mixture
-    )
+    core = lax.axis_index("exp") % CORES
+    way = 1 - 2 * core
+    half = STEP_BLOCKS // 2
+    first = core * half
+
+    def sent(part, dz, first):
+        low = [(part, i, (1, dz, first + i)) for i in range(half)]
+        return low + [(part, half + i, (1, dz, half - first + i)) for i in range(half)]
+
+    steps = [
+        sent(beside, -way, first),
+        sent(beside_other, way, half - first),
+        halves(far, far_other, 0, 2, first),
+        halves(side_far, side_far_other, 1, 2, first),
+    ]
+    far_top = attend(mask, queries, steps, False, scores, top, total, mixture)
     near_row_top = near_top[:, :1]
     both_top = jnp.maximum(near_row_top, far_top)
     near_scale = jnp.exp2((near_row_top - both_top) * factor)
@@ -165,13 +213,11 @@
             ).astype(BF16)
         )
     flat_heads = jnp.concatenate(per_head, axis=1)
-    copy.wait()
     out_width = 1024
     half = tokens // 2
 
-    @pl.loop(0, weight.shape[1] // out_width)
-    def _(step):
-        columns = pl.ds(pl.multiple_of(step * out_width, out_width), out_width)
+    for step in range(weight.shape[1] // out_width):
+        columns = slice(step * out_width, (step + 1) * out_width)
         term = jnp.dot(flat_heads, weight[:, columns], preferred_element_type=F32)
         out_keep[:, columns] = term[:half].astype(BF16)
         out_send[:, columns] = term[half:].astype(BF16)
@@ -181,7 +227,7 @@
     return pltpu.VMEM((blocks // STEP_BLOCKS, rows, STEP_BLOCKS * block), F32)
 
 
-def near_call(live, queries, near, value_up):
+def near_call(mask, queries, near, value_up, output_weight):
     rows, block = queries.shape[0], near[0].shape[2]
     vmem = pl.BlockSpec(memory_space=pltpu.VMEM)
     lanes = jax.ShapeDtypeStruct((rows, block), F32)
@@ -191,45 +237,48 @@
             lanes,
             lanes,
             jax.ShapeDtypeStruct((rows, value_up.shape[1]), F32),
+            pltpu.VMEM(output_weight.shape, BF16),
             jax.ShapeDtypeStruct((8, block), F32),
         ),
-        in_specs=[pl.BlockSpec(memory_space=pltpu.SMEM)] + [vmem] * (1 + len(near)),
-        out_specs=(vmem,) * 4,
-        scratch_shapes=[score_scratch(sum(part.shape[0] for part in near), rows, block)],
-        compiler_params=pltpu.CompilerParams(vmem_limit_bytes=VMEM_LIMIT),
+        in_specs=[pl.BlockSpec(memory_space=pltpu.SMEM)]
+        + [vmem] * (1 + len(near))
+        + [pl.BlockSpec(memory_space=pltpu.HBM)],
+        out_specs=(vmem,) * 5,
+        scratch_shapes=[
+            score_scratch(sum(part.shape[0] for part in near), rows, block),
+            pltpu.SemaphoreType.DMA,
+        ],
+        compiler_params=pltpu.CompilerParams(vmem_limit_bytes=32 * 2**20),
         cost_estimate=pl.CostEstimate(
-            flops=3 * 10**9, bytes_accessed=6 * 10**6, transcendentals=10**6
+            flops=3 * 10**9, bytes_accessed=12 * 10**6, transcendentals=10**6
         ),
         name="attention_near",
-    )(live, queries, *near)
-
-
-def far_call(live, queries, far, state, value_up, output_weight):
+    )(mask, queries, *near, in_hbm(output_weight))
+
+
+def far_call(mask, queries, far, state, value_up):
     rows, block = queries.shape[0], far[0].shape[2]
     tokens = rows // value_up.shape[0]
     vmem = pl.BlockSpec(memory_space=pltpu.VMEM)
-    out = jax.ShapeDtypeStruct((tokens // 2, output_weight.shape[1]), BF16)
+    out = jax.ShapeDtypeStruct((tokens // 2, state[3].shape[1]), BF16)
     return pl.pallas_call(
         far_kernel,
         out_shape=(out, out),
         in_specs=[pl.BlockSpec(memory_space=pltpu.SMEM)]
-        + [vmem] * 11
-        + [pl.BlockSpec(memory_space=pltpu.HBM)],
+        + [vmem] * (2 + len(far) + len(state)),
         out_specs=(vmem, vmem),
         scratch_shapes=[
             score_scratch(sum(part.shape[0] for part in far), rows, block),
             pltpu.VMEM((rows, block), F32),
             pltpu.VMEM((rows, block), F32),
             pltpu.VMEM((rows, value_up.shape[1]), F32),
-            pltpu.VMEM(output_weight.shape, BF16),
-            pltpu.SemaphoreType.DMA,
         ],
-        compiler_params=pltpu.CompilerParams(vmem_limit_bytes=49 * 2**20),
+        compiler_params=pltpu.CompilerParams(vmem_limit_bytes=32 * 2**20),
         cost_estimate=pl.CostEstimate(
             flops=4 * 10**9, bytes_accessed=14 * 10**6, transcendentals=10**6
         ),
         name="attention_far",
-    )(live, queries, *far, *state, value_up, output_weight)
+    )(mask, queries, *far, *state, value_up)
 
 
 def own_half(blocks, core):
@@ -237,9 +286,17 @@
     return lax.dynamic_slice_in_dim(blocks, core * half_blocks, half_blocks, 0)
 
 
+def after(value, event):
+    one = event[(0,) * event.ndim].astype(F32) * 0.0 + 1.0
+    tile = value[(slice(0, 1),) * (value.ndim - 2) + (slice(0, 16), slice(0, 128))]
+    tile = (tile.astype(F32) * one).astype(value.dtype)
+    return lax.dynamic_update_slice(value, tile, (0,) * value.ndim)
+
+
 def gather_codes(blocks, core):
+    blocks = lax.optimization_barrier(blocks)
+    beside = over_ctx(blocks, AHEAD)
     side = over_ctx(own_half(blocks, core), ACROSS)
-    beside = over_ctx(blocks, AHEAD)
     beside_half = own_half(beside, core)
     far = over_ctx(beside_half, AHEAD)
     side_other, _ = lax.optimization_barrier((core_swap(side), beside_half))
@@ -248,41 +305,11 @@
     near = (blocks, beside, core_swap(beside), side, side_other)
 
     def far_blocks(done):
-        held = side_far * done[0, 0].astype(BF16)
+        held = after(side_far, done)
         swapped = [core_swap(part) for part in (side_beside, far, held)]
         return (side_beside, swapped[0], far, swapped[1], held, swapped[2])
 
     return near, far_blocks
-
-
-def block_flags(block_mask, ctx_index, core, prior_blocks):
-    owners = block_mask.shape[0]
-    mask_row = lax.dynamic_index_in_dim(block_mask, ctx_index, 0, keepdims=False)
-    prior = mask_row[: owners * prior_blocks].reshape(owners, prior_blocks)
-    fresh = mask_row[owners * prior_blocks :].reshape(owners, 1)
-    flags = jnp.concatenate([prior, fresh], axis=1)
-    half = flags.shape[1] // 2
-    y, z = ctx_index // Z, ctx_index % Z
-    way = 1 - 2 * core
-
-    def of(dy, dz):
-        owner = (y + dy) % Y_HI * Z + (z + dz) % Z
-        return jnp.sum(jnp.where(jnp.arange(owners)[:, None] == owner, flags, 0), axis=0)
-
-    def mine_first(found):
-        return jnp.where(core == 0, found, jnp.roll(found, half))
-
-    ordered = (
-        of(0, 0),
-        of(0, -way),
-        of(0, way),
-        mine_first(of(1, 0)),
-        mine_first(of(1, -way)),
-        jnp.roll(mine_first(of(1, way)), half),
-        mine_first(of(0, 2)),
-        mine_first(of(1, 2)),
-    )
-    return jnp.concatenate(ordered + (core[None],)).astype(jnp.int32)
 
 
 def store_rows(results, columns, term):
@@ -352,7 +379,8 @@
     out_shape = [jax.ShapeDtypeStruct(block.shape, BF16) for block in blocks]
     scratch = [pltpu.VMEM((row_count, blocks[0].shape[1]), BF16)]
     if holds:
-        out_shape += [jax.ShapeDtypeStruct(weight.shape[1:], BF16) for weight in weights]
+        out_shape += [pltpu.VMEM(weight.shape[1:], BF16) for weight in weights]
+        weights = [in_hbm(weight) for weight in weights]
         scratch.append(pltpu.SemaphoreType.DMA((3, 4)))
     found = pl.pallas_call(
         functools.partial(experts_kernel, len(blocks), holds),
@@ -418,7 +446,6 @@
     up_weight,
     down_weight,
 ):
-    ctx_index = lax.axis_index("ctx")
     core = lax.axis_index("exp") % CORES
     rows_block, head_count, key_width = queries.shape
     prior_blocks = prior_powers.shape[0]
@@ -429,7 +456,6 @@
     blocks_here = jnp.transpose(blocks_here, (1, 0, 2)).astype(F32)
     blocks_here = (blocks_here * scales[:, None, None]).astype(BF16)
     near, far_blocks = gather_codes(blocks_here, core)
-    live = block_flags(block_mask, ctx_index, core, prior_blocks)
     groups = rows_block // 16
     split = queries.reshape(groups, 2, 8, head_count, key_width)
     first = jnp.where(core == 0, split[:, 0], split[:, 1])
@@ -437,10 +463,10 @@
     ordered = jnp.stack([first, second], axis=0)
     ordered = jnp.transpose(ordered, (3, 0, 1, 2, 4)).reshape(head_count * rows_block, key_width)
 
-    state = near_call(live, ordered, near, value_up)
+    state = near_call(block_mask, ordered, near, value_up, output_weight)
     *state, done = state
     far = far_blocks(done)
-    keep, send = far_call(live, ordered, far, state, value_up, output_weight)
+    keep, send = far_call(block_mask, ordered, far, state, value_up)
     expert_count = router.shape[1]
     token_count, route_count = route_ids.shape
     capacity = token_count * route_count * 2 // expert_count

time: 171 us -> 162 us (0.947)
  Pallas kernels: 25.6 us -> 14.5 us
  starting transfers between devices: 29.4 us -> 37.1 us
  other arithmetic: 10.3 us -> 4.76 us
  waiting for transfers between devices: 50.2 us -> 54.7 us
  local copies, waits for them, and re-layouts: 5.7 us -> 2.01 us
    ppermute x19, starting transfers between devices: 23.7 us -> 33.2 us  [over_ctx(): return lax.ppermute(value, ('ctx', 'exp'), pairs)]
    pallas_call x1, Pallas kernels: 9.71 us -> 4.08 us  [far_call(): pl.pallas_call(far_kernel, out_shape=(out, out), in_specs=[pl.BlockSpec(m...]
    ppermute x19, waiting for transfers between devices: 46.7 us -> 50.6 us  [over_ctx(): return lax.ppermute(value, ('ctx', 'exp'), pairs)]
    pallas_call x2, Pallas kernels: 10.2 us -> 6.69 us  [experts_call(): pl.pallas_call(functools.partial(experts_kernel, len(blocks), holds), out...]
    pallas_call x1, Pallas kernels: 5.7 us -> 3.7 us  [near_call(): pl.pallas_call(near_kernel, out_shape=(lanes, lanes, jax.ShapeDtypeStruct...]
    ppermute x6, starting transfers between devices: 5.78 us -> 3.88 us  [core_swap(): return lax.ppermute(value, 'exp', CORE_SWAP)]
  transfers between devices with their start and end apart: 25 -> 25, of which waited for: 15 -> 14; matrix products, arithmetic and copies ran while one was open for 6% -> 2% of each run, Pallas kernels for 7% -> 5%
where the time goes in v3:
time: 162 us
  waiting for transfers between devices  54.7 us (34%)
  blocking collectives  46.6 us (29%)
  starting transfers between devices  37.1 us (23%)
  Pallas kernels  14.5 us (9%)
  other arithmetic  4.76 us (3%)
  local copies, waits for them, and re-layouts  2.01 us (1%)
  between operations  1.66 us (1%)
    ppermute x19, waiting for transfers between devices, over_ctx(): return lax.ppermute(value, ('ctx', 'exp'), pairs)  50.6 us
    ppermute x19, starting transfers between devices, over_ctx(): return lax.ppermute(value, ('ctx', 'exp'), pairs)  33.2 us
    all_to_all x1, blocking collectives, on_device(): lax.all_to_all(paired.reshape(groups, 8, model_width), 'exp', split_axis=...  18.3 us
    all_to_all x1, blocking collectives, on_device(): lax.all_to_all(summed.reshape(expert_count, capacity, model_width), 'exp'...  15.7 us
    all_to_all x1, blocking collectives, on_device(): lax.all_to_all(buffer.reshape(expert_count, capacity, model_width), 'exp'...  12.6 us
    pallas_call x2, Pallas kernels, experts_call(): pl.pallas_call(functools.partial(experts_kernel, len(blocks), holds), out...  6.69 us
    ppermute x6, waiting for transfers between devices, core_swap(): return lax.ppermute(value, 'exp', CORE_SWAP)  4.1 us
    pallas_call x1, Pallas kernels, far_call(): pl.pallas_call(far_kernel, out_shape=(out, out), in_specs=[pl.BlockSpec(m...  4.08 us
  transfers between devices with their start and end apart: 25, of which 14 were waited for; matrix products, arithmetic and copies ran while one was open for 2% of the time, Pallas kernels for 5%

profile of v3, /device:TPU:1, one launch (start us, length us, event | category | flops | bytes accessed | tf_op | source)
XLA Modules:
  0.0 161.9 jit_solution(13405866108638122760)
XLA Ops:
  2.8 4.7 %collective-permute-start.2 = (bf16[4,576,128]{2,1,0:T(8,128)(2,1)S(1)}, bf16[4,576,128]{2,1,0:T(8,128)(2,1)S(1)}, u32[]{:S(2)}, u32[]{:S(2)}) collective-permute-start(bf16[4,576,128]{2,1,0:T(8,128)(2,1)S(1)} %fusion.6.own), channel_id=1, source_target_pairs={{0,16},{1,49},{2,18},{3,51},{4,20},{5,53},{6,22},{7,55},{8,24},{9,... | collective-permute-start | bytes 1769480 | tf_op jit(solution)/shard_map/ppermute | solution.py:43
  7.4 3.0 %collective-permute-start = (bf16[2,576,128]{2,1,0:T(8,128)(2,1)S(1)}, bf16[2,576,128]{2,1,0:T(8,128)(2,1)S(1)}, u32[]{:S(2)}, u32[]{:S(2)}) collective-permute-start(bf16[2,576,128]{2,1,0:T(8,128)(2,1)S(1)} %constant_dynamic-slice_fusion.1), channel_id=1, source_target_pairs={{0,64},{1,65},{2,66},{3,67},{4,68},{5,69},{6,70},{7,71},{8,72},{9,... | collective-permute-start | bytes 884744 | tf_op jit(solution)/shard_map/ppermute | solution.py:43
  11.0 6.0 %collective-permute-done.side = bf16[2,576,128]{2,1,0:T(8,128)(2,1)S(1)} collective-permute-done((bf16[2,576,128]{2,1,0:T(8,128)(2,1)S(1)}, bf16[2,576,128]{2,1,0:T(8,128)(2,1)S(1)}, u32[]{:S(2)}, u32[]{:S(2)}) %collective-permute-start) | collective-permute-done | bytes 294944 | tf_op jit(solution)/shard_map/ppermute | solution.py:43
  19.9 4.0 %collective-permute-done.5.far = bf16[2,576,128]{2,1,0:T(8,128)(2,1)S(1)} collective-permute-done((bf16[2,576,128]{2,1,0:T(8,128)(2,1)S(1)}, bf16[2,576,128]{2,1,0:T(8,128)(2,1)S(1)}, u32[]{:S(2)}, u32[]{:S(2)}) %collective-permute-start.5) | collective-permute-done | bytes 294944 | tf_op jit(solution)/shard_map/ppermute | solution.py:43
  23.9 2.9 %collective-permute-start.7 = (bf16[2,576,128]{2,1,0:T(8,128)(2,1)S(1)}, bf16[2,576,128]{2,1,0:T(8,128)(2,1)S(1)}, u32[]{:S(2)}, u32[]{:S(2)}) collective-permute-start(bf16[2,576,128]{2,1,0:T(8,128)(2,1)S(1)} %collective-permute-done.5.far), channel_id=1, source_target_pairs={{0,64},{1,65},{2,66},{3,67},{4,68},{5,69},{6,70},{7,71},{8,72},{9,... | collective-permute-start | bytes 884744 | tf_op jit(solution)/shard_map/ppermute | solution.py:43
  27.0 2.5 %collective-permute-start.6 = (bf16[2,576,128]{2,1,0:T(8,128)(2,1)S(1)}, bf16[2,576,128]{2,1,0:T(8,128)(2,1)S(1)}, u32[]{:S(2)}, u32[]{:S(2)}) collective-permute-start(bf16[2,576,128]{2,1,0:T(8,128)(2,1)S(1)} %collective-permute-done.5.far), channel_id=1, source_target_pairs={{0,1},{1,0},{2,3},{3,2},{4,5},{5,4},{6,7},{7,6},{8,9},{9,8},{10,11... | collective-permute-start | bytes 884744 | tf_op jit(solution)/shard_map/ppermute | solution.py:47
  29.5 3.7 %attention_near.1 = (f32[512,128]{1,0:T(8,128)S(1)}, f32[512,128]{1,0:T(8,128)S(1)}, f32[512,512]{1,0:T(8,128)S(1)}, bf16[512,7168]{1,0:T(8,128)(2,1)S(1)}, f32[8,128]{1,0:T(8,128)S(1)}) custom-call(s32[8,32]{1,0:T(8,128)S(1)} %copy-done.2, bf16[512,576]{1,0:T(8,128)(2,1)S(1)} %bitcast.42, bf16[4,576,128]{2,1,0:T(8,128)(2,1)S(1)} %fusion.6.own, ...), custom_call_target="tpu_custom_call" | custom-call | flops 3000000000 | bytes 12000000 | tf_op jit(solution)/shard_map/attention_near/pallas_call | solution.py:234
  36.9 4.1 %attention_far.1 = (bf16[64,7168]{1,0:T(8,128)(2,1)S(1)}, bf16[64,7168]{1,0:T(8,128)(2,1)S(1)}) custom-call(s32[8,32]{1,0:T(8,128)S(1)} %copy-done.2, bf16[512,576]{1,0:T(8,128)(2,1)S(1)} %bitcast.43, bf16[4,576,128]{2,1,0:T(8,128)(2,1)S(1)} %collective-permute-done.3.beside, bf16[4,576,128]{2,1,0:T(8,128)(2,1)S(1)} %collective-permute-done.4.beside_other, ...), custom_call_target="tpu_custom_call" | custom-call | flops 4000000000 | bytes 14000000 | tf_op jit(solution)/shard_map/attention_far/pallas_call | solution.py:264
  43.7 18.3 %all_to_all.15 = bf16[8,8,7168]{2,1,0:T(8,128)(2,1)S(1)} all-to-all(bf16[8,8,7168]{2,1,0:T(8,128)(2,1)S(1)} %fusion.5), channel_id=1, replica_groups={{0,2,4,6,8,10,12,14},{1,3,5,7,9,11,13,15},{16,18,20,22,24,26,28,30},{17..., dimensions={0} | all-to-all | bytes 1835008 | tf_op jit(solution)/shard_map/all_to_all | solution.py:486
  63.1 12.6 %all_to_all.16 = bf16[16,2,7168]{2,1,0:T(2,128)(2,1)S(1)} all-to-all(bf16[16,2,7168]{2,1,0:T(2,128)(2,1)S(1)} %reshape.134), channel_id=1, replica_groups=mesh['ctx'=8,'exp'=16] {'exp'}, dimensions={0} | all-to-all | bytes 917504 | tf_op jit(solution)/shard_map/all_to_all | solution.py:508
  76.9 3.7 %collective-permute-start.13 = (bf16[32,7168]{1,0:T(8,128)(2,1)S(1)}, bf16[32,7168]{1,0:T(8,128)(2,1)S(1)}, u32[]{:S(2)}, u32[]{:S(2)}) collective-permute-start(bf16[32,7168]{1,0:T(8,128)(2,1)S(1)} %reshape.135.refs_0_), channel_id=1, source_target_pairs={{0,64},{1,65},{2,66},{3,67},{4,68},{5,69},{6,70},{7,71},{8,72},{9,... | collective-permute-start | bytes 1376264 | tf_op jit(solution)/shard_map/ppermute | solution.py:43
  80.5 3.1 %collective-permute-done.11.refs_1_ = bf16[32,7168]{1,0:T(8,128)(2,1)S(1)} collective-permute-done((bf16[32,7168]{1,0:T(8,128)(2,1)S(1)}, bf16[32,7168]{1,0:T(8,128)(2,1)S(1)}, u32[]{:S(2)}, u32[]{:S(2)}) %collective-permute-start.11) | collective-permute-done | bytes 458784 | tf_op jit(solution)/shard_map/ppermute | solution.py:43
  85.7 5.6 %collective-permute-done.13.refs_3_ = bf16[32,7168]{1,0:T(8,128)(2,1)S(1)} collective-permute-done((bf16[32,7168]{1,0:T(8,128)(2,1)S(1)}, bf16[32,7168]{1,0:T(8,128)(2,1)S(1)}, u32[]{:S(2)}, u32[]{:S(2)}) %collective-permute-start.13) | collective-permute-done | bytes 458784 | tf_op jit(solution)/shard_map/ppermute | solution.py:43
  91.5 2.5 %collective-permute-start.16 = (bf16[32,7168]{1,0:T(8,128)(2,1)S(1)}, bf16[32,7168]{1,0:T(8,128)(2,1)S(1)}, u32[]{:S(2)}, u32[]{:S(2)}) collective-permute-start(bf16[32,7168]{1,0:T(8,128)(2,1)S(1)} %collective-permute-done.13.refs_3_), channel_id=1, source_target_pairs={{0,16},{1,49},{2,18},{3,51},{4,20},{5,53},{6,22},{7,55},{8,24},{9,... | collective-permute-start | bytes 1376264 | tf_op jit(solution)/shard_map/ppermute | solution.py:43
  94.0 3.2 %collective-permute-start.18 = (bf16[32,7168]{1,0:T(8,128)(2,1)S(1)}, bf16[32,7168]{1,0:T(8,128)(2,1)S(1)}, u32[]{:S(2)}, u32[]{:S(2)}) collective-permute-start(bf16[32,7168]{1,0:T(8,128)(2,1)S(1)} %collective-permute-done.15.refs_0_), channel_id=1, source_target_pairs={{0,64},{1,65},{2,66},{3,67},{4,68},{5,69},{6,70},{7,71},{8,72},{9,... | collective-permute-start | bytes 1376264 | tf_op jit(solution)/shard_map/ppermute | solution.py:43
  97.6 4.9 %experts_near.1 = (bf16[32,7168]{1,0:T(8,128)(2,1)S(1)}, bf16[32,7168]{1,0:T(8,128)(2,1)S(1)}, bf16[32,7168]{1,0:T(8,128)(2,1)S(1)}, bf16[32,7168]{1,0:T(8,128)(...) custom-call(bf16[32,7168]{1,0:T(8,128)(2,1)S(1)} %reshape.135.refs_0_, ...), custom_call_target="tpu_custom_call" | custom-call | flops 1500000000 | bytes 15000000 | tf_op jit(solution)/shard_map/experts_near/pallas_call | solution.py:385
  102.5 4.9 %collective-permute-done.17.refs_2_ = bf16[32,7168]{1,0:T(8,128)(2,1)S(1)} collective-permute-done((bf16[32,7168]{1,0:T(8,128)(2,1)S(1)}, bf16[32,7168]{1,0:T(8,128)(2,1)S(1)}, u32[]{:S(2)}, u32[]{:S(2)}) %collective-permute-start.17) | collective-permute-done | bytes 458784 | tf_op jit(solution)/shard_map/ppermute | solution.py:43
  109.3 4.6 %collective-permute-start.22 = (bf16[32,7168]{1,0:T(8,128)(2,1)S(1)}, bf16[32,7168]{1,0:T(8,128)(2,1)S(1)}, u32[]{:S(2)}, u32[]{:S(2)}) collective-permute-start(bf16[32,7168]{1,0:T(8,128)(2,1)S(1)} %get-tuple-element.57), channel_id=1, source_target_pairs={{0,64},{1,65},{2,66},{3,67},{4,68},{5,69},{6,70},{7,71},{8,72},{9,... | collective-permute-start | bytes 1376264 | tf_op jit(solution)/shard_map/ppermute | solution.py:43
  116.5 5.2 %collective-permute-done.22 = bf16[32,7168]{1,0:T(8,128)(2,1)S(1)} collective-permute-done((bf16[32,7168]{1,0:T(8,128)(2,1)S(1)}, bf16[32,7168]{1,0:T(8,128)(2,1)S(1)}, u32[]{:S(2)}, u32[]{:S(2)}) %collective-permute-start.22) | collective-permute-done | bytes 458784 | tf_op jit(solution)/shard_map/ppermute | solution.py:43
  121.9 2.6 %collective-permute-done.19 = bf16[32,7168]{1,0:T(8,128)(2,1)S(1)} collective-permute-done((bf16[32,7168]{1,0:T(8,128)(2,1)S(1)}, bf16[32,7168]{1,0:T(8,128)(2,1)S(1)}, u32[]{:S(2)}, u32[]{:S(2)}) %collective-permute-start.19) | collective-permute-done | bytes 458784 | tf_op jit(solution)/shard_map/ppermute | solution.py:43
  124.6 8.6 %collective-permute-done.20 = bf16[32,7168]{1,0:T(8,128)(2,1)S(1)} collective-permute-done((bf16[32,7168]{1,0:T(8,128)(2,1)S(1)}, bf16[32,7168]{1,0:T(8,128)(2,1)S(1)}, u32[]{:S(2)}, u32[]{:S(2)}) %collective-permute-start.20) | collective-permute-done | bytes 458784 | tf_op jit(solution)/shard_map/ppermute | solution.py:43
  137.0 5.2 %collective-permute-done.21 = bf16[32,7168]{1,0:T(8,128)(2,1)S(1)} collective-permute-done((bf16[32,7168]{1,0:T(8,128)(2,1)S(1)}, bf16[32,7168]{1,0:T(8,128)(2,1)S(1)}, u32[]{:S(2)}, u32[]{:S(2)}) %collective-permute-start.21) | collective-permute-done | bytes 458784 | tf_op jit(solution)/shard_map/ppermute | solution.py:43
  142.3 2.5 %collective-permute-done.24 = bf16[32,7168]{1,0:T(8,128)(2,1)S(1)} collective-permute-done((bf16[32,7168]{1,0:T(8,128)(2,1)S(1)}, bf16[32,7168]{1,0:T(8,128)(2,1)S(1)}, u32[]{:S(2)}, u32[]{:S(2)}) %collective-permute-start.24) | collective-permute-done | bytes 458784 | tf_op jit(solution)/shard_map/ppermute | solution.py:43
  145.2 15.7 %all_to_all.17 = bf16[16,2,7168]{2,1,0:T(2,128)(2,1)S(1)} all-to-all(bf16[16,2,7168]{2,1,0:T(2,128)(2,1)S(1)} %reshape.136), channel_id=1, replica_groups=mesh['ctx'=8,'exp'=16] {'exp'}, dimensions={0} | all-to-all | bytes 917504 | tf_op jit(solution)/shard_map/all_to_all | solution.py:523
  (89 shorter events, 26.2 us)
Async XLA Ops:
  2.8 14.6 %collective-permute-start.2 = (bf16[4,576,128]{2,1,0:T(8,128)(2,1)S(1)}, bf16[4,576,128]{2,1,0:T(8,128)(2,1)S(1)}, u32[]{:S(2)}, u32[]{:S(2)}) collective-permute-start(bf16[4,576,128]{2,1,0:T(8,128)(2,1)S(1)} %fusion.6.own), channel_id=1, source_target_pairs={{0,16},{1,49},{2,18},{3,51},{4,20},{5,53},{6,22},{7,55},{8,24},{9,... | collective-permute-start | bytes 1769480 | tf_op jit(solution)/shard_map/ppermute | solution.py:43
  7.4 9.6 %collective-permute-start = (bf16[2,576,128]{2,1,0:T(8,128)(2,1)S(1)}, bf16[2,576,128]{2,1,0:T(8,128)(2,1)S(1)}, u32[]{:S(2)}, u32[]{:S(2)}) collective-permute-start(bf16[2,576,128]{2,1,0:T(8,128)(2,1)S(1)} %constant_dynamic-slice_fusion.1), channel_id=1, source_target_pairs={{0,64},{1,65},{2,66},{3,67},{4,68},{5,69},{6,70},{7,71},{8,72},{9,... | collective-permute-start | bytes 884744 | tf_op jit(solution)/shard_map/ppermute | solution.py:43
  17.4 12.1 %collective-permute-start.8 = (bf16[4,576,128]{2,1,0:T(8,128)(2,1)S(1)}, bf16[4,576,128]{2,1,0:T(8,128)(2,1)S(1)}, u32[]{:S(2)}, u32[]{:S(2)}) collective-permute-start(bf16[4,576,128]{2,1,0:T(8,128)(2,1)S(1)} %collective-permute-done.2.beside), channel_id=1, source_target_pairs={{0,1},{1,0},{2,3},{3,2},{4,5},{5,4},{6,7},{7,6},{8,9},{9,8},{10,11... | collective-permute-start | bytes 1769480 | tf_op jit(solution)/shard_map/ppermute | solution.py:47
  18.0 5.9 %collective-permute-start.5 = (bf16[2,576,128]{2,1,0:T(8,128)(2,1)S(1)}, bf16[2,576,128]{2,1,0:T(8,128)(2,1)S(1)}, u32[]{:S(2)}, u32[]{:S(2)}) collective-permute-start(bf16[2,576,128]{2,1,0:T(8,128)(2,1)S(1)} %constant_dynamic-slice_fusion), channel_id=1, source_target_pairs={{0,16},{1,49},{2,18},{3,51},{4,20},{5,53},{6,22},{7,55},{8,24},{9,... | collective-permute-start | bytes 884744 | tf_op jit(solution)/shard_map/ppermute | solution.py:43
  19.1 15.2 %collective-permute-start.3 = (bf16[4,576,128]{2,1,0:T(8,128)(2,1)S(1)}, bf16[4,576,128]{2,1,0:T(8,128)(2,1)S(1)}, u32[]{:S(2)}, u32[]{:S(2)}) collective-permute-start(bf16[4,576,128]{2,1,0:T(8,128)(2,1)S(1)} %pad_maximum_fusion), channel_id=1, source_target_pairs={{0,16},{1,49},{2,18},{3,51},{4,20},{5,53},{6,22},{7,55},{8,24},{9,... | collective-permute-start | bytes 1769480 | tf_op jit(solution)/shard_map/ppermute | solution.py:43
  23.9 10.6 %collective-permute-start.7 = (bf16[2,576,128]{2,1,0:T(8,128)(2,1)S(1)}, bf16[2,576,128]{2,1,0:T(8,128)(2,1)S(1)}, u32[]{:S(2)}, u32[]{:S(2)}) collective-permute-start(bf16[2,576,128]{2,1,0:T(8,128)(2,1)S(1)} %collective-permute-done.5.far), channel_id=1, source_target_pairs={{0,64},{1,65},{2,66},{3,67},{4,68},{5,69},{6,70},{7,71},{8,72},{9,... | collective-permute-start | bytes 884744 | tf_op jit(solution)/shard_map/ppermute | solution.py:43
  27.0 8.1 %collective-permute-start.6 = (bf16[2,576,128]{2,1,0:T(8,128)(2,1)S(1)}, bf16[2,576,128]{2,1,0:T(8,128)(2,1)S(1)}, u32[]{:S(2)}, u32[]{:S(2)}) collective-permute-start(bf16[2,576,128]{2,1,0:T(8,128)(2,1)S(1)} %collective-permute-done.5.far), channel_id=1, source_target_pairs={{0,1},{1,0},{2,3},{3,2},{4,5},{5,4},{6,7},{7,6},{8,9},{9,8},{10,11... | collective-permute-start | bytes 884744 | tf_op jit(solution)/shard_map/ppermute | solution.py:47
  34.3 2.5 %collective-permute-start.4 = (bf16[4,576,128]{2,1,0:T(8,128)(2,1)S(1)}, bf16[4,576,128]{2,1,0:T(8,128)(2,1)S(1)}, u32[]{:S(2)}, u32[]{:S(2)}) collective-permute-start(bf16[4,576,128]{2,1,0:T(8,128)(2,1)S(1)} %collective-permute-done.3.beside), channel_id=1, source_target_pairs={{0,1},{1,0},{2,3},{3,2},{4,5},{5,4},{6,7},{7,6},{8,9},{9,8},{10,11... | collective-permute-start | bytes 1769480 | tf_op jit(solution)/shard_map/ppermute | solution.py:47
  34.5 2.4 %collective-permute-start.9 = (bf16[2,576,128]{2,1,0:T(8,128)(2,1)S(1)}, bf16[2,576,128]{2,1,0:T(8,128)(2,1)S(1)}, u32[]{:S(2)}, u32[]{:S(2)}) collective-permute-start(bf16[2,576,128]{2,1,0:T(8,128)(2,1)S(1)} %fusion.15.side_far), channel_id=1, source_target_pairs={{0,1},{1,0},{2,3},{3,2},{4,5},{5,4},{6,7},{7,6},{8,9},{9,8},{10,11... | collective-permute-start | bytes 884744 | tf_op jit(solution)/shard_map/ppermute | solution.py:47
  40.9 2.6 %collective-permute-start.10 = (bf16[64,7168]{1,0:T(8,128)(2,1)S(1)}, bf16[64,7168]{1,0:T(8,128)(2,1)S(1)}, u32[]{:S(2)}, u32[]{:S(2)}) collective-permute-start(bf16[64,7168]{1,0:T(8,128)(2,1)S(1)} %get-tuple-element.44), channel_id=1, source_target_pairs={{0,1},{1,0},{2,3},{3,2},{4,5},{5,4},{6,7},{7,6},{8,9},{9,8},{10,11... | collective-permute-start | bytes 2752520 | tf_op jit(solution)/shard_map/ppermute | solution.py:47
  75.9 7.7 %collective-permute-start.11 = (bf16[32,7168]{1,0:T(8,128)(2,1)S(1)}, bf16[32,7168]{1,0:T(8,128)(2,1)S(1)}, u32[]{:S(2)}, u32[]{:S(2)}) collective-permute-start(bf16[32,7168]{1,0:T(8,128)(2,1)S(1)} %reshape.135.refs_0_), channel_id=1, source_target_pairs={{0,16},{1,49},{2,18},{3,51},{4,20},{5,53},{6,22},{7,55},{8,24},{9,... | collective-permute-start | bytes 1376264 | tf_op jit(solution)/shard_map/ppermute | solution.py:43
  76.9 14.5 %collective-permute-start.13 = (bf16[32,7168]{1,0:T(8,128)(2,1)S(1)}, bf16[32,7168]{1,0:T(8,128)(2,1)S(1)}, u32[]{:S(2)}, u32[]{:S(2)}) collective-permute-start(bf16[32,7168]{1,0:T(8,128)(2,1)S(1)} %reshape.135.refs_0_), channel_id=1, source_target_pairs={{0,64},{1,65},{2,66},{3,67},{4,68},{5,69},{6,70},{7,71},{8,72},{9,... | collective-permute-start | bytes 1376264 | tf_op jit(solution)/shard_map/ppermute | solution.py:43
  83.6 10.4 %collective-permute-start.15 = (bf16[32,7168]{1,0:T(8,128)(2,1)S(1)}, bf16[32,7168]{1,0:T(8,128)(2,1)S(1)}, u32[]{:S(2)}, u32[]{:S(2)}) collective-permute-start(bf16[32,7168]{1,0:T(8,128)(2,1)S(1)} %collective-permute-done.11.refs_1_), channel_id=1, source_target_pairs={{0,16},{1,49},{2,18},{3,51},{4,20},{5,53},{6,22},{7,55},{8,24},{9,... | collective-permute-start | bytes 1376264 | tf_op jit(solution)/shard_map/ppermute | solution.py:43
  85.7 11.9 %collective-permute-start.12 = (bf16[32,7168]{1,0:T(8,128)(2,1)S(1)}, bf16[32,7168]{1,0:T(8,128)(2,1)S(1)}, u32[]{:S(2)}, u32[]{:S(2)}) collective-permute-start(bf16[32,7168]{1,0:T(8,128)(2,1)S(1)} %reshape.135.refs_0_), channel_id=1, source_target_pairs={{0,48},{1,17},{2,50},{3,19},{4,52},{5,21},{6,54},{7,23},{8,56},{9,... | collective-permute-start | bytes 1376264 | tf_op jit(solution)/shard_map/ppermute | solution.py:43
  91.3 16.1 %collective-permute-start.17 = (bf16[32,7168]{1,0:T(8,128)(2,1)S(1)}, bf16[32,7168]{1,0:T(8,128)(2,1)S(1)}, u32[]{:S(2)}, u32[]{:S(2)}) collective-permute-start(bf16[32,7168]{1,0:T(8,128)(2,1)S(1)} %collective-permute-done.13.refs_3_), channel_id=1, source_target_pairs={{0,48},{1,17},{2,50},{3,19},{4,52},{5,21},{6,54},{7,23},{8,56},{9,... | collective-permute-start | bytes 1376264 | tf_op jit(solution)/shard_map/ppermute | solution.py:43
  91.5 16.0 %collective-permute-start.16 = (bf16[32,7168]{1,0:T(8,128)(2,1)S(1)}, bf16[32,7168]{1,0:T(8,128)(2,1)S(1)}, u32[]{:S(2)}, u32[]{:S(2)}) collective-permute-start(bf16[32,7168]{1,0:T(8,128)(2,1)S(1)} %collective-permute-done.13.refs_3_), channel_id=1, source_target_pairs={{0,16},{1,49},{2,18},{3,51},{4,20},{5,53},{6,22},{7,55},{8,24},{9,... | collective-permute-start | bytes 1376264 | tf_op jit(solution)/shard_map/ppermute | solution.py:43
  94.0 13.5 %collective-permute-start.18 = (bf16[32,7168]{1,0:T(8,128)(2,1)S(1)}, bf16[32,7168]{1,0:T(8,128)(2,1)S(1)}, u32[]{:S(2)}, u32[]{:S(2)}) collective-permute-start(bf16[32,7168]{1,0:T(8,128)(2,1)S(1)} %collective-permute-done.15.refs_0_), channel_id=1, source_target_pairs={{0,64},{1,65},{2,66},{3,67},{4,68},{5,69},{6,70},{7,71},{8,72},{9,... | collective-permute-start | bytes 1376264 | tf_op jit(solution)/shard_map/ppermute | solution.py:43
  109.3 12.5 %collective-permute-start.22 = (bf16[32,7168]{1,0:T(8,128)(2,1)S(1)}, bf16[32,7168]{1,0:T(8,128)(2,1)S(1)}, u32[]{:S(2)}, u32[]{:S(2)}) collective-permute-start(bf16[32,7168]{1,0:T(8,128)(2,1)S(1)} %get-tuple-element.57), channel_id=1, source_target_pairs={{0,64},{1,65},{2,66},{3,67},{4,68},{5,69},{6,70},{7,71},{8,72},{9,... | collective-permute-start | bytes 1376264 | tf_op jit(solution)/shard_map/ppermute | solution.py:43
  113.8 23.2 %collective-permute-start.14 = (bf16[32,7168]{1,0:T(8,128)(2,1)S(1)}, bf16[32,7168]{1,0:T(8,128)(2,1)S(1)}, u32[]{:S(2)}, u32[]{:S(2)}) collective-permute-start(bf16[32,7168]{1,0:T(8,128)(2,1)S(1)} %get-tuple-element.47), channel_id=1, source_target_pairs={{0,16},{1,49},{2,18},{3,51},{4,20},{5,53},{6,22},{7,55},{8,24},{9,... | collective-permute-start | bytes 1376264 | tf_op jit(solution)/shard_map/ppermute | solution.py:43
  113.8 10.7 %collective-permute-start.19 = (bf16[32,7168]{1,0:T(8,128)(2,1)S(1)}, bf16[32,7168]{1,0:T(8,128)(2,1)S(1)}, u32[]{:S(2)}, u32[]{:S(2)}) collective-permute-start(bf16[32,7168]{1,0:T(8,128)(2,1)S(1)} %get-tuple-element.53), channel_id=1, source_target_pairs={{0,48},{1,17},{2,50},{3,19},{4,52},{5,21},{6,54},{7,23},{8,56},{9,... | collective-permute-start | bytes 1376264 | tf_op jit(solution)/shard_map/ppermute | solution.py:43
  115.3 17.9 %collective-permute-start.20 = (bf16[32,7168]{1,0:T(8,128)(2,1)S(1)}, bf16[32,7168]{1,0:T(8,128)(2,1)S(1)}, u32[]{:S(2)}, u32[]{:S(2)}) collective-permute-start(bf16[32,7168]{1,0:T(8,128)(2,1)S(1)} %get-tuple-element.54), channel_id=1, source_target_pairs={{0,16},{1,49},{2,18},{3,51},{4,20},{5,53},{6,22},{7,55},{8,24},{9,... | collective-permute-start | bytes 1376264 | tf_op jit(solution)/shard_map/ppermute | solution.py:43
  121.9 13.9 %collective-permute-start.23 = (bf16[32,7168]{1,0:T(8,128)(2,1)S(1)}, bf16[32,7168]{1,0:T(8,128)(2,1)S(1)}, u32[]{:S(2)}, u32[]{:S(2)}) collective-permute-start(bf16[32,7168]{1,0:T(8,128)(2,1)S(1)} %add_convert_fusion.3), channel_id=1, source_target_pairs={{0,48},{1,17},{2,50},{3,19},{4,52},{5,21},{6,54},{7,23},{8,56},{9,... | collective-permute-start | bytes 1376264 | tf_op jit(solution)/shard_map/ppermute | solution.py:43
  133.4 8.9 %collective-permute-start.21 = (bf16[32,7168]{1,0:T(8,128)(2,1)S(1)}, bf16[32,7168]{1,0:T(8,128)(2,1)S(1)}, u32[]{:S(2)}, u32[]{:S(2)}) collective-permute-start(bf16[32,7168]{1,0:T(8,128)(2,1)S(1)} %add_convert_fusion.4), channel_id=1, source_target_pairs={{0,64},{1,65},{2,66},{3,67},{4,68},{5,69},{6,70},{7,71},{8,72},{9,... | collective-permute-start | bytes 1376264 | tf_op jit(solution)/shard_map/ppermute | solution.py:43
  135.8 8.9 %collective-permute-start.24 = (bf16[32,7168]{1,0:T(8,128)(2,1)S(1)}, bf16[32,7168]{1,0:T(8,128)(2,1)S(1)}, u32[]{:S(2)}, u32[]{:S(2)}) collective-permute-start(bf16[32,7168]{1,0:T(8,128)(2,1)S(1)} %add_convert_fusion.2), channel_id=1, source_target_pairs={{0,48},{1,17},{2,50},{3,19},{4,52},{5,21},{6,54},{7,23},{8,56},{9,... | collective-permute-start | bytes 1376264 | tf_op jit(solution)/shard_map/ppermute | solution.py:43
  (8 other events, 201.4 us)

commit v4 on v3

--- a/solution.py
+++ b/solution.py
@@ -88,25 +88,25 @@
     def flags_of(number):
         return [flag(place) for _, _, place in steps[number]]
 
+    all_flags = [flags_of(number) for number in range(len(steps))]
+    live = [(sum(flags) > 0).astype(jnp.int32) for flags in all_flags]
+    straight = sum(live) >= len(steps) - 1
+
     def score(step, number):
-        flags = flags_of(number)
-
-        @pl.when(sum(flags) > 0)
-        def _():
-            found = jnp.dot(
-                queries[...], keys_of(step, queries.shape[1]), preferred_element_type=F32
-            )
-            column = lax.broadcasted_iota(jnp.int32, (1, STEP_BLOCKS * block), 1) // block
-            shown = jnp.zeros(column.shape, jnp.int32)
-            for i, flag in enumerate(flags):
-                shown = jnp.where(column == i, flag, shown)
-            found = jnp.where(shown > 0, found, -1e30)
-            if diagonal and number == 0:
-                last = (STEP_BLOCKS - 1) * block
-                seen = jnp.where(causal(), found[:, last:], -1e30)
-                found = jnp.concatenate([found[:, :last], seen], axis=1)
-            scores[number] = found
-            top[...] = jnp.maximum(top[...], lane_fold(found, jnp.maximum))
+        found = jnp.dot(
+            queries[...], keys_of(step, queries.shape[1]), preferred_element_type=F32
+        )
+        column = lax.broadcasted_iota(jnp.int32, (1, STEP_BLOCKS * block), 1) // block
+        shown = jnp.zeros(column.shape, jnp.int32)
+        for i, flag in enumerate(all_flags[number]):
+            shown = jnp.where(column == i, flag, shown)
+        found = jnp.where(shown > 0, found, -1e30)
+        if diagonal and number == 0:
+            last = (STEP_BLOCKS - 1) * block
+            seen = jnp.where(causal(), found[:, last:], -1e30)
+            found = jnp.concatenate([found[:, :last], seen], axis=1)
+        scores[number] = found
+        top[...] = jnp.maximum(top[...], lane_fold(found, jnp.maximum))
 
     def causal():
         tokens = rows // HEADS_HERE
@@ -117,25 +117,31 @@
         token = within // 8 * 16 + side * 8 + within % 8
         return lax.broadcasted_iota(jnp.int32, (1, block), 1) <= token
 
-    for number, step in enumerate(steps):
-        score(step, number)
-    row_top = jnp.max(top[...], axis=1, keepdims=True)
-
-    def mix(step, number):
-        @pl.when(sum(flags_of(number)) > 0)
-        def _():
-            weights = jnp.exp2((scores[number] - row_top) * factor)
-            total[...] += lane_fold(weights, jnp.add)
-            mixture[...] += lax.dot_general(
-                weights.astype(BF16),
-                keys_of(step, latent_width),
-                (((1,), (1,)), ((), ())),
-                preferred_element_type=F32,
-            )
-
-    for number, step in enumerate(steps):
-        mix(step, number)
-    return row_top
+    def mix(row_top, step, number):
+        weights = jnp.exp2((scores[number] - row_top) * factor)
+        total[...] += lane_fold(weights, jnp.add)
+        mixture[...] += lax.dot_general(
+            weights.astype(BF16),
+            keys_of(step, latent_width),
+            (((1,), (1,)), ((), ())),
+            preferred_element_type=F32,
+        )
+
+    def all_steps(branches):
+        def each_step(body):
+            for number, step in enumerate(steps):
+                if branches:
+                    pl.when(live[number] > 0)(functools.partial(body, step, number))
+                else:
+                    body(step, number)
+
+        each_step(score)
+        row_top = jnp.max(top[...], axis=1, keepdims=True)
+        each_step(functools.partial(mix, row_top))
+        top[...] = jnp.broadcast_to(row_top, top.shape)
+
+    pl.when(straight)(functools.partial(all_steps, False))
+    pl.when(jnp.logical_not(straight))(functools.partial(all_steps, True))
 
 
 def whole(part, dy, dz):
@@ -166,8 +172,7 @@
         whole(beside_other, 0, way),
         halves(side, side_other, 1, 0, first),
     ]
-    row_top = attend(mask, queries, steps, True, scores, top, total, mixture)
-    top[...] = jnp.broadcast_to(row_top, top.shape)
+    attend(mask, queries, steps, True, scores, top, total, mixture)
     done[...] = jnp.ones_like(done)
     copy.wait()
 
@@ -195,7 +200,8 @@
         halves(far, far_other, 0, 2, first),
         halves(side_far, side_far_other, 1, 2, first),
     ]
-    far_top = attend(mask, queries, steps, False, scores, top, total, mixture)
+    attend(mask, queries, steps, False, scores, top, total, mixture)
+    far_top = top[:, :1]
     near_row_top = near_top[:, :1]
     both_top = jnp.maximum(near_row_top, far_top)
     near_scale = jnp.exp2((near_row_top - both_top) * factor)

time: 162 us -> 161 us (level)
  starting transfers between devices: 37.1 us -> 32.1 us
  Pallas kernels: 14.5 us -> 16.3 us
  waiting for transfers between devices: 54.7 us -> 56.4 us
    ppermute x19, starting transfers between devices: 33.2 us -> 28.2 us  [over_ctx(): return lax.ppermute(value, ('ctx', 'exp'), pairs)]
    pallas_call x1, Pallas kernels: 4.08 us -> 5.9 us  [far_call(): pl.pallas_call(far_kernel, out_shape=(out, out), in_specs=[pl.BlockSpec(m...]
    ppermute x19, waiting for transfers between devices: 50.6 us -> 52.3 us  [over_ctx(): return lax.ppermute(value, ('ctx', 'exp'), pairs)]
  transfers between devices with their start and end apart: 25 -> 25, of which waited for: 14 -> 15; matrix products, arithmetic and copies ran while one was open for 2% -> 2% of each run, Pallas kernels for 5% -> 5%
where the time goes in v4:
time: 161 us
  waiting for transfers between devices  56.4 us (35%)
  blocking collectives  46.9 us (29%)
  starting transfers between devices  32.1 us (20%)
  Pallas kernels  16.3 us (10%)
  other arithmetic  4.76 us (3%)
  local copies, waits for them, and re-layouts  2.01 us (1%)
  between operations  1.67 us (1%)
    ppermute x19, waiting for transfers between devices, over_ctx(): return lax.ppermute(value, ('ctx', 'exp'), pairs)  52.3 us
    ppermute x19, starting transfers between devices, over_ctx(): return lax.ppermute(value, ('ctx', 'exp'), pairs)  28.2 us
    all_to_all x1, blocking collectives, on_device(): lax.all_to_all(paired.reshape(groups, 8, model_width), 'exp', split_axis=...  18.2 us
    all_to_all x1, blocking collectives, on_device(): lax.all_to_all(summed.reshape(expert_count, capacity, model_width), 'exp'...  16 us
    all_to_all x1, blocking collectives, on_device(): lax.all_to_all(buffer.reshape(expert_count, capacity, model_width), 'exp'...  12.6 us
    pallas_call x2, Pallas kernels, experts_call(): pl.pallas_call(functools.partial(experts_kernel, len(blocks), holds), out...  6.69 us
    pallas_call x1, Pallas kernels, far_call(): pl.pallas_call(far_kernel, out_shape=(out, out), in_specs=[pl.BlockSpec(m...  5.9 us
    ppermute x6, waiting for transfers between devices, core_swap(): return lax.ppermute(value, 'exp', CORE_SWAP)  4.07 us
  transfers between devices with their start and end apart: 25, of which 15 were waited for; matrix products, arithmetic and copies ran while one was open for 2% of the time, Pallas kernels for 5%

profile of v4, /device:TPU:1, one launch (start us, length us, event | category | flops | bytes accessed | tf_op | source)
XLA Modules:
  0.0 160.8 jit_solution(9971565740917394054)
XLA Ops:
  2.8 4.7 %collective-permute-start.2 = (bf16[4,576,128]{2,1,0:T(8,128)(2,1)S(1)}, bf16[4,576,128]{2,1,0:T(8,128)(2,1)S(1)}, u32[]{:S(2)}, u32[]{:S(2)}) collective-permute-start(bf16[4,576,128]{2,1,0:T(8,128)(2,1)S(1)} %fusion.6.own), channel_id=1, source_target_pairs={{0,16},{1,49},{2,18},{3,51},{4,20},{5,53},{6,22},{7,55},{8,24},{9,... | collective-permute-start | bytes 1769480 | tf_op jit(solution)/shard_map/ppermute | solution.py:43
  7.4 3.0 %collective-permute-start = (bf16[2,576,128]{2,1,0:T(8,128)(2,1)S(1)}, bf16[2,576,128]{2,1,0:T(8,128)(2,1)S(1)}, u32[]{:S(2)}, u32[]{:S(2)}) collective-permute-start(bf16[2,576,128]{2,1,0:T(8,128)(2,1)S(1)} %constant_dynamic-slice_fusion.1), channel_id=1, source_target_pairs={{0,64},{1,65},{2,66},{3,67},{4,68},{5,69},{6,70},{7,71},{8,72},{9,... | collective-permute-start | bytes 884744 | tf_op jit(solution)/shard_map/ppermute | solution.py:43
  11.0 6.0 %collective-permute-done.side = bf16[2,576,128]{2,1,0:T(8,128)(2,1)S(1)} collective-permute-done((bf16[2,576,128]{2,1,0:T(8,128)(2,1)S(1)}, bf16[2,576,128]{2,1,0:T(8,128)(2,1)S(1)}, u32[]{:S(2)}, u32[]{:S(2)}) %collective-permute-start) | collective-permute-done | bytes 294944 | tf_op jit(solution)/shard_map/ppermute | solution.py:43
  19.9 4.0 %collective-permute-done.5.far = bf16[2,576,128]{2,1,0:T(8,128)(2,1)S(1)} collective-permute-done((bf16[2,576,128]{2,1,0:T(8,128)(2,1)S(1)}, bf16[2,576,128]{2,1,0:T(8,128)(2,1)S(1)}, u32[]{:S(2)}, u32[]{:S(2)}) %collective-permute-start.5) | collective-permute-done | bytes 294944 | tf_op jit(solution)/shard_map/ppermute | solution.py:43
  23.9 2.9 %collective-permute-start.7 = (bf16[2,576,128]{2,1,0:T(8,128)(2,1)S(1)}, bf16[2,576,128]{2,1,0:T(8,128)(2,1)S(1)}, u32[]{:S(2)}, u32[]{:S(2)}) collective-permute-start(bf16[2,576,128]{2,1,0:T(8,128)(2,1)S(1)} %collective-permute-done.5.far), channel_id=1, source_target_pairs={{0,64},{1,65},{2,66},{3,67},{4,68},{5,69},{6,70},{7,71},{8,72},{9,... | collective-permute-start | bytes 884744 | tf_op jit(solution)/shard_map/ppermute | solution.py:43
  27.0 2.5 %collective-permute-start.6 = (bf16[2,576,128]{2,1,0:T(8,128)(2,1)S(1)}, bf16[2,576,128]{2,1,0:T(8,128)(2,1)S(1)}, u32[]{:S(2)}, u32[]{:S(2)}) collective-permute-start(bf16[2,576,128]{2,1,0:T(8,128)(2,1)S(1)} %collective-permute-done.5.far), channel_id=1, source_target_pairs={{0,1},{1,0},{2,3},{3,2},{4,5},{5,4},{6,7},{7,6},{8,9},{9,8},{10,11... | collective-permute-start | bytes 884744 | tf_op jit(solution)/shard_map/ppermute | solution.py:47
  29.5 3.7 %attention_near.1 = (f32[512,128]{1,0:T(8,128)S(1)}, f32[512,128]{1,0:T(8,128)S(1)}, f32[512,512]{1,0:T(8,128)S(1)}, bf16[512,7168]{1,0:T(8,128)(2,1)S(1)}, f32[8,128]{1,0:T(8,128)S(1)}) custom-call(s32[8,32]{1,0:T(8,128)S(1)} %copy-done.2, bf16[512,576]{1,0:T(8,128)(2,1)S(1)} %bitcast.42, bf16[4,576,128]{2,1,0:T(8,128)(2,1)S(1)} %fusion.6.own, ...), custom_call_target="tpu_custom_call" | custom-call | flops 3000000000 | bytes 12000000 | tf_op jit(solution)/shard_map/attention_near/pallas_call | solution.py:240
  36.9 5.9 %attention_far.1 = (bf16[64,7168]{1,0:T(8,128)(2,1)S(1)}, bf16[64,7168]{1,0:T(8,128)(2,1)S(1)}) custom-call(s32[8,32]{1,0:T(8,128)S(1)} %copy-done.2, bf16[512,576]{1,0:T(8,128)(2,1)S(1)} %bitcast.43, bf16[4,576,128]{2,1,0:T(8,128)(2,1)S(1)} %collective-permute-done.3.beside, bf16[4,576,128]{2,1,0:T(8,128)(2,1)S(1)} %collective-permute-done.4.beside_other, ...), custom_call_target="tpu_custom_call" | custom-call | flops 4000000000 | bytes 14000000 | tf_op jit(solution)/shard_map/attention_far/pallas_call | solution.py:270
  43.0 2.3 %collective-permute-done.10 = bf16[64,7168]{1,0:T(8,128)(2,1)S(1)} collective-permute-done((bf16[64,7168]{1,0:T(8,128)(2,1)S(1)}, bf16[64,7168]{1,0:T(8,128)(2,1)S(1)}, u32[]{:S(2)}, u32[]{:S(2)}) %collective-permute-start.10) | collective-permute-done | bytes 917536 | tf_op jit(solution)/shard_map/ppermute | solution.py:47
  45.5 18.2 %all_to_all.15 = bf16[8,8,7168]{2,1,0:T(8,128)(2,1)S(1)} all-to-all(bf16[8,8,7168]{2,1,0:T(8,128)(2,1)S(1)} %fusion.5), channel_id=1, replica_groups={{0,2,4,6,8,10,12,14},{1,3,5,7,9,11,13,15},{16,18,20,22,24,26,28,30},{17..., dimensions={0} | all-to-all | bytes 1835008 | tf_op jit(solution)/shard_map/all_to_all | solution.py:492
  64.9 12.6 %all_to_all.16 = bf16[16,2,7168]{2,1,0:T(2,128)(2,1)S(1)} all-to-all(bf16[16,2,7168]{2,1,0:T(2,128)(2,1)S(1)} %reshape.134), channel_id=1, replica_groups=mesh['ctx'=8,'exp'=16] {'exp'}, dimensions={0} | all-to-all | bytes 917504 | tf_op jit(solution)/shard_map/all_to_all | solution.py:514
  79.4 6.0 %collective-permute-done.11.refs_1_ = bf16[32,7168]{1,0:T(8,128)(2,1)S(1)} collective-permute-done((bf16[32,7168]{1,0:T(8,128)(2,1)S(1)}, bf16[32,7168]{1,0:T(8,128)(2,1)S(1)}, u32[]{:S(2)}, u32[]{:S(2)}) %collective-permute-start.11) | collective-permute-done | bytes 458784 | tf_op jit(solution)/shard_map/ppermute | solution.py:43
  86.9 3.2 %collective-permute-done.13.refs_3_ = bf16[32,7168]{1,0:T(8,128)(2,1)S(1)} collective-permute-done((bf16[32,7168]{1,0:T(8,128)(2,1)S(1)}, bf16[32,7168]{1,0:T(8,128)(2,1)S(1)}, u32[]{:S(2)}, u32[]{:S(2)}) %collective-permute-start.13) | collective-permute-done | bytes 458784 | tf_op jit(solution)/shard_map/ppermute | solution.py:43
  94.0 2.1 %collective-permute-start.18 = (bf16[32,7168]{1,0:T(8,128)(2,1)S(1)}, bf16[32,7168]{1,0:T(8,128)(2,1)S(1)}, u32[]{:S(2)}, u32[]{:S(2)}) collective-permute-start(bf16[32,7168]{1,0:T(8,128)(2,1)S(1)} %collective-permute-done.15.refs_0_), channel_id=1, source_target_pairs={{0,64},{1,65},{2,66},{3,67},{4,68},{5,69},{6,70},{7,71},{8,72},{9,... | collective-permute-start | bytes 1376264 | tf_op jit(solution)/shard_map/ppermute | solution.py:43
  97.1 4.9 %experts_near.1 = (bf16[32,7168]{1,0:T(8,128)(2,1)S(1)}, bf16[32,7168]{1,0:T(8,128)(2,1)S(1)}, bf16[32,7168]{1,0:T(8,128)(2,1)S(1)}, bf16[32,7168]{1,0:T(8,128)(...) custom-call(bf16[32,7168]{1,0:T(8,128)(2,1)S(1)} %reshape.135.refs_0_, ...), custom_call_target="tpu_custom_call" | custom-call | flops 1500000000 | bytes 15000000 | tf_op jit(solution)/shard_map/experts_near/pallas_call | solution.py:391
  102.0 4.9 %collective-permute-done.17.refs_2_ = bf16[32,7168]{1,0:T(8,128)(2,1)S(1)} collective-permute-done((bf16[32,7168]{1,0:T(8,128)(2,1)S(1)}, bf16[32,7168]{1,0:T(8,128)(2,1)S(1)}, u32[]{:S(2)}, u32[]{:S(2)}) %collective-permute-start.17) | collective-permute-done | bytes 458784 | tf_op jit(solution)/shard_map/ppermute | solution.py:43
  108.7 4.0 %collective-permute-start.22 = (bf16[32,7168]{1,0:T(8,128)(2,1)S(1)}, bf16[32,7168]{1,0:T(8,128)(2,1)S(1)}, u32[]{:S(2)}, u32[]{:S(2)}) collective-permute-start(bf16[32,7168]{1,0:T(8,128)(2,1)S(1)} %get-tuple-element.57), channel_id=1, source_target_pairs={{0,64},{1,65},{2,66},{3,67},{4,68},{5,69},{6,70},{7,71},{8,72},{9,... | collective-permute-start | bytes 1376264 | tf_op jit(solution)/shard_map/ppermute | solution.py:43
  115.4 4.8 %collective-permute-done.22 = bf16[32,7168]{1,0:T(8,128)(2,1)S(1)} collective-permute-done((bf16[32,7168]{1,0:T(8,128)(2,1)S(1)}, bf16[32,7168]{1,0:T(8,128)(2,1)S(1)}, u32[]{:S(2)}, u32[]{:S(2)}) %collective-permute-start.22) | collective-permute-done | bytes 458784 | tf_op jit(solution)/shard_map/ppermute | solution.py:43
  120.4 2.9 %collective-permute-done.19 = bf16[32,7168]{1,0:T(8,128)(2,1)S(1)} collective-permute-done((bf16[32,7168]{1,0:T(8,128)(2,1)S(1)}, bf16[32,7168]{1,0:T(8,128)(2,1)S(1)}, u32[]{:S(2)}, u32[]{:S(2)}) %collective-permute-start.19) | collective-permute-done | bytes 458784 | tf_op jit(solution)/shard_map/ppermute | solution.py:43
  123.3 8.4 %collective-permute-done.20 = bf16[32,7168]{1,0:T(8,128)(2,1)S(1)} collective-permute-done((bf16[32,7168]{1,0:T(8,128)(2,1)S(1)}, bf16[32,7168]{1,0:T(8,128)(2,1)S(1)}, u32[]{:S(2)}, u32[]{:S(2)}) %collective-permute-start.20) | collective-permute-done | bytes 458784 | tf_op jit(solution)/shard_map/ppermute | solution.py:43
  131.9 2.3 %collective-permute-done.23 = bf16[32,7168]{1,0:T(8,128)(2,1)S(1)} collective-permute-done((bf16[32,7168]{1,0:T(8,128)(2,1)S(1)}, bf16[32,7168]{1,0:T(8,128)(2,1)S(1)}, u32[]{:S(2)}, u32[]{:S(2)}) %collective-permute-start.23) | collective-permute-done | bytes 458784 | tf_op jit(solution)/shard_map/ppermute | solution.py:43
  135.7 5.0 %collective-permute-done.21 = bf16[32,7168]{1,0:T(8,128)(2,1)S(1)} collective-permute-done((bf16[32,7168]{1,0:T(8,128)(2,1)S(1)}, bf16[32,7168]{1,0:T(8,128)(2,1)S(1)}, u32[]{:S(2)}, u32[]{:S(2)}) %collective-permute-start.21) | collective-permute-done | bytes 458784 | tf_op jit(solution)/shard_map/ppermute | solution.py:43
  140.8 2.5 %collective-permute-done.24 = bf16[32,7168]{1,0:T(8,128)(2,1)S(1)} collective-permute-done((bf16[32,7168]{1,0:T(8,128)(2,1)S(1)}, bf16[32,7168]{1,0:T(8,128)(2,1)S(1)}, u32[]{:S(2)}, u32[]{:S(2)}) %collective-permute-start.24) | collective-permute-done | bytes 458784 | tf_op jit(solution)/shard_map/ppermute | solution.py:43
  143.7 16.0 %all_to_all.17 = bf16[16,2,7168]{2,1,0:T(2,128)(2,1)S(1)} all-to-all(bf16[16,2,7168]{2,1,0:T(2,128)(2,1)S(1)} %reshape.136), channel_id=1, replica_groups=mesh['ctx'=8,'exp'=16] {'exp'}, dimensions={0} | all-to-all | bytes 917504 | tf_op jit(solution)/shard_map/all_to_all | solution.py:529
  (89 shorter events, 26.2 us)
Async XLA Ops:
  2.8 14.6 %collective-permute-start.2 = (bf16[4,576,128]{2,1,0:T(8,128)(2,1)S(1)}, bf16[4,576,128]{2,1,0:T(8,128)(2,1)S(1)}, u32[]{:S(2)}, u32[]{:S(2)}) collective-permute-start(bf16[4,576,128]{2,1,0:T(8,128)(2,1)S(1)} %fusion.6.own), channel_id=1, source_target_pairs={{0,16},{1,49},{2,18},{3,51},{4,20},{5,53},{6,22},{7,55},{8,24},{9,... | collective-permute-start | bytes 1769480 | tf_op jit(solution)/shard_map/ppermute | solution.py:43
  7.4 9.6 %collective-permute-start = (bf16[2,576,128]{2,1,0:T(8,128)(2,1)S(1)}, bf16[2,576,128]{2,1,0:T(8,128)(2,1)S(1)}, u32[]{:S(2)}, u32[]{:S(2)}) collective-permute-start(bf16[2,576,128]{2,1,0:T(8,128)(2,1)S(1)} %constant_dynamic-slice_fusion.1), channel_id=1, source_target_pairs={{0,64},{1,65},{2,66},{3,67},{4,68},{5,69},{6,70},{7,71},{8,72},{9,... | collective-permute-start | bytes 884744 | tf_op jit(solution)/shard_map/ppermute | solution.py:43
  17.4 12.1 %collective-permute-start.8 = (bf16[4,576,128]{2,1,0:T(8,128)(2,1)S(1)}, bf16[4,576,128]{2,1,0:T(8,128)(2,1)S(1)}, u32[]{:S(2)}, u32[]{:S(2)}) collective-permute-start(bf16[4,576,128]{2,1,0:T(8,128)(2,1)S(1)} %collective-permute-done.2.beside), channel_id=1, source_target_pairs={{0,1},{1,0},{2,3},{3,2},{4,5},{5,4},{6,7},{7,6},{8,9},{9,8},{10,11... | collective-permute-start | bytes 1769480 | tf_op jit(solution)/shard_map/ppermute | solution.py:47
  18.0 5.9 %collective-permute-start.5 = (bf16[2,576,128]{2,1,0:T(8,128)(2,1)S(1)}, bf16[2,576,128]{2,1,0:T(8,128)(2,1)S(1)}, u32[]{:S(2)}, u32[]{:S(2)}) collective-permute-start(bf16[2,576,128]{2,1,0:T(8,128)(2,1)S(1)} %constant_dynamic-slice_fusion), channel_id=1, source_target_pairs={{0,16},{1,49},{2,18},{3,51},{4,20},{5,53},{6,22},{7,55},{8,24},{9,... | collective-permute-start | bytes 884744 | tf_op jit(solution)/shard_map/ppermute | solution.py:43
  19.1 15.2 %collective-permute-start.3 = (bf16[4,576,128]{2,1,0:T(8,128)(2,1)S(1)}, bf16[4,576,128]{2,1,0:T(8,128)(2,1)S(1)}, u32[]{:S(2)}, u32[]{:S(2)}) collective-permute-start(bf16[4,576,128]{2,1,0:T(8,128)(2,1)S(1)} %pad_maximum_fusion), channel_id=1, source_target_pairs={{0,16},{1,49},{2,18},{3,51},{4,20},{5,53},{6,22},{7,55},{8,24},{9,... | collective-permute-start | bytes 1769480 | tf_op jit(solution)/shard_map/ppermute | solution.py:43
  23.9 10.6 %collective-permute-start.7 = (bf16[2,576,128]{2,1,0:T(8,128)(2,1)S(1)}, bf16[2,576,128]{2,1,0:T(8,128)(2,1)S(1)}, u32[]{:S(2)}, u32[]{:S(2)}) collective-permute-start(bf16[2,576,128]{2,1,0:T(8,128)(2,1)S(1)} %collective-permute-done.5.far), channel_id=1, source_target_pairs={{0,64},{1,65},{2,66},{3,67},{4,68},{5,69},{6,70},{7,71},{8,72},{9,... | collective-permute-start | bytes 884744 | tf_op jit(solution)/shard_map/ppermute | solution.py:43
  27.0 8.1 %collective-permute-start.6 = (bf16[2,576,128]{2,1,0:T(8,128)(2,1)S(1)}, bf16[2,576,128]{2,1,0:T(8,128)(2,1)S(1)}, u32[]{:S(2)}, u32[]{:S(2)}) collective-permute-start(bf16[2,576,128]{2,1,0:T(8,128)(2,1)S(1)} %collective-permute-done.5.far), channel_id=1, source_target_pairs={{0,1},{1,0},{2,3},{3,2},{4,5},{5,4},{6,7},{7,6},{8,9},{9,8},{10,11... | collective-permute-start | bytes 884744 | tf_op jit(solution)/shard_map/ppermute | solution.py:47
  34.3 2.5 %collective-permute-start.4 = (bf16[4,576,128]{2,1,0:T(8,128)(2,1)S(1)}, bf16[4,576,128]{2,1,0:T(8,128)(2,1)S(1)}, u32[]{:S(2)}, u32[]{:S(2)}) collective-permute-start(bf16[4,576,128]{2,1,0:T(8,128)(2,1)S(1)} %collective-permute-done.3.beside), channel_id=1, source_target_pairs={{0,1},{1,0},{2,3},{3,2},{4,5},{5,4},{6,7},{7,6},{8,9},{9,8},{10,11... | collective-permute-start | bytes 1769480 | tf_op jit(solution)/shard_map/ppermute | solution.py:47
  34.5 2.4 %collective-permute-start.9 = (bf16[2,576,128]{2,1,0:T(8,128)(2,1)S(1)}, bf16[2,576,128]{2,1,0:T(8,128)(2,1)S(1)}, u32[]{:S(2)}, u32[]{:S(2)}) collective-permute-start(bf16[2,576,128]{2,1,0:T(8,128)(2,1)S(1)} %fusion.15.side_far), channel_id=1, source_target_pairs={{0,1},{1,0},{2,3},{3,2},{4,5},{5,4},{6,7},{7,6},{8,9},{9,8},{10,11... | collective-permute-start | bytes 884744 | tf_op jit(solution)/shard_map/ppermute | solution.py:47
  42.8 2.6 %collective-permute-start.10 = (bf16[64,7168]{1,0:T(8,128)(2,1)S(1)}, bf16[64,7168]{1,0:T(8,128)(2,1)S(1)}, u32[]{:S(2)}, u32[]{:S(2)}) collective-permute-start(bf16[64,7168]{1,0:T(8,128)(2,1)S(1)} %get-tuple-element.44), channel_id=1, source_target_pairs={{0,1},{1,0},{2,3},{3,2},{4,5},{5,4},{6,7},{7,6},{8,9},{9,8},{10,11... | collective-permute-start | bytes 2752520 | tf_op jit(solution)/shard_map/ppermute | solution.py:47
  77.7 7.7 %collective-permute-start.11 = (bf16[32,7168]{1,0:T(8,128)(2,1)S(1)}, bf16[32,7168]{1,0:T(8,128)(2,1)S(1)}, u32[]{:S(2)}, u32[]{:S(2)}) collective-permute-start(bf16[32,7168]{1,0:T(8,128)(2,1)S(1)} %reshape.135.refs_0_), channel_id=1, source_target_pairs={{0,16},{1,49},{2,18},{3,51},{4,20},{5,53},{6,22},{7,55},{8,24},{9,... | collective-permute-start | bytes 1376264 | tf_op jit(solution)/shard_map/ppermute | solution.py:43
  77.8 12.3 %collective-permute-start.13 = (bf16[32,7168]{1,0:T(8,128)(2,1)S(1)}, bf16[32,7168]{1,0:T(8,128)(2,1)S(1)}, u32[]{:S(2)}, u32[]{:S(2)}) collective-permute-start(bf16[32,7168]{1,0:T(8,128)(2,1)S(1)} %reshape.135.refs_0_), channel_id=1, source_target_pairs={{0,64},{1,65},{2,66},{3,67},{4,68},{5,69},{6,70},{7,71},{8,72},{9,... | collective-permute-start | bytes 1376264 | tf_op jit(solution)/shard_map/ppermute | solution.py:43
  85.4 8.6 %collective-permute-start.15 = (bf16[32,7168]{1,0:T(8,128)(2,1)S(1)}, bf16[32,7168]{1,0:T(8,128)(2,1)S(1)}, u32[]{:S(2)}, u32[]{:S(2)}) collective-permute-start(bf16[32,7168]{1,0:T(8,128)(2,1)S(1)} %collective-permute-done.11.refs_1_), channel_id=1, source_target_pairs={{0,16},{1,49},{2,18},{3,51},{4,20},{5,53},{6,22},{7,55},{8,24},{9,... | collective-permute-start | bytes 1376264 | tf_op jit(solution)/shard_map/ppermute | solution.py:43
  86.3 10.8 %collective-permute-start.12 = (bf16[32,7168]{1,0:T(8,128)(2,1)S(1)}, bf16[32,7168]{1,0:T(8,128)(2,1)S(1)}, u32[]{:S(2)}, u32[]{:S(2)}) collective-permute-start(bf16[32,7168]{1,0:T(8,128)(2,1)S(1)} %reshape.135.refs_0_), channel_id=1, source_target_pairs={{0,48},{1,17},{2,50},{3,19},{4,52},{5,21},{6,54},{7,23},{8,56},{9,... | collective-permute-start | bytes 1376264 | tf_op jit(solution)/shard_map/ppermute | solution.py:43
  90.1 16.8 %collective-permute-start.17 = (bf16[32,7168]{1,0:T(8,128)(2,1)S(1)}, bf16[32,7168]{1,0:T(8,128)(2,1)S(1)}, u32[]{:S(2)}, u32[]{:S(2)}) collective-permute-start(bf16[32,7168]{1,0:T(8,128)(2,1)S(1)} %collective-permute-done.13.refs_3_), channel_id=1, source_target_pairs={{0,48},{1,17},{2,50},{3,19},{4,52},{5,21},{6,54},{7,23},{8,56},{9,... | collective-permute-start | bytes 1376264 | tf_op jit(solution)/shard_map/ppermute | solution.py:43
  91.1 15.8 %collective-permute-start.16 = (bf16[32,7168]{1,0:T(8,128)(2,1)S(1)}, bf16[32,7168]{1,0:T(8,128)(2,1)S(1)}, u32[]{:S(2)}, u32[]{:S(2)}) collective-permute-start(bf16[32,7168]{1,0:T(8,128)(2,1)S(1)} %collective-permute-done.13.refs_3_), channel_id=1, source_target_pairs={{0,16},{1,49},{2,18},{3,51},{4,20},{5,53},{6,22},{7,55},{8,24},{9,... | collective-permute-start | bytes 1376264 | tf_op jit(solution)/shard_map/ppermute | solution.py:43
  94.0 12.9 %collective-permute-start.18 = (bf16[32,7168]{1,0:T(8,128)(2,1)S(1)}, bf16[32,7168]{1,0:T(8,128)(2,1)S(1)}, u32[]{:S(2)}, u32[]{:S(2)}) collective-permute-start(bf16[32,7168]{1,0:T(8,128)(2,1)S(1)} %collective-permute-done.15.refs_0_), channel_id=1, source_target_pairs={{0,64},{1,65},{2,66},{3,67},{4,68},{5,69},{6,70},{7,71},{8,72},{9,... | collective-permute-start | bytes 1376264 | tf_op jit(solution)/shard_map/ppermute | solution.py:43
  108.7 11.5 %collective-permute-start.22 = (bf16[32,7168]{1,0:T(8,128)(2,1)S(1)}, bf16[32,7168]{1,0:T(8,128)(2,1)S(1)}, u32[]{:S(2)}, u32[]{:S(2)}) collective-permute-start(bf16[32,7168]{1,0:T(8,128)(2,1)S(1)} %get-tuple-element.57), channel_id=1, source_target_pairs={{0,64},{1,65},{2,66},{3,67},{4,68},{5,69},{6,70},{7,71},{8,72},{9,... | collective-permute-start | bytes 1376264 | tf_op jit(solution)/shard_map/ppermute | solution.py:43
  112.8 23.0 %collective-permute-start.14 = (bf16[32,7168]{1,0:T(8,128)(2,1)S(1)}, bf16[32,7168]{1,0:T(8,128)(2,1)S(1)}, u32[]{:S(2)}, u32[]{:S(2)}) collective-permute-start(bf16[32,7168]{1,0:T(8,128)(2,1)S(1)} %get-tuple-element.47), channel_id=1, source_target_pairs={{0,16},{1,49},{2,18},{3,51},{4,20},{5,53},{6,22},{7,55},{8,24},{9,... | collective-permute-start | bytes 1376264 | tf_op jit(solution)/shard_map/ppermute | solution.py:43
  112.8 10.6 %collective-permute-start.19 = (bf16[32,7168]{1,0:T(8,128)(2,1)S(1)}, bf16[32,7168]{1,0:T(8,128)(2,1)S(1)}, u32[]{:S(2)}, u32[]{:S(2)}) collective-permute-start(bf16[32,7168]{1,0:T(8,128)(2,1)S(1)} %get-tuple-element.53), channel_id=1, source_target_pairs={{0,48},{1,17},{2,50},{3,19},{4,52},{5,21},{6,54},{7,23},{8,56},{9,... | collective-permute-start | bytes 1376264 | tf_op jit(solution)/shard_map/ppermute | solution.py:43
  114.2 17.5 %collective-permute-start.20 = (bf16[32,7168]{1,0:T(8,128)(2,1)S(1)}, bf16[32,7168]{1,0:T(8,128)(2,1)S(1)}, u32[]{:S(2)}, u32[]{:S(2)}) collective-permute-start(bf16[32,7168]{1,0:T(8,128)(2,1)S(1)} %get-tuple-element.54), channel_id=1, source_target_pairs={{0,16},{1,49},{2,18},{3,51},{4,20},{5,53},{6,22},{7,55},{8,24},{9,... | collective-permute-start | bytes 1376264 | tf_op jit(solution)/shard_map/ppermute | solution.py:43
  120.4 13.9 %collective-permute-start.23 = (bf16[32,7168]{1,0:T(8,128)(2,1)S(1)}, bf16[32,7168]{1,0:T(8,128)(2,1)S(1)}, u32[]{:S(2)}, u32[]{:S(2)}) collective-permute-start(bf16[32,7168]{1,0:T(8,128)(2,1)S(1)} %add_convert_fusion.3), channel_id=1, source_target_pairs={{0,48},{1,17},{2,50},{3,19},{4,52},{5,21},{6,54},{7,23},{8,56},{9,... | collective-permute-start | bytes 1376264 | tf_op jit(solution)/shard_map/ppermute | solution.py:43
  131.8 8.9 %collective-permute-start.21 = (bf16[32,7168]{1,0:T(8,128)(2,1)S(1)}, bf16[32,7168]{1,0:T(8,128)(2,1)S(1)}, u32[]{:S(2)}, u32[]{:S(2)}) collective-permute-start(bf16[32,7168]{1,0:T(8,128)(2,1)S(1)} %add_convert_fusion.4), channel_id=1, source_target_pairs={{0,64},{1,65},{2,66},{3,67},{4,68},{5,69},{6,70},{7,71},{8,72},{9,... | collective-permute-start | bytes 1376264 | tf_op jit(solution)/shard_map/ppermute | solution.py:43
  134.3 8.9 %collective-permute-start.24 = (bf16[32,7168]{1,0:T(8,128)(2,1)S(1)}, bf16[32,7168]{1,0:T(8,128)(2,1)S(1)}, u32[]{:S(2)}, u32[]{:S(2)}) collective-permute-start(bf16[32,7168]{1,0:T(8,128)(2,1)S(1)} %add_convert_fusion.2), channel_id=1, source_target_pairs={{0,48},{1,17},{2,50},{3,19},{4,52},{5,21},{6,54},{7,23},{8,56},{9,... | collective-permute-start | bytes 1376264 | tf_op jit(solution)/shard_map/ppermute | solution.py:43
  (8 other events, 200.0 us)

commit v5 on v4

--- a/solution.py
+++ b/solution.py
@@ -34,6 +34,7 @@
 
 AHEAD = ctx_pairs(lambda y, z, way: (y, (z + way) % Z))
 BACK = ctx_pairs(lambda y, z, way: (y, (z - way) % Z))
+OPPOSITE = ctx_pairs(lambda y, z, way: (y, (z + 2) % Z))
 ACROSS = ctx_pairs(lambda y, z, way: (1 - y, z))
 CORE_SWAP = [(i, i ^ 1) for i in range(Y_LO * X * CORES)]
 SAME_CORE = [[2 * i + core for i in range(Y_LO * X)] for core in range(CORES)]
@@ -404,13 +405,12 @@
 
 
 def gather_rows(own):
+    far = over_ctx(own, OPPOSITE)
     side = over_ctx(own, ACROSS)
     ahead = over_ctx(own, AHEAD)
     back = over_ctx(own, BACK)
-    far = over_ctx(ahead, AHEAD)
-    side_now, _ = lax.optimization_barrier((side, ahead))
-    side_ahead = over_ctx(side_now, AHEAD)
-    side_back = over_ctx(side_now, BACK)
+    side_ahead = over_ctx(side, AHEAD)
+    side_back = over_ctx(side, BACK)
     side_far = over_ctx(far, ACROSS)
     return (ahead, back, side), (far, side_ahead, side_back, side_far)
 
@@ -428,11 +428,11 @@
     side_far_in = over_ctx(side_far, ACROSS)
     side_ahead_in = over_ctx(side_ahead, BACK)
     side_back_in = over_ctx(side_back, AHEAD)
-    far_in = over_ctx(added(far, side_far_in), BACK)
     side_in = over_ctx(added(side, side_ahead_in, side_back_in), ACROSS)
+    far_in = over_ctx(added(far, side_far_in), OPPOSITE)
+    ahead_in = over_ctx(ahead, BACK)
     back_in = over_ctx(back, AHEAD)
-    ahead_in = over_ctx(added(ahead, far_in), BACK)
-    return added(own, back_in, side_in, ahead_in)
+    return added(own, ahead_in, back_in, side_in, far_in)
 
 
 def on_device(

time: 161 us -> 161 us (level)
  starting transfers between devices: 32.1 us -> 34.7 us
  blocking collectives: 46.9 us -> 44.6 us
    ppermute x19, starting transfers between devices: 28.2 us -> 30.8 us  [over_ctx(): return lax.ppermute(value, ('ctx', 'exp'), pairs)]
    all_to_all x1, blocking collectives: 16 us -> 13.7 us  [on_device(): lax.all_to_all(summed.reshape(expert_count, capacity, model_width), 'exp'...]
  transfers between devices with their start and end apart: 25 -> 25, of which waited for: 15 -> 14; matrix products, arithmetic and copies ran while one was open for 2% -> 1% of each run, Pallas kernels for 5% -> 5%
where the time goes in v5:
time: 161 us
  waiting for transfers between devices  56.1 us (35%)
  blocking collectives  44.6 us (28%)
  starting transfers between devices  34.7 us (22%)
  Pallas kernels  16.3 us (10%)
  other arithmetic  4.72 us (3%)
  local copies, waits for them, and re-layouts  2.01 us (1%)
  between operations  1.67 us (1%)
    ppermute x19, waiting for transfers between devices, over_ctx(): return lax.ppermute(value, ('ctx', 'exp'), pairs)  52.1 us
    ppermute x19, starting transfers between devices, over_ctx(): return lax.ppermute(value, ('ctx', 'exp'), pairs)  30.8 us
    all_to_all x1, blocking collectives, on_device(): lax.all_to_all(paired.reshape(groups, 8, model_width), 'exp', split_axis=...  18.2 us
    all_to_all x1, blocking collectives, on_device(): lax.all_to_all(summed.reshape(expert_count, capacity, model_width), 'exp'...  13.7 us
    all_to_all x1, blocking collectives, on_device(): lax.all_to_all(buffer.reshape(expert_count, capacity, model_width), 'exp'...  12.6 us
    pallas_call x2, Pallas kernels, experts_call(): pl.pallas_call(functools.partial(experts_kernel, len(blocks), holds), out...  6.69 us
    pallas_call x1, Pallas kernels, far_call(): pl.pallas_call(far_kernel, out_shape=(out, out), in_specs=[pl.BlockSpec(m...  5.9 us
    ppermute x6, waiting for transfers between devices, core_swap(): return lax.ppermute(value, 'exp', CORE_SWAP)  4.07 us
  transfers between devices with their start and end apart: 25, of which 14 were waited for; matrix products, arithmetic and copies ran while one was open for 1% of the time, Pallas kernels for 5%

profile of v5, /device:TPU:1, one launch (start us, length us, event | category | flops | bytes accessed | tf_op | source)
XLA Modules:
  0.0 160.7 jit_solution(1164373383759597983)
XLA Ops:
  2.8 4.7 %collective-permute-start.2 = (bf16[4,576,128]{2,1,0:T(8,128)(2,1)S(1)}, bf16[4,576,128]{2,1,0:T(8,128)(2,1)S(1)}, u32[]{:S(2)}, u32[]{:S(2)}) collective-permute-start(bf16[4,576,128]{2,1,0:T(8,128)(2,1)S(1)} %fusion.6.own), channel_id=1, source_target_pairs={{0,16},{1,49},{2,18},{3,51},{4,20},{5,53},{6,22},{7,55},{8,24},{9,... | collective-permute-start | bytes 1769480 | tf_op jit(solution)/shard_map/ppermute | solution.py:44
  7.4 3.0 %collective-permute-start = (bf16[2,576,128]{2,1,0:T(8,128)(2,1)S(1)}, bf16[2,576,128]{2,1,0:T(8,128)(2,1)S(1)}, u32[]{:S(2)}, u32[]{:S(2)}) collective-permute-start(bf16[2,576,128]{2,1,0:T(8,128)(2,1)S(1)} %constant_dynamic-slice_fusion.1), channel_id=1, source_target_pairs={{0,64},{1,65},{2,66},{3,67},{4,68},{5,69},{6,70},{7,71},{8,72},{9,... | collective-permute-start | bytes 884744 | tf_op jit(solution)/shard_map/ppermute | solution.py:44
  11.0 6.0 %collective-permute-done.side = bf16[2,576,128]{2,1,0:T(8,128)(2,1)S(1)} collective-permute-done((bf16[2,576,128]{2,1,0:T(8,128)(2,1)S(1)}, bf16[2,576,128]{2,1,0:T(8,128)(2,1)S(1)}, u32[]{:S(2)}, u32[]{:S(2)}) %collective-permute-start) | collective-permute-done | bytes 294944 | tf_op jit(solution)/shard_map/ppermute | solution.py:44
  19.9 4.0 %collective-permute-done.5.far = bf16[2,576,128]{2,1,0:T(8,128)(2,1)S(1)} collective-permute-done((bf16[2,576,128]{2,1,0:T(8,128)(2,1)S(1)}, bf16[2,576,128]{2,1,0:T(8,128)(2,1)S(1)}, u32[]{:S(2)}, u32[]{:S(2)}) %collective-permute-start.5) | collective-permute-done | bytes 294944 | tf_op jit(solution)/shard_map/ppermute | solution.py:44
  23.9 2.9 %collective-permute-start.7 = (bf16[2,576,128]{2,1,0:T(8,128)(2,1)S(1)}, bf16[2,576,128]{2,1,0:T(8,128)(2,1)S(1)}, u32[]{:S(2)}, u32[]{:S(2)}) collective-permute-start(bf16[2,576,128]{2,1,0:T(8,128)(2,1)S(1)} %collective-permute-done.5.far), channel_id=1, source_target_pairs={{0,64},{1,65},{2,66},{3,67},{4,68},{5,69},{6,70},{7,71},{8,72},{9,... | collective-permute-start | bytes 884744 | tf_op jit(solution)/shard_map/ppermute | solution.py:44
  27.0 2.5 %collective-permute-start.6 = (bf16[2,576,128]{2,1,0:T(8,128)(2,1)S(1)}, bf16[2,576,128]{2,1,0:T(8,128)(2,1)S(1)}, u32[]{:S(2)}, u32[]{:S(2)}) collective-permute-start(bf16[2,576,128]{2,1,0:T(8,128)(2,1)S(1)} %collective-permute-done.5.far), channel_id=1, source_target_pairs={{0,1},{1,0},{2,3},{3,2},{4,5},{5,4},{6,7},{7,6},{8,9},{9,8},{10,11... | collective-permute-start | bytes 884744 | tf_op jit(solution)/shard_map/ppermute | solution.py:48
  29.5 3.7 %attention_near.1 = (f32[512,128]{1,0:T(8,128)S(1)}, f32[512,128]{1,0:T(8,128)S(1)}, f32[512,512]{1,0:T(8,128)S(1)}, bf16[512,7168]{1,0:T(8,128)(2,1)S(1)}, f32[8,128]{1,0:T(8,128)S(1)}) custom-call(s32[8,32]{1,0:T(8,128)S(1)} %copy-done.2, bf16[512,576]{1,0:T(8,128)(2,1)S(1)} %bitcast.42, bf16[4,576,128]{2,1,0:T(8,128)(2,1)S(1)} %fusion.6.own, ...), custom_call_target="tpu_custom_call" | custom-call | flops 3000000000 | bytes 12000000 | tf_op jit(solution)/shard_map/attention_near/pallas_call | solution.py:241
  36.9 5.9 %attention_far.1 = (bf16[64,7168]{1,0:T(8,128)(2,1)S(1)}, bf16[64,7168]{1,0:T(8,128)(2,1)S(1)}) custom-call(s32[8,32]{1,0:T(8,128)S(1)} %copy-done.2, bf16[512,576]{1,0:T(8,128)(2,1)S(1)} %bitcast.43, bf16[4,576,128]{2,1,0:T(8,128)(2,1)S(1)} %collective-permute-done.3.beside, bf16[4,576,128]{2,1,0:T(8,128)(2,1)S(1)} %collective-permute-done.4.beside_other, ...), custom_call_target="tpu_custom_call" | custom-call | flops 4000000000 | bytes 14000000 | tf_op jit(solution)/shard_map/attention_far/pallas_call | solution.py:271
  45.5 18.2 %all_to_all.15 = bf16[8,8,7168]{2,1,0:T(8,128)(2,1)S(1)} all-to-all(bf16[8,8,7168]{2,1,0:T(8,128)(2,1)S(1)} %fusion.5), channel_id=1, replica_groups={{0,2,4,6,8,10,12,14},{1,3,5,7,9,11,13,15},{16,18,20,22,24,26,28,30},{17..., dimensions={0} | all-to-all | bytes 1835008 | tf_op jit(solution)/shard_map/all_to_all | solution.py:492
  64.9 12.6 %all_to_all.16 = bf16[16,2,7168]{2,1,0:T(2,128)(2,1)S(1)} all-to-all(bf16[16,2,7168]{2,1,0:T(2,128)(2,1)S(1)} %reshape.134), channel_id=1, replica_groups=mesh['ctx'=8,'exp'=16] {'exp'}, dimensions={0} | all-to-all | bytes 917504 | tf_op jit(solution)/shard_map/all_to_all | solution.py:514
  80.0 2.4 %collective-permute-start.11 = (bf16[32,7168]{1,0:T(8,128)(2,1)S(1)}, bf16[32,7168]{1,0:T(8,128)(2,1)S(1)}, u32[]{:S(2)}, u32[]{:S(2)}) collective-permute-start(bf16[32,7168]{1,0:T(8,128)(2,1)S(1)} %reshape.135.refs_0_), channel_id=1, source_target_pairs={{0,16},{1,49},{2,18},{3,51},{4,20},{5,53},{6,22},{7,55},{8,24},{9,... | collective-permute-start | bytes 1376264 | tf_op jit(solution)/shard_map/ppermute | solution.py:44
  82.4 7.6 %collective-permute-done.16.refs_0_ = bf16[32,7168]{1,0:T(8,128)(2,1)S(1)} collective-permute-done((bf16[32,7168]{1,0:T(8,128)(2,1)S(1)}, bf16[32,7168]{1,0:T(8,128)(2,1)S(1)}, u32[]{:S(2)}, u32[]{:S(2)}) %collective-permute-start.16) | collective-permute-done | bytes 458784 | tf_op jit(solution)/shard_map/ppermute | solution.py:44
  91.8 2.7 %collective-permute-start.17 = (bf16[32,7168]{1,0:T(8,128)(2,1)S(1)}, bf16[32,7168]{1,0:T(8,128)(2,1)S(1)}, u32[]{:S(2)}, u32[]{:S(2)}) collective-permute-start(bf16[32,7168]{1,0:T(8,128)(2,1)S(1)} %collective-permute-done.13.refs_3_), channel_id=1, source_target_pairs={{0,16},{1,49},{2,18},{3,51},{4,20},{5,53},{6,22},{7,55},{8,24},{9,... | collective-permute-start | bytes 1376264 | tf_op jit(solution)/shard_map/ppermute | solution.py:44
  94.5 7.0 %collective-permute-done.12.refs_2_ = bf16[32,7168]{1,0:T(8,128)(2,1)S(1)} collective-permute-done((bf16[32,7168]{1,0:T(8,128)(2,1)S(1)}, bf16[32,7168]{1,0:T(8,128)(2,1)S(1)}, u32[]{:S(2)}, u32[]{:S(2)}) %collective-permute-start.12) | collective-permute-done | bytes 458784 | tf_op jit(solution)/shard_map/ppermute | solution.py:44
  101.6 4.9 %experts_near.1 = (bf16[32,7168]{1,0:T(8,128)(2,1)S(1)}, bf16[32,7168]{1,0:T(8,128)(2,1)S(1)}, bf16[32,7168]{1,0:T(8,128)(2,1)S(1)}, bf16[32,7168]{1,0:T(8,128)(...) custom-call(bf16[32,7168]{1,0:T(8,128)(2,1)S(1)} %reshape.135.refs_0_, ...), custom_call_target="tpu_custom_call" | custom-call | flops 1500000000 | bytes 15000000 | tf_op jit(solution)/shard_map/experts_near/pallas_call | solution.py:392
  106.5 4.9 %collective-permute-done.18.refs_2_ = bf16[32,7168]{1,0:T(8,128)(2,1)S(1)} collective-permute-done((bf16[32,7168]{1,0:T(8,128)(2,1)S(1)}, bf16[32,7168]{1,0:T(8,128)(2,1)S(1)}, u32[]{:S(2)}, u32[]{:S(2)}) %collective-permute-start.18) | collective-permute-done | bytes 458784 | tf_op jit(solution)/shard_map/ppermute | solution.py:44
  113.3 2.7 %collective-permute-start.21 = (bf16[32,7168]{1,0:T(8,128)(2,1)S(1)}, bf16[32,7168]{1,0:T(8,128)(2,1)S(1)}, u32[]{:S(2)}, u32[]{:S(2)}) collective-permute-start(bf16[32,7168]{1,0:T(8,128)(2,1)S(1)} %get-tuple-element.53), channel_id=1, source_target_pairs={{0,16},{1,49},{2,18},{3,51},{4,20},{5,53},{6,22},{7,55},{8,24},{9,... | collective-permute-start | bytes 1376264 | tf_op jit(solution)/shard_map/ppermute | solution.py:44
  116.0 2.7 %collective-permute-start.15 = (bf16[32,7168]{1,0:T(8,128)(2,1)S(1)}, bf16[32,7168]{1,0:T(8,128)(2,1)S(1)}, u32[]{:S(2)}, u32[]{:S(2)}) collective-permute-start(bf16[32,7168]{1,0:T(8,128)(2,1)S(1)} %get-tuple-element.47), channel_id=1, source_target_pairs={{0,16},{1,49},{2,18},{3,51},{4,20},{5,53},{6,22},{7,55},{8,24},{9,... | collective-permute-start | bytes 1376264 | tf_op jit(solution)/shard_map/ppermute | solution.py:44
  120.5 5.0 %collective-permute-done.20 = bf16[32,7168]{1,0:T(8,128)(2,1)S(1)} collective-permute-done((bf16[32,7168]{1,0:T(8,128)(2,1)S(1)}, bf16[32,7168]{1,0:T(8,128)(2,1)S(1)}, u32[]{:S(2)}, u32[]{:S(2)}) %collective-permute-start.20) | collective-permute-done | bytes 458784 | tf_op jit(solution)/shard_map/ppermute | solution.py:44
  128.4 3.6 %collective-permute-done.23 = bf16[32,7168]{1,0:T(8,128)(2,1)S(1)} collective-permute-done((bf16[32,7168]{1,0:T(8,128)(2,1)S(1)}, bf16[32,7168]{1,0:T(8,128)(2,1)S(1)}, u32[]{:S(2)}, u32[]{:S(2)}) %collective-permute-start.23) | collective-permute-done | bytes 458784 | tf_op jit(solution)/shard_map/ppermute | solution.py:44
  132.7 2.5 %collective-permute-done.14 = bf16[32,7168]{1,0:T(8,128)(2,1)S(1)} collective-permute-done((bf16[32,7168]{1,0:T(8,128)(2,1)S(1)}, bf16[32,7168]{1,0:T(8,128)(2,1)S(1)}, u32[]{:S(2)}, u32[]{:S(2)}) %collective-permute-start.14) | collective-permute-done | bytes 458784 | tf_op jit(solution)/shard_map/ppermute | solution.py:44
  135.4 5.0 %collective-permute-done.22 = bf16[32,7168]{1,0:T(8,128)(2,1)S(1)} collective-permute-done((bf16[32,7168]{1,0:T(8,128)(2,1)S(1)}, bf16[32,7168]{1,0:T(8,128)(2,1)S(1)}, u32[]{:S(2)}, u32[]{:S(2)}) %collective-permute-start.22) | collective-permute-done | bytes 458784 | tf_op jit(solution)/shard_map/ppermute | solution.py:44
  140.5 5.1 %collective-permute-done.24 = bf16[32,7168]{1,0:T(8,128)(2,1)S(1)} collective-permute-done((bf16[32,7168]{1,0:T(8,128)(2,1)S(1)}, bf16[32,7168]{1,0:T(8,128)(2,1)S(1)}, u32[]{:S(2)}, u32[]{:S(2)}) %collective-permute-start.24) | collective-permute-done | bytes 458784 | tf_op jit(solution)/shard_map/ppermute | solution.py:44
  146.0 13.7 %all_to_all.17 = bf16[16,2,7168]{2,1,0:T(2,128)(2,1)S(1)} all-to-all(bf16[16,2,7168]{2,1,0:T(2,128)(2,1)S(1)} %reshape.136), channel_id=1, replica_groups=mesh['ctx'=8,'exp'=16] {'exp'}, dimensions={0} | all-to-all | bytes 917504 | tf_op jit(solution)/shard_map/all_to_all | solution.py:529
  (88 shorter events, 25.7 us)
Async XLA Ops:
  2.8 14.6 %collective-permute-start.2 = (bf16[4,576,128]{2,1,0:T(8,128)(2,1)S(1)}, bf16[4,576,128]{2,1,0:T(8,128)(2,1)S(1)}, u32[]{:S(2)}, u32[]{:S(2)}) collective-permute-start(bf16[4,576,128]{2,1,0:T(8,128)(2,1)S(1)} %fusion.6.own), channel_id=1, source_target_pairs={{0,16},{1,49},{2,18},{3,51},{4,20},{5,53},{6,22},{7,55},{8,24},{9,... | collective-permute-start | bytes 1769480 | tf_op jit(solution)/shard_map/ppermute | solution.py:44
  7.4 9.6 %collective-permute-start = (bf16[2,576,128]{2,1,0:T(8,128)(2,1)S(1)}, bf16[2,576,128]{2,1,0:T(8,128)(2,1)S(1)}, u32[]{:S(2)}, u32[]{:S(2)}) collective-permute-start(bf16[2,576,128]{2,1,0:T(8,128)(2,1)S(1)} %constant_dynamic-slice_fusion.1), channel_id=1, source_target_pairs={{0,64},{1,65},{2,66},{3,67},{4,68},{5,69},{6,70},{7,71},{8,72},{9,... | collective-permute-start | bytes 884744 | tf_op jit(solution)/shard_map/ppermute | solution.py:44
  17.4 12.1 %collective-permute-start.8 = (bf16[4,576,128]{2,1,0:T(8,128)(2,1)S(1)}, bf16[4,576,128]{2,1,0:T(8,128)(2,1)S(1)}, u32[]{:S(2)}, u32[]{:S(2)}) collective-permute-start(bf16[4,576,128]{2,1,0:T(8,128)(2,1)S(1)} %collective-permute-done.2.beside), channel_id=1, source_target_pairs={{0,1},{1,0},{2,3},{3,2},{4,5},{5,4},{6,7},{7,6},{8,9},{9,8},{10,11... | collective-permute-start | bytes 1769480 | tf_op jit(solution)/shard_map/ppermute | solution.py:48
  18.0 5.9 %collective-permute-start.5 = (bf16[2,576,128]{2,1,0:T(8,128)(2,1)S(1)}, bf16[2,576,128]{2,1,0:T(8,128)(2,1)S(1)}, u32[]{:S(2)}, u32[]{:S(2)}) collective-permute-start(bf16[2,576,128]{2,1,0:T(8,128)(2,1)S(1)} %constant_dynamic-slice_fusion), channel_id=1, source_target_pairs={{0,16},{1,49},{2,18},{3,51},{4,20},{5,53},{6,22},{7,55},{8,24},{9,... | collective-permute-start | bytes 884744 | tf_op jit(solution)/shard_map/ppermute | solution.py:44
  19.1 15.2 %collective-permute-start.3 = (bf16[4,576,128]{2,1,0:T(8,128)(2,1)S(1)}, bf16[4,576,128]{2,1,0:T(8,128)(2,1)S(1)}, u32[]{:S(2)}, u32[]{:S(2)}) collective-permute-start(bf16[4,576,128]{2,1,0:T(8,128)(2,1)S(1)} %pad_maximum_fusion), channel_id=1, source_target_pairs={{0,16},{1,49},{2,18},{3,51},{4,20},{5,53},{6,22},{7,55},{8,24},{9,... | collective-permute-start | bytes 1769480 | tf_op jit(solution)/shard_map/ppermute | solution.py:44
  23.9 10.6 %collective-permute-start.7 = (bf16[2,576,128]{2,1,0:T(8,128)(2,1)S(1)}, bf16[2,576,128]{2,1,0:T(8,128)(2,1)S(1)}, u32[]{:S(2)}, u32[]{:S(2)}) collective-permute-start(bf16[2,576,128]{2,1,0:T(8,128)(2,1)S(1)} %collective-permute-done.5.far), channel_id=1, source_target_pairs={{0,64},{1,65},{2,66},{3,67},{4,68},{5,69},{6,70},{7,71},{8,72},{9,... | collective-permute-start | bytes 884744 | tf_op jit(solution)/shard_map/ppermute | solution.py:44
  27.0 8.1 %collective-permute-start.6 = (bf16[2,576,128]{2,1,0:T(8,128)(2,1)S(1)}, bf16[2,576,128]{2,1,0:T(8,128)(2,1)S(1)}, u32[]{:S(2)}, u32[]{:S(2)}) collective-permute-start(bf16[2,576,128]{2,1,0:T(8,128)(2,1)S(1)} %collective-permute-done.5.far), channel_id=1, source_target_pairs={{0,1},{1,0},{2,3},{3,2},{4,5},{5,4},{6,7},{7,6},{8,9},{9,8},{10,11... | collective-permute-start | bytes 884744 | tf_op jit(solution)/shard_map/ppermute | solution.py:48
  34.3 2.5 %collective-permute-start.4 = (bf16[4,576,128]{2,1,0:T(8,128)(2,1)S(1)}, bf16[4,576,128]{2,1,0:T(8,128)(2,1)S(1)}, u32[]{:S(2)}, u32[]{:S(2)}) collective-permute-start(bf16[4,576,128]{2,1,0:T(8,128)(2,1)S(1)} %collective-permute-done.3.beside), channel_id=1, source_target_pairs={{0,1},{1,0},{2,3},{3,2},{4,5},{5,4},{6,7},{7,6},{8,9},{9,8},{10,11... | collective-permute-start | bytes 1769480 | tf_op jit(solution)/shard_map/ppermute | solution.py:48
  34.5 2.4 %collective-permute-start.9 = (bf16[2,576,128]{2,1,0:T(8,128)(2,1)S(1)}, bf16[2,576,128]{2,1,0:T(8,128)(2,1)S(1)}, u32[]{:S(2)}, u32[]{:S(2)}) collective-permute-start(bf16[2,576,128]{2,1,0:T(8,128)(2,1)S(1)} %fusion.15.side_far), channel_id=1, source_target_pairs={{0,1},{1,0},{2,3},{3,2},{4,5},{5,4},{6,7},{7,6},{8,9},{9,8},{10,11... | collective-permute-start | bytes 884744 | tf_op jit(solution)/shard_map/ppermute | solution.py:48
  42.8 2.6 %collective-permute-start.10 = (bf16[64,7168]{1,0:T(8,128)(2,1)S(1)}, bf16[64,7168]{1,0:T(8,128)(2,1)S(1)}, u32[]{:S(2)}, u32[]{:S(2)}) collective-permute-start(bf16[64,7168]{1,0:T(8,128)(2,1)S(1)} %get-tuple-element.43), channel_id=1, source_target_pairs={{0,1},{1,0},{2,3},{3,2},{4,5},{5,4},{6,7},{7,6},{8,9},{9,8},{10,11... | collective-permute-start | bytes 2752520 | tf_op jit(solution)/shard_map/ppermute | solution.py:48
  77.7 12.3 %collective-permute-start.16 = (bf16[32,7168]{1,0:T(8,128)(2,1)S(1)}, bf16[32,7168]{1,0:T(8,128)(2,1)S(1)}, u32[]{:S(2)}, u32[]{:S(2)}) collective-permute-start(bf16[32,7168]{1,0:T(8,128)(2,1)S(1)} %reshape.135.refs_0_), channel_id=1, source_target_pairs={{0,32},{1,33},{2,34},{3,35},{4,36},{5,37},{6,38},{7,39},{8,40},{9,... | collective-permute-start | bytes 1376264 | tf_op jit(solution)/shard_map/ppermute | solution.py:44
  77.8 14.0 %collective-permute-start.13 = (bf16[32,7168]{1,0:T(8,128)(2,1)S(1)}, bf16[32,7168]{1,0:T(8,128)(2,1)S(1)}, u32[]{:S(2)}, u32[]{:S(2)}) collective-permute-start(bf16[32,7168]{1,0:T(8,128)(2,1)S(1)} %reshape.135.refs_0_), channel_id=1, source_target_pairs={{0,64},{1,65},{2,66},{3,67},{4,68},{5,69},{6,70},{7,71},{8,72},{9,... | collective-permute-start | bytes 1376264 | tf_op jit(solution)/shard_map/ppermute | solution.py:44
  79.7 21.9 %collective-permute-start.12 = (bf16[32,7168]{1,0:T(8,128)(2,1)S(1)}, bf16[32,7168]{1,0:T(8,128)(2,1)S(1)}, u32[]{:S(2)}, u32[]{:S(2)}) collective-permute-start(bf16[32,7168]{1,0:T(8,128)(2,1)S(1)} %reshape.135.refs_0_), channel_id=1, source_target_pairs={{0,48},{1,17},{2,50},{3,19},{4,52},{5,21},{6,54},{7,23},{8,56},{9,... | collective-permute-start | bytes 1376264 | tf_op jit(solution)/shard_map/ppermute | solution.py:44
  80.0 21.6 %collective-permute-start.11 = (bf16[32,7168]{1,0:T(8,128)(2,1)S(1)}, bf16[32,7168]{1,0:T(8,128)(2,1)S(1)}, u32[]{:S(2)}, u32[]{:S(2)}) collective-permute-start(bf16[32,7168]{1,0:T(8,128)(2,1)S(1)} %reshape.135.refs_0_), channel_id=1, source_target_pairs={{0,16},{1,49},{2,18},{3,51},{4,20},{5,53},{6,22},{7,55},{8,24},{9,... | collective-permute-start | bytes 1376264 | tf_op jit(solution)/shard_map/ppermute | solution.py:44
  90.0 16.4 %collective-permute-start.19 = (bf16[32,7168]{1,0:T(8,128)(2,1)S(1)}, bf16[32,7168]{1,0:T(8,128)(2,1)S(1)}, u32[]{:S(2)}, u32[]{:S(2)}) collective-permute-start(bf16[32,7168]{1,0:T(8,128)(2,1)S(1)} %collective-permute-done.16.refs_0_), channel_id=1, source_target_pairs={{0,64},{1,65},{2,66},{3,67},{4,68},{5,69},{6,70},{7,71},{8,72},{9,... | collective-permute-start | bytes 1376264 | tf_op jit(solution)/shard_map/ppermute | solution.py:44
  91.8 19.6 %collective-permute-start.18 = (bf16[32,7168]{1,0:T(8,128)(2,1)S(1)}, bf16[32,7168]{1,0:T(8,128)(2,1)S(1)}, u32[]{:S(2)}, u32[]{:S(2)}) collective-permute-start(bf16[32,7168]{1,0:T(8,128)(2,1)S(1)} %collective-permute-done.13.refs_3_), channel_id=1, source_target_pairs={{0,48},{1,17},{2,50},{3,19},{4,52},{5,21},{6,54},{7,23},{8,56},{9,... | collective-permute-start | bytes 1376264 | tf_op jit(solution)/shard_map/ppermute | solution.py:44
  91.8 19.6 %collective-permute-start.17 = (bf16[32,7168]{1,0:T(8,128)(2,1)S(1)}, bf16[32,7168]{1,0:T(8,128)(2,1)S(1)}, u32[]{:S(2)}, u32[]{:S(2)}) collective-permute-start(bf16[32,7168]{1,0:T(8,128)(2,1)S(1)} %collective-permute-done.13.refs_3_), channel_id=1, source_target_pairs={{0,16},{1,49},{2,18},{3,51},{4,20},{5,53},{6,22},{7,55},{8,24},{9,... | collective-permute-start | bytes 1376264 | tf_op jit(solution)/shard_map/ppermute | solution.py:44
  113.2 12.2 %collective-permute-start.20 = (bf16[32,7168]{1,0:T(8,128)(2,1)S(1)}, bf16[32,7168]{1,0:T(8,128)(2,1)S(1)}, u32[]{:S(2)}, u32[]{:S(2)}) collective-permute-start(bf16[32,7168]{1,0:T(8,128)(2,1)S(1)} %get-tuple-element.52), channel_id=1, source_target_pairs={{0,48},{1,17},{2,50},{3,19},{4,52},{5,21},{6,54},{7,23},{8,56},{9,... | collective-permute-start | bytes 1376264 | tf_op jit(solution)/shard_map/ppermute | solution.py:44
  113.3 13.1 %collective-permute-start.21 = (bf16[32,7168]{1,0:T(8,128)(2,1)S(1)}, bf16[32,7168]{1,0:T(8,128)(2,1)S(1)}, u32[]{:S(2)}, u32[]{:S(2)}) collective-permute-start(bf16[32,7168]{1,0:T(8,128)(2,1)S(1)} %get-tuple-element.53), channel_id=1, source_target_pairs={{0,16},{1,49},{2,18},{3,51},{4,20},{5,53},{6,22},{7,55},{8,24},{9,... | collective-permute-start | bytes 1376264 | tf_op jit(solution)/shard_map/ppermute | solution.py:44
  116.0 19.3 %collective-permute-start.14 = (bf16[32,7168]{1,0:T(8,128)(2,1)S(1)}, bf16[32,7168]{1,0:T(8,128)(2,1)S(1)}, u32[]{:S(2)}, u32[]{:S(2)}) collective-permute-start(bf16[32,7168]{1,0:T(8,128)(2,1)S(1)} %get-tuple-element.46), channel_id=1, source_target_pairs={{0,48},{1,17},{2,50},{3,19},{4,52},{5,21},{6,54},{7,23},{8,56},{9,... | collective-permute-start | bytes 1376264 | tf_op jit(solution)/shard_map/ppermute | solution.py:44
  116.0 19.5 %collective-permute-start.15 = (bf16[32,7168]{1,0:T(8,128)(2,1)S(1)}, bf16[32,7168]{1,0:T(8,128)(2,1)S(1)}, u32[]{:S(2)}, u32[]{:S(2)}) collective-permute-start(bf16[32,7168]{1,0:T(8,128)(2,1)S(1)} %get-tuple-element.47), channel_id=1, source_target_pairs={{0,16},{1,49},{2,18},{3,51},{4,20},{5,53},{6,22},{7,55},{8,24},{9,... | collective-permute-start | bytes 1376264 | tf_op jit(solution)/shard_map/ppermute | solution.py:44
  118.6 13.4 %collective-permute-start.23 = (bf16[32,7168]{1,0:T(8,128)(2,1)S(1)}, bf16[32,7168]{1,0:T(8,128)(2,1)S(1)}, u32[]{:S(2)}, u32[]{:S(2)}) collective-permute-start(bf16[32,7168]{1,0:T(8,128)(2,1)S(1)} %get-tuple-element.55), channel_id=1, source_target_pairs={{0,64},{1,65},{2,66},{3,67},{4,68},{5,69},{6,70},{7,71},{8,72},{9,... | collective-permute-start | bytes 1376264 | tf_op jit(solution)/shard_map/ppermute | solution.py:44
  126.5 13.9 %collective-permute-start.22 = (bf16[32,7168]{1,0:T(8,128)(2,1)S(1)}, bf16[32,7168]{1,0:T(8,128)(2,1)S(1)}, u32[]{:S(2)}, u32[]{:S(2)}) collective-permute-start(bf16[32,7168]{1,0:T(8,128)(2,1)S(1)} %add_convert_fusion.3), channel_id=1, source_target_pairs={{0,64},{1,65},{2,66},{3,67},{4,68},{5,69},{6,70},{7,71},{8,72},{9,... | collective-permute-start | bytes 1376264 | tf_op jit(solution)/shard_map/ppermute | solution.py:44
  132.2 13.3 %collective-permute-start.24 = (bf16[32,7168]{1,0:T(8,128)(2,1)S(1)}, bf16[32,7168]{1,0:T(8,128)(2,1)S(1)}, u32[]{:S(2)}, u32[]{:S(2)}) collective-permute-start(bf16[32,7168]{1,0:T(8,128)(2,1)S(1)} %add_convert_fusion.2), channel_id=1, source_target_pairs={{0,32},{1,33},{2,34},{3,35},{4,36},{5,37},{6,38},{7,39},{8,40},{9,... | collective-permute-start | bytes 1376264 | tf_op jit(solution)/shard_map/ppermute | solution.py:44
  (8 other events, 197.0 us)

commit v6 on v5

--- a/solution.py
+++ b/solution.py
@@ -61,9 +61,6 @@
     latent_width = mixture.shape[1]
     block = top.shape[1]
     factor = 1.4426950408889634 / (NOPE + ROPE) ** 0.5
-    top[...] = jnp.full_like(top, -1e30)
-    total[...] = jnp.zeros_like(total)
-    mixture[...] = jnp.zeros_like(mixture)
 
     def keys_of(step, height):
         return jnp.concatenate([part[i, :height] for part, i, _ in step], axis=1)
@@ -93,7 +90,7 @@
     live = [(sum(flags) > 0).astype(jnp.int32) for flags in all_flags]
     straight = sum(live) >= len(steps) - 1
 
-    def score(step, number):
+    def score(step, number, first):
         found = jnp.dot(
             queries[...], keys_of(step, queries.shape[1]), preferred_element_type=F32
         )
@@ -107,7 +104,8 @@
             seen = jnp.where(causal(), found[:, last:], -1e30)
             found = jnp.concatenate([found[:, :last], seen], axis=1)
         scores[number] = found
-        top[...] = jnp.maximum(top[...], lane_fold(found, jnp.maximum))
+        found_top = lane_fold(found, jnp.maximum)
+        top[...] = found_top if first else jnp.maximum(top[...], found_top)
 
     def causal():
         tokens = rows // HEADS_HERE
@@ -118,23 +116,30 @@
         token = within // 8 * 16 + side * 8 + within % 8
         return lax.broadcasted_iota(jnp.int32, (1, block), 1) <= token
 
-    def mix(row_top, step, number):
+    def mix(row_top, step, number, first):
         weights = jnp.exp2((scores[number] - row_top) * factor)
-        total[...] += lane_fold(weights, jnp.add)
-        mixture[...] += lax.dot_general(
+        found_total = lane_fold(weights, jnp.add)
+        found_mixture = lax.dot_general(
             weights.astype(BF16),
             keys_of(step, latent_width),
             (((1,), (1,)), ((), ())),
             preferred_element_type=F32,
         )
+        total[...] = found_total if first else total[...] + found_total
+        mixture[...] = found_mixture if first else mixture[...] + found_mixture
 
     def all_steps(branches):
+        if branches:
+            top[...] = jnp.full_like(top, -1e30)
+            total[...] = jnp.zeros_like(total)
+            mixture[...] = jnp.zeros_like(mixture)
+
         def each_step(body):
             for number, step in enumerate(steps):
                 if branches:
-                    pl.when(live[number] > 0)(functools.partial(body, step, number))
+                    pl.when(live[number] > 0)(functools.partial(body, step, number, False))
                 else:
-                    body(step, number)
+                    body(step, number, number == 0)
 
         each_step(score)
         row_top = jnp.max(top[...], axis=1, keepdims=True)

time: 161 us -> 161 us (level)
  starting transfers between devices: 34.7 us -> 27.8 us
  waiting for transfers between devices: 56.1 us -> 63 us
    ppermute x19, waiting for transfers between devices: 52.1 us -> 58.9 us  [over_ctx(): return lax.ppermute(value, ('ctx', 'exp'), pairs)]
    ppermute x19, starting transfers between devices: 30.8 us -> 23.9 us  [over_ctx(): return lax.ppermute(value, ('ctx', 'exp'), pairs)]
where the time goes in v6:
time: 161 us
  waiting for transfers between devices  63 us (39%)
  blocking collectives  44.2 us (27%)
  starting transfers between devices  27.8 us (17%)
  Pallas kernels  16.5 us (10%)
  other arithmetic  4.72 us (3%)
  local copies, waits for them, and re-layouts  2.01 us (1%)
  between operations  1.68 us (1%)
    ppermute x19, waiting for transfers between devices, over_ctx(): return lax.ppermute(value, ('ctx', 'exp'), pairs)  58.9 us
    ppermute x19, starting transfers between devices, over_ctx(): return lax.ppermute(value, ('ctx', 'exp'), pairs)  23.9 us
    all_to_all x1, blocking collectives, on_device(): lax.all_to_all(paired.reshape(groups, 8, model_width), 'exp', split_axis=...  18.2 us
    all_to_all x1, blocking collectives, on_device(): lax.all_to_all(summed.reshape(expert_count, capacity, model_width), 'exp'...  13.4 us
    all_to_all x1, blocking collectives, on_device(): lax.all_to_all(buffer.reshape(expert_count, capacity, model_width), 'exp'...  12.6 us
    pallas_call x2, Pallas kernels, experts_call(): pl.pallas_call(functools.partial(experts_kernel, len(blocks), holds), out...  6.68 us
    pallas_call x1, Pallas kernels, far_call(): pl.pallas_call(far_kernel, out_shape=(out, out), in_specs=[pl.BlockSpec(m...  5.89 us
    ppermute x6, waiting for transfers between devices, core_swap(): return lax.ppermute(value, 'exp', CORE_SWAP)  4.07 us
  transfers between devices with their start and end apart: 25, of which 14 were waited for; matrix products, arithmetic and copies ran while one was open for 1% of the time, Pallas kernels for 5%

profile of v6, /device:TPU:1, one launch (start us, length us, event | category | flops | bytes accessed | tf_op | source)
XLA Modules:
  0.0 160.6 jit_solution(7661418505275566913)
XLA Ops:
  2.8 4.7 %collective-permute-start.2 = (bf16[4,576,128]{2,1,0:T(8,128)(2,1)S(1)}, bf16[4,576,128]{2,1,0:T(8,128)(2,1)S(1)}, u32[]{:S(2)}, u32[]{:S(2)}) collective-permute-start(bf16[4,576,128]{2,1,0:T(8,128)(2,1)S(1)} %fusion.6.own), channel_id=1, source_target_pairs={{0,16},{1,49},{2,18},{3,51},{4,20},{5,53},{6,22},{7,55},{8,24},{9,... | collective-permute-start | bytes 1769480 | tf_op jit(solution)/shard_map/ppermute | solution.py:44
  7.4 3.0 %collective-permute-start = (bf16[2,576,128]{2,1,0:T(8,128)(2,1)S(1)}, bf16[2,576,128]{2,1,0:T(8,128)(2,1)S(1)}, u32[]{:S(2)}, u32[]{:S(2)}) collective-permute-start(bf16[2,576,128]{2,1,0:T(8,128)(2,1)S(1)} %constant_dynamic-slice_fusion.1), channel_id=1, source_target_pairs={{0,64},{1,65},{2,66},{3,67},{4,68},{5,69},{6,70},{7,71},{8,72},{9,... | collective-permute-start | bytes 884744 | tf_op jit(solution)/shard_map/ppermute | solution.py:44
  11.0 6.0 %collective-permute-done.side = bf16[2,576,128]{2,1,0:T(8,128)(2,1)S(1)} collective-permute-done((bf16[2,576,128]{2,1,0:T(8,128)(2,1)S(1)}, bf16[2,576,128]{2,1,0:T(8,128)(2,1)S(1)}, u32[]{:S(2)}, u32[]{:S(2)}) %collective-permute-start) | collective-permute-done | bytes 294944 | tf_op jit(solution)/shard_map/ppermute | solution.py:44
  19.9 4.0 %collective-permute-done.5.far = bf16[2,576,128]{2,1,0:T(8,128)(2,1)S(1)} collective-permute-done((bf16[2,576,128]{2,1,0:T(8,128)(2,1)S(1)}, bf16[2,576,128]{2,1,0:T(8,128)(2,1)S(1)}, u32[]{:S(2)}, u32[]{:S(2)}) %collective-permute-start.5) | collective-permute-done | bytes 294944 | tf_op jit(solution)/shard_map/ppermute | solution.py:44
  23.9 2.9 %collective-permute-start.7 = (bf16[2,576,128]{2,1,0:T(8,128)(2,1)S(1)}, bf16[2,576,128]{2,1,0:T(8,128)(2,1)S(1)}, u32[]{:S(2)}, u32[]{:S(2)}) collective-permute-start(bf16[2,576,128]{2,1,0:T(8,128)(2,1)S(1)} %collective-permute-done.5.far), channel_id=1, source_target_pairs={{0,64},{1,65},{2,66},{3,67},{4,68},{5,69},{6,70},{7,71},{8,72},{9,... | collective-permute-start | bytes 884744 | tf_op jit(solution)/shard_map/ppermute | solution.py:44
  27.0 2.5 %collective-permute-start.6 = (bf16[2,576,128]{2,1,0:T(8,128)(2,1)S(1)}, bf16[2,576,128]{2,1,0:T(8,128)(2,1)S(1)}, u32[]{:S(2)}, u32[]{:S(2)}) collective-permute-start(bf16[2,576,128]{2,1,0:T(8,128)(2,1)S(1)} %collective-permute-done.5.far), channel_id=1, source_target_pairs={{0,1},{1,0},{2,3},{3,2},{4,5},{5,4},{6,7},{7,6},{8,9},{9,8},{10,11... | collective-permute-start | bytes 884744 | tf_op jit(solution)/shard_map/ppermute | solution.py:48
  29.5 3.9 %attention_near.1 = (f32[512,128]{1,0:T(8,128)S(1)}, f32[512,128]{1,0:T(8,128)S(1)}, f32[512,512]{1,0:T(8,128)S(1)}, bf16[512,7168]{1,0:T(8,128)(2,1)S(1)}, f32[8,128]{1,0:T(8,128)S(1)}) custom-call(s32[8,32]{1,0:T(8,128)S(1)} %copy-done.2, bf16[512,576]{1,0:T(8,128)(2,1)S(1)} %bitcast.42, bf16[4,576,128]{2,1,0:T(8,128)(2,1)S(1)} %fusion.6.own, ...), custom_call_target="tpu_custom_call" | custom-call | flops 3000000000 | bytes 12000000 | tf_op jit(solution)/shard_map/attention_near/pallas_call | solution.py:246
  37.1 5.9 %attention_far.1 = (bf16[64,7168]{1,0:T(8,128)(2,1)S(1)}, bf16[64,7168]{1,0:T(8,128)(2,1)S(1)}) custom-call(s32[8,32]{1,0:T(8,128)S(1)} %copy-done.2, bf16[512,576]{1,0:T(8,128)(2,1)S(1)} %bitcast.43, bf16[4,576,128]{2,1,0:T(8,128)(2,1)S(1)} %collective-permute-done.3.beside, bf16[4,576,128]{2,1,0:T(8,128)(2,1)S(1)} %collective-permute-done.4.beside_other, ...), custom_call_target="tpu_custom_call" | custom-call | flops 4000000000 | bytes 14000000 | tf_op jit(solution)/shard_map/attention_far/pallas_call | solution.py:276
  43.2 2.3 %collective-permute-done.10 = bf16[64,7168]{1,0:T(8,128)(2,1)S(1)} collective-permute-done((bf16[64,7168]{1,0:T(8,128)(2,1)S(1)}, bf16[64,7168]{1,0:T(8,128)(2,1)S(1)}, u32[]{:S(2)}, u32[]{:S(2)}) %collective-permute-start.10) | collective-permute-done | bytes 917536 | tf_op jit(solution)/shard_map/ppermute | solution.py:48
  45.8 18.2 %all_to_all.15 = bf16[8,8,7168]{2,1,0:T(8,128)(2,1)S(1)} all-to-all(bf16[8,8,7168]{2,1,0:T(8,128)(2,1)S(1)} %fusion.5), channel_id=1, replica_groups={{0,2,4,6,8,10,12,14},{1,3,5,7,9,11,13,15},{16,18,20,22,24,26,28,30},{17..., dimensions={0} | all-to-all | bytes 1835008 | tf_op jit(solution)/shard_map/all_to_all | solution.py:497
  65.0 12.6 %all_to_all.16 = bf16[16,2,7168]{2,1,0:T(2,128)(2,1)S(1)} all-to-all(bf16[16,2,7168]{2,1,0:T(2,128)(2,1)S(1)} %reshape.134), channel_id=1, replica_groups=mesh['ctx'=8,'exp'=16] {'exp'}, dimensions={0} | all-to-all | bytes 917504 | tf_op jit(solution)/shard_map/all_to_all | solution.py:519
  81.0 9.1 %collective-permute-done.16.refs_0_ = bf16[32,7168]{1,0:T(8,128)(2,1)S(1)} collective-permute-done((bf16[32,7168]{1,0:T(8,128)(2,1)S(1)}, bf16[32,7168]{1,0:T(8,128)(2,1)S(1)}, u32[]{:S(2)}, u32[]{:S(2)}) %collective-permute-start.16) | collective-permute-done | bytes 458784 | tf_op jit(solution)/shard_map/ppermute | solution.py:44
  90.2 2.7 %collective-permute-start.17 = (bf16[32,7168]{1,0:T(8,128)(2,1)S(1)}, bf16[32,7168]{1,0:T(8,128)(2,1)S(1)}, u32[]{:S(2)}, u32[]{:S(2)}) collective-permute-start(bf16[32,7168]{1,0:T(8,128)(2,1)S(1)} %collective-permute-done.13.refs_3_), channel_id=1, source_target_pairs={{0,16},{1,49},{2,18},{3,51},{4,20},{5,53},{6,22},{7,55},{8,24},{9,... | collective-permute-start | bytes 1376264 | tf_op jit(solution)/shard_map/ppermute | solution.py:44
  92.8 8.8 %collective-permute-done.12.refs_2_ = bf16[32,7168]{1,0:T(8,128)(2,1)S(1)} collective-permute-done((bf16[32,7168]{1,0:T(8,128)(2,1)S(1)}, bf16[32,7168]{1,0:T(8,128)(2,1)S(1)}, u32[]{:S(2)}, u32[]{:S(2)}) %collective-permute-start.12) | collective-permute-done | bytes 458784 | tf_op jit(solution)/shard_map/ppermute | solution.py:44
  101.7 4.9 %experts_near.1 = (bf16[32,7168]{1,0:T(8,128)(2,1)S(1)}, bf16[32,7168]{1,0:T(8,128)(2,1)S(1)}, bf16[32,7168]{1,0:T(8,128)(2,1)S(1)}, bf16[32,7168]{1,0:T(8,128)(...) custom-call(bf16[32,7168]{1,0:T(8,128)(2,1)S(1)} %reshape.135.refs_0_, ...), custom_call_target="tpu_custom_call" | custom-call | flops 1500000000 | bytes 15000000 | tf_op jit(solution)/shard_map/experts_near/pallas_call | solution.py:397
  106.6 4.9 %collective-permute-done.18.refs_2_ = bf16[32,7168]{1,0:T(8,128)(2,1)S(1)} collective-permute-done((bf16[32,7168]{1,0:T(8,128)(2,1)S(1)}, bf16[32,7168]{1,0:T(8,128)(2,1)S(1)}, u32[]{:S(2)}, u32[]{:S(2)}) %collective-permute-start.18) | collective-permute-done | bytes 458784 | tf_op jit(solution)/shard_map/ppermute | solution.py:44
  113.4 2.7 %collective-permute-start.21 = (bf16[32,7168]{1,0:T(8,128)(2,1)S(1)}, bf16[32,7168]{1,0:T(8,128)(2,1)S(1)}, u32[]{:S(2)}, u32[]{:S(2)}) collective-permute-start(bf16[32,7168]{1,0:T(8,128)(2,1)S(1)} %get-tuple-element.53), channel_id=1, source_target_pairs={{0,16},{1,49},{2,18},{3,51},{4,20},{5,53},{6,22},{7,55},{8,24},{9,... | collective-permute-start | bytes 1376264 | tf_op jit(solution)/shard_map/ppermute | solution.py:44
  116.0 2.7 %collective-permute-start.15 = (bf16[32,7168]{1,0:T(8,128)(2,1)S(1)}, bf16[32,7168]{1,0:T(8,128)(2,1)S(1)}, u32[]{:S(2)}, u32[]{:S(2)}) collective-permute-start(bf16[32,7168]{1,0:T(8,128)(2,1)S(1)} %get-tuple-element.47), channel_id=1, source_target_pairs={{0,16},{1,49},{2,18},{3,51},{4,20},{5,53},{6,22},{7,55},{8,24},{9,... | collective-permute-start | bytes 1376264 | tf_op jit(solution)/shard_map/ppermute | solution.py:44
  118.7 6.8 %collective-permute-done.20 = bf16[32,7168]{1,0:T(8,128)(2,1)S(1)} collective-permute-done((bf16[32,7168]{1,0:T(8,128)(2,1)S(1)}, bf16[32,7168]{1,0:T(8,128)(2,1)S(1)}, u32[]{:S(2)}, u32[]{:S(2)}) %collective-permute-start.20) | collective-permute-done | bytes 458784 | tf_op jit(solution)/shard_map/ppermute | solution.py:44
  126.7 5.5 %collective-permute-done.23 = bf16[32,7168]{1,0:T(8,128)(2,1)S(1)} collective-permute-done((bf16[32,7168]{1,0:T(8,128)(2,1)S(1)}, bf16[32,7168]{1,0:T(8,128)(2,1)S(1)}, u32[]{:S(2)}, u32[]{:S(2)}) %collective-permute-start.23) | collective-permute-done | bytes 458784 | tf_op jit(solution)/shard_map/ppermute | solution.py:44
  132.8 2.5 %collective-permute-done.14 = bf16[32,7168]{1,0:T(8,128)(2,1)S(1)} collective-permute-done((bf16[32,7168]{1,0:T(8,128)(2,1)S(1)}, bf16[32,7168]{1,0:T(8,128)(2,1)S(1)}, u32[]{:S(2)}, u32[]{:S(2)}) %collective-permute-start.14) | collective-permute-done | bytes 458784 | tf_op jit(solution)/shard_map/ppermute | solution.py:44
  135.5 5.0 %collective-permute-done.22 = bf16[32,7168]{1,0:T(8,128)(2,1)S(1)} collective-permute-done((bf16[32,7168]{1,0:T(8,128)(2,1)S(1)}, bf16[32,7168]{1,0:T(8,128)(2,1)S(1)}, u32[]{:S(2)}, u32[]{:S(2)}) %collective-permute-start.22) | collective-permute-done | bytes 458784 | tf_op jit(solution)/shard_map/ppermute | solution.py:44
  140.5 5.1 %collective-permute-done.24 = bf16[32,7168]{1,0:T(8,128)(2,1)S(1)} collective-permute-done((bf16[32,7168]{1,0:T(8,128)(2,1)S(1)}, bf16[32,7168]{1,0:T(8,128)(2,1)S(1)}, u32[]{:S(2)}, u32[]{:S(2)}) %collective-permute-start.24) | collective-permute-done | bytes 458784 | tf_op jit(solution)/shard_map/ppermute | solution.py:44
  146.1 13.4 %all_to_all.17 = bf16[16,2,7168]{2,1,0:T(2,128)(2,1)S(1)} all-to-all(bf16[16,2,7168]{2,1,0:T(2,128)(2,1)S(1)} %reshape.136), channel_id=1, replica_groups=mesh['ctx'=8,'exp'=16] {'exp'}, dimensions={0} | all-to-all | bytes 917504 | tf_op jit(solution)/shard_map/all_to_all | solution.py:534
  (88 shorter events, 18.9 us)
Async XLA Ops:
  2.8 14.6 %collective-permute-start.2 = (bf16[4,576,128]{2,1,0:T(8,128)(2,1)S(1)}, bf16[4,576,128]{2,1,0:T(8,128)(2,1)S(1)}, u32[]{:S(2)}, u32[]{:S(2)}) collective-permute-start(bf16[4,576,128]{2,1,0:T(8,128)(2,1)S(1)} %fusion.6.own), channel_id=1, source_target_pairs={{0,16},{1,49},{2,18},{3,51},{4,20},{5,53},{6,22},{7,55},{8,24},{9,... | collective-permute-start | bytes 1769480 | tf_op jit(solution)/shard_map/ppermute | solution.py:44
  7.4 9.6 %collective-permute-start = (bf16[2,576,128]{2,1,0:T(8,128)(2,1)S(1)}, bf16[2,576,128]{2,1,0:T(8,128)(2,1)S(1)}, u32[]{:S(2)}, u32[]{:S(2)}) collective-permute-start(bf16[2,576,128]{2,1,0:T(8,128)(2,1)S(1)} %constant_dynamic-slice_fusion.1), channel_id=1, source_target_pairs={{0,64},{1,65},{2,66},{3,67},{4,68},{5,69},{6,70},{7,71},{8,72},{9,... | collective-permute-start | bytes 884744 | tf_op jit(solution)/shard_map/ppermute | solution.py:44
  17.4 12.1 %collective-permute-start.8 = (bf16[4,576,128]{2,1,0:T(8,128)(2,1)S(1)}, bf16[4,576,128]{2,1,0:T(8,128)(2,1)S(1)}, u32[]{:S(2)}, u32[]{:S(2)}) collective-permute-start(bf16[4,576,128]{2,1,0:T(8,128)(2,1)S(1)} %collective-permute-done.2.beside), channel_id=1, source_target_pairs={{0,1},{1,0},{2,3},{3,2},{4,5},{5,4},{6,7},{7,6},{8,9},{9,8},{10,11... | collective-permute-start | bytes 1769480 | tf_op jit(solution)/shard_map/ppermute | solution.py:48
  18.0 5.9 %collective-permute-start.5 = (bf16[2,576,128]{2,1,0:T(8,128)(2,1)S(1)}, bf16[2,576,128]{2,1,0:T(8,128)(2,1)S(1)}, u32[]{:S(2)}, u32[]{:S(2)}) collective-permute-start(bf16[2,576,128]{2,1,0:T(8,128)(2,1)S(1)} %constant_dynamic-slice_fusion), channel_id=1, source_target_pairs={{0,16},{1,49},{2,18},{3,51},{4,20},{5,53},{6,22},{7,55},{8,24},{9,... | collective-permute-start | bytes 884744 | tf_op jit(solution)/shard_map/ppermute | solution.py:44
  19.1 15.4 %collective-permute-start.3 = (bf16[4,576,128]{2,1,0:T(8,128)(2,1)S(1)}, bf16[4,576,128]{2,1,0:T(8,128)(2,1)S(1)}, u32[]{:S(2)}, u32[]{:S(2)}) collective-permute-start(bf16[4,576,128]{2,1,0:T(8,128)(2,1)S(1)} %pad_maximum_fusion), channel_id=1, source_target_pairs={{0,16},{1,49},{2,18},{3,51},{4,20},{5,53},{6,22},{7,55},{8,24},{9,... | collective-permute-start | bytes 1769480 | tf_op jit(solution)/shard_map/ppermute | solution.py:44
  23.9 10.8 %collective-permute-start.7 = (bf16[2,576,128]{2,1,0:T(8,128)(2,1)S(1)}, bf16[2,576,128]{2,1,0:T(8,128)(2,1)S(1)}, u32[]{:S(2)}, u32[]{:S(2)}) collective-permute-start(bf16[2,576,128]{2,1,0:T(8,128)(2,1)S(1)} %collective-permute-done.5.far), channel_id=1, source_target_pairs={{0,64},{1,65},{2,66},{3,67},{4,68},{5,69},{6,70},{7,71},{8,72},{9,... | collective-permute-start | bytes 884744 | tf_op jit(solution)/shard_map/ppermute | solution.py:44
  27.0 8.4 %collective-permute-start.6 = (bf16[2,576,128]{2,1,0:T(8,128)(2,1)S(1)}, bf16[2,576,128]{2,1,0:T(8,128)(2,1)S(1)}, u32[]{:S(2)}, u32[]{:S(2)}) collective-permute-start(bf16[2,576,128]{2,1,0:T(8,128)(2,1)S(1)} %collective-permute-done.5.far), channel_id=1, source_target_pairs={{0,1},{1,0},{2,3},{3,2},{4,5},{5,4},{6,7},{7,6},{8,9},{9,8},{10,11... | collective-permute-start | bytes 884744 | tf_op jit(solution)/shard_map/ppermute | solution.py:48
  34.6 2.5 %collective-permute-start.4 = (bf16[4,576,128]{2,1,0:T(8,128)(2,1)S(1)}, bf16[4,576,128]{2,1,0:T(8,128)(2,1)S(1)}, u32[]{:S(2)}, u32[]{:S(2)}) collective-permute-start(bf16[4,576,128]{2,1,0:T(8,128)(2,1)S(1)} %collective-permute-done.3.beside), channel_id=1, source_target_pairs={{0,1},{1,0},{2,3},{3,2},{4,5},{5,4},{6,7},{7,6},{8,9},{9,8},{10,11... | collective-permute-start | bytes 1769480 | tf_op jit(solution)/shard_map/ppermute | solution.py:48
  34.7 2.4 %collective-permute-start.9 = (bf16[2,576,128]{2,1,0:T(8,128)(2,1)S(1)}, bf16[2,576,128]{2,1,0:T(8,128)(2,1)S(1)}, u32[]{:S(2)}, u32[]{:S(2)}) collective-permute-start(bf16[2,576,128]{2,1,0:T(8,128)(2,1)S(1)} %fusion.15.side_far), channel_id=1, source_target_pairs={{0,1},{1,0},{2,3},{3,2},{4,5},{5,4},{6,7},{7,6},{8,9},{9,8},{10,11... | collective-permute-start | bytes 884744 | tf_op jit(solution)/shard_map/ppermute | solution.py:48
  43.0 2.6 %collective-permute-start.10 = (bf16[64,7168]{1,0:T(8,128)(2,1)S(1)}, bf16[64,7168]{1,0:T(8,128)(2,1)S(1)}, u32[]{:S(2)}, u32[]{:S(2)}) collective-permute-start(bf16[64,7168]{1,0:T(8,128)(2,1)S(1)} %get-tuple-element.43), channel_id=1, source_target_pairs={{0,1},{1,0},{2,3},{3,2},{4,5},{5,4},{6,7},{7,6},{8,9},{9,8},{10,11... | collective-permute-start | bytes 2752520 | tf_op jit(solution)/shard_map/ppermute | solution.py:48
  77.8 12.3 %collective-permute-start.16 = (bf16[32,7168]{1,0:T(8,128)(2,1)S(1)}, bf16[32,7168]{1,0:T(8,128)(2,1)S(1)}, u32[]{:S(2)}, u32[]{:S(2)}) collective-permute-start(bf16[32,7168]{1,0:T(8,128)(2,1)S(1)} %reshape.135.refs_0_), channel_id=1, source_target_pairs={{0,32},{1,33},{2,34},{3,35},{4,36},{5,37},{6,38},{7,39},{8,40},{9,... | collective-permute-start | bytes 1376264 | tf_op jit(solution)/shard_map/ppermute | solution.py:44
  77.9 12.3 %collective-permute-start.13 = (bf16[32,7168]{1,0:T(8,128)(2,1)S(1)}, bf16[32,7168]{1,0:T(8,128)(2,1)S(1)}, u32[]{:S(2)}, u32[]{:S(2)}) collective-permute-start(bf16[32,7168]{1,0:T(8,128)(2,1)S(1)} %reshape.135.refs_0_), channel_id=1, source_target_pairs={{0,64},{1,65},{2,66},{3,67},{4,68},{5,69},{6,70},{7,71},{8,72},{9,... | collective-permute-start | bytes 1376264 | tf_op jit(solution)/shard_map/ppermute | solution.py:44
  78.4 23.3 %collective-permute-start.12 = (bf16[32,7168]{1,0:T(8,128)(2,1)S(1)}, bf16[32,7168]{1,0:T(8,128)(2,1)S(1)}, u32[]{:S(2)}, u32[]{:S(2)}) collective-permute-start(bf16[32,7168]{1,0:T(8,128)(2,1)S(1)} %reshape.135.refs_0_), channel_id=1, source_target_pairs={{0,48},{1,17},{2,50},{3,19},{4,52},{5,21},{6,54},{7,23},{8,56},{9,... | collective-permute-start | bytes 1376264 | tf_op jit(solution)/shard_map/ppermute | solution.py:44
  80.1 21.6 %collective-permute-start.11 = (bf16[32,7168]{1,0:T(8,128)(2,1)S(1)}, bf16[32,7168]{1,0:T(8,128)(2,1)S(1)}, u32[]{:S(2)}, u32[]{:S(2)}) collective-permute-start(bf16[32,7168]{1,0:T(8,128)(2,1)S(1)} %reshape.135.refs_0_), channel_id=1, source_target_pairs={{0,16},{1,49},{2,18},{3,51},{4,20},{5,53},{6,22},{7,55},{8,24},{9,... | collective-permute-start | bytes 1376264 | tf_op jit(solution)/shard_map/ppermute | solution.py:44
  90.1 16.4 %collective-permute-start.19 = (bf16[32,7168]{1,0:T(8,128)(2,1)S(1)}, bf16[32,7168]{1,0:T(8,128)(2,1)S(1)}, u32[]{:S(2)}, u32[]{:S(2)}) collective-permute-start(bf16[32,7168]{1,0:T(8,128)(2,1)S(1)} %collective-permute-done.16.refs_0_), channel_id=1, source_target_pairs={{0,64},{1,65},{2,66},{3,67},{4,68},{5,69},{6,70},{7,71},{8,72},{9,... | collective-permute-start | bytes 1376264 | tf_op jit(solution)/shard_map/ppermute | solution.py:44
  90.2 21.3 %collective-permute-start.18 = (bf16[32,7168]{1,0:T(8,128)(2,1)S(1)}, bf16[32,7168]{1,0:T(8,128)(2,1)S(1)}, u32[]{:S(2)}, u32[]{:S(2)}) collective-permute-start(bf16[32,7168]{1,0:T(8,128)(2,1)S(1)} %collective-permute-done.13.refs_3_), channel_id=1, source_target_pairs={{0,48},{1,17},{2,50},{3,19},{4,52},{5,21},{6,54},{7,23},{8,56},{9,... | collective-permute-start | bytes 1376264 | tf_op jit(solution)/shard_map/ppermute | solution.py:44
  90.2 21.3 %collective-permute-start.17 = (bf16[32,7168]{1,0:T(8,128)(2,1)S(1)}, bf16[32,7168]{1,0:T(8,128)(2,1)S(1)}, u32[]{:S(2)}, u32[]{:S(2)}) collective-permute-start(bf16[32,7168]{1,0:T(8,128)(2,1)S(1)} %collective-permute-done.13.refs_3_), channel_id=1, source_target_pairs={{0,16},{1,49},{2,18},{3,51},{4,20},{5,53},{6,22},{7,55},{8,24},{9,... | collective-permute-start | bytes 1376264 | tf_op jit(solution)/shard_map/ppermute | solution.py:44
  113.3 12.2 %collective-permute-start.20 = (bf16[32,7168]{1,0:T(8,128)(2,1)S(1)}, bf16[32,7168]{1,0:T(8,128)(2,1)S(1)}, u32[]{:S(2)}, u32[]{:S(2)}) collective-permute-start(bf16[32,7168]{1,0:T(8,128)(2,1)S(1)} %get-tuple-element.52), channel_id=1, source_target_pairs={{0,48},{1,17},{2,50},{3,19},{4,52},{5,21},{6,54},{7,23},{8,56},{9,... | collective-permute-start | bytes 1376264 | tf_op jit(solution)/shard_map/ppermute | solution.py:44
  113.4 13.1 %collective-permute-start.21 = (bf16[32,7168]{1,0:T(8,128)(2,1)S(1)}, bf16[32,7168]{1,0:T(8,128)(2,1)S(1)}, u32[]{:S(2)}, u32[]{:S(2)}) collective-permute-start(bf16[32,7168]{1,0:T(8,128)(2,1)S(1)} %get-tuple-element.53), channel_id=1, source_target_pairs={{0,16},{1,49},{2,18},{3,51},{4,20},{5,53},{6,22},{7,55},{8,24},{9,... | collective-permute-start | bytes 1376264 | tf_op jit(solution)/shard_map/ppermute | solution.py:44
  116.0 19.3 %collective-permute-start.14 = (bf16[32,7168]{1,0:T(8,128)(2,1)S(1)}, bf16[32,7168]{1,0:T(8,128)(2,1)S(1)}, u32[]{:S(2)}, u32[]{:S(2)}) collective-permute-start(bf16[32,7168]{1,0:T(8,128)(2,1)S(1)} %get-tuple-element.46), channel_id=1, source_target_pairs={{0,48},{1,17},{2,50},{3,19},{4,52},{5,21},{6,54},{7,23},{8,56},{9,... | collective-permute-start | bytes 1376264 | tf_op jit(solution)/shard_map/ppermute | solution.py:44
  116.0 19.5 %collective-permute-start.15 = (bf16[32,7168]{1,0:T(8,128)(2,1)S(1)}, bf16[32,7168]{1,0:T(8,128)(2,1)S(1)}, u32[]{:S(2)}, u32[]{:S(2)}) collective-permute-start(bf16[32,7168]{1,0:T(8,128)(2,1)S(1)} %get-tuple-element.47), channel_id=1, source_target_pairs={{0,16},{1,49},{2,18},{3,51},{4,20},{5,53},{6,22},{7,55},{8,24},{9,... | collective-permute-start | bytes 1376264 | tf_op jit(solution)/shard_map/ppermute | solution.py:44
  118.7 13.4 %collective-permute-start.23 = (bf16[32,7168]{1,0:T(8,128)(2,1)S(1)}, bf16[32,7168]{1,0:T(8,128)(2,1)S(1)}, u32[]{:S(2)}, u32[]{:S(2)}) collective-permute-start(bf16[32,7168]{1,0:T(8,128)(2,1)S(1)} %get-tuple-element.55), channel_id=1, source_target_pairs={{0,64},{1,65},{2,66},{3,67},{4,68},{5,69},{6,70},{7,71},{8,72},{9,... | collective-permute-start | bytes 1376264 | tf_op jit(solution)/shard_map/ppermute | solution.py:44
  126.6 13.9 %collective-permute-start.22 = (bf16[32,7168]{1,0:T(8,128)(2,1)S(1)}, bf16[32,7168]{1,0:T(8,128)(2,1)S(1)}, u32[]{:S(2)}, u32[]{:S(2)}) collective-permute-start(bf16[32,7168]{1,0:T(8,128)(2,1)S(1)} %add_convert_fusion.3), channel_id=1, source_target_pairs={{0,64},{1,65},{2,66},{3,67},{4,68},{5,69},{6,70},{7,71},{8,72},{9,... | collective-permute-start | bytes 1376264 | tf_op jit(solution)/shard_map/ppermute | solution.py:44
  132.3 13.3 %collective-permute-start.24 = (bf16[32,7168]{1,0:T(8,128)(2,1)S(1)}, bf16[32,7168]{1,0:T(8,128)(2,1)S(1)}, u32[]{:S(2)}, u32[]{:S(2)}) collective-permute-start(bf16[32,7168]{1,0:T(8,128)(2,1)S(1)} %add_convert_fusion.2), channel_id=1, source_target_pairs={{0,32},{1,33},{2,34},{3,35},{4,36},{5,37},{6,38},{7,39},{8,40},{9,... | collective-permute-start | bytes 1376264 | tf_op jit(solution)/shard_map/ppermute | solution.py:44
  (8 other events, 197.4 us)
